TPU v7x, 32 devices: a whole 2x2x4 slice. The times are simulated.
32 devices in a mesh: rows: 8 (over z, x), lat: 4 (over y, core).
Axes of the slice: x: 2, y: 2, z: 4, core: 2. Of those that a mesh axis runs over, the one named last changes fastest.
Arguments:
- token_ids: int32 [32768], P('rows'), may hold values from 0 to 50303
- token_mask: int32 [32768], P('rows'), may hold values from 0 to 1
- scale_index: int32 [32768], P('rows'), may hold values from 0 to 7
- embed: bfloat16 [50304, 512], P('lat'), may hold values from -6 to 6
- norm_params: float32 [4, 512], replicated
- frozen_bias: float32 [4608], replicated, may hold values from -2 to 2
- w_joined: bfloat16 [512, 1536], replicated, may hold values from -0.25 to 0.25
- w_attn_out: bfloat16 [512, 512], replicated, may hold values from -1 to 1
- w_mlp_in: bfloat16 [512, 2048], replicated, may hold values from -0.25 to 0.25
- w_mlp_out: bfloat16 [2048, 512], replicated, may hold values from -0.1875 to 0.1875
- enc_weight: float32 [512, 16384], P('rows', 'lat'), may hold values from -0.25 to 0.25
- enc_moment: float32 [512, 16384], P('rows', 'lat'), may hold values from -6.1035156e-05 to 6.1035156e-05
- enc_second: float32 [512, 16384], P('rows', 'lat'), may hold values from 7.2759577e-13 to 1.1641532e-11
- dec_weight: float32 [16384, 512], P('lat', 'rows')
- dec_moment: float32 [16384, 512], P('lat', 'rows'), may hold values from -0.00048828125 to 0.00048828125
- dec_second: float32 [16384, 512], P('lat', 'rows'), may hold values from 5.960465e-11 to 9.536744e-10
- enc_bias: float32 [16384], P('lat')
- enc_bias_moment: float32 [16384], P('lat'), may hold values from -0.0034179688 to 0.0034179688
- enc_bias_second: float32 [16384], P('lat'), may hold values from 2.1457671e-09 to 3.4332274e-08
- dec_bias: float32 [512], replicated, may hold values from -6 to 6
- dec_bias_moment: float32 [512], replicated, may hold values from -0.01171875 to 0.01171875
- dec_bias_second: float32 [512], replicated, may hold values from 2.384186e-10 to 3.8146974e-09
Outputs:
- enc_weight_new: float32 [512, 16384], P('rows', 'lat')
- enc_moment_new: float32 [512, 16384], P('rows', 'lat')
- enc_second_new: float32 [512, 16384], P('rows', 'lat')
- dec_weight_new: float32 [16384, 512], P('lat', 'rows')
- dec_moment_new: float32 [16384, 512], P('lat', 'rows')
- dec_second_new: float32 [16384, 512], P('lat', 'rows')
- enc_bias_new: float32 [16384], P('lat')
- enc_bias_moment_new: float32 [16384], P('lat')
- enc_bias_second_new: float32 [16384], P('lat')
- dec_bias_new: float32 [512], replicated
- dec_bias_moment_new: float32 [512], replicated
- dec_bias_second_new: float32 [512], replicated
- grad_norm: float32 [], replicated
- loss_sum: float32 [], replicated
- token_count: float32 [], replicated
All inputs are finite; a program needn't handle non-finite values.
Results may differ from a plain program's by a relative error of at most 0.0003.
The roundings to bfloat16 on the way count: a program that leaves them out, or rounds other values in their place, can miss the bound.
Values may be sent and summed in bfloat16 or wider, within the bound.
A program may use at most 256 MiB of HBM per device.

v0:
```python
import jax
import jax.numpy as jnp
from jax import lax
from jax.sharding import PartitionSpec as P

HEADS = 8
ROT = 16
STEP = 10


lasso_coef = 5.0
clip_bound = 1.0
learn_rate = 0.03
beta_one = 0.9
beta_two = 0.999
adam_eps = 1e-08
weight_decay = 0.01


def layer_norm(values, gain, shift):
    centred = values - jnp.mean(values, axis=-1, keepdims=True)
    spread = jnp.mean(centred * centred, axis=-1, keepdims=True)
    return centred * lax.rsqrt(spread + 1e-05) * gain + shift


def rotary(values, rotated):
    length = values.shape[0]
    half = rotated // 2
    freqs = 10000.0 ** (-2.0 * jnp.arange(half, dtype=jnp.float32) / rotated)
    angles = jnp.arange(length, dtype=jnp.float32)[:, None] * freqs[None, :]
    cosines = jnp.concatenate([jnp.cos(angles), jnp.cos(angles)], -1)[:, None, :]
    sines = jnp.concatenate([jnp.sin(angles), jnp.sin(angles)], -1)[:, None, :]
    head = values[..., :rotated]
    turned = jnp.concatenate([-head[..., half:], head[..., :half]], -1)
    return jnp.concatenate([head * cosines + turned * sines, values[..., rotated:]], -1)


def contract_rows(left, right):
    return lax.dot_general(
        left, right, (((0,), (0,)), ((), ())), preferred_element_type=jnp.float32
    )


def contract_cols(left, right):
    return lax.dot_general(
        left, right, (((1,), (1,)), ((), ())), preferred_element_type=jnp.float32
    )


def frozen_layer(embedded, norm_params, frozen_bias, w_joined, w_attn_out, w_mlp_in, w_mlp_out):
    length, width = embedded.shape
    head_dim = width // HEADS
    hidden_units = w_mlp_in.shape[1]
    attn_in = layer_norm(embedded, norm_params[0], norm_params[1]).astype(jnp.bfloat16)
    joined = (
        jnp.dot(attn_in, w_joined, preferred_element_type=jnp.float32) + frozen_bias[: 3 * width]
    )
    queries = rotary(joined[:, :width].reshape(length, HEADS, head_dim), ROT).astype(jnp.bfloat16)
    keys = rotary(joined[:, width : 2 * width].reshape(length, HEADS, head_dim), ROT).astype(
        jnp.bfloat16
    )
    values = joined[:, 2 * width :].reshape(length, HEADS, head_dim).astype(jnp.bfloat16)
    block_rows = min(512, length)
    key_places = jnp.arange(length)

    def attend(block_start):
        block_queries = lax.dynamic_slice_in_dim(queries, block_start, block_rows, 0)
        scores = jnp.einsum(
            "qhd,khd->hqk", block_queries, keys, preferred_element_type=jnp.float32
        ) * head_dim ** (-0.5)
        query_places = block_start + jnp.arange(block_rows)
        causal = query_places[None, :, None] >= key_places[None, None, :]
        probs = jax.nn.softmax(jnp.where(causal, scores, -1e30), axis=-1).astype(jnp.bfloat16)
        return jnp.einsum("hqk,khd->qhd", probs, values, preferred_element_type=jnp.float32)

    starts = jnp.arange(0, length, block_rows)
    context = lax.map(attend, starts).reshape(length, width).astype(jnp.bfloat16)
    attended = (
        jnp.dot(context, w_attn_out, preferred_element_type=jnp.float32)
        + frozen_bias[3 * width : 4 * width]
    )
    mlp_in = layer_norm(embedded, norm_params[2], norm_params[3]).astype(jnp.bfloat16)
    inner = (
        jnp.dot(mlp_in, w_mlp_in, preferred_element_type=jnp.float32)
        + frozen_bias[4 * width : 4 * width + hidden_units]
    )
    inner = jax.nn.gelu(inner, approximate=False).astype(jnp.bfloat16)
    mlp_out = (
        jnp.dot(inner, w_mlp_out, preferred_element_type=jnp.float32)
        + frozen_bias[4 * width + hidden_units :]
    )
    return embedded + attended + mlp_out


def adam_update(weight, moment, second, grad, decay):
    moment_new = beta_one * moment + (1.0 - beta_one) * grad
    second_new = beta_two * second + (1.0 - beta_two) * grad * grad
    corrected = moment_new / (1.0 - beta_one**STEP)
    scaled = jnp.sqrt(second_new / (1.0 - beta_two**STEP)) + adam_eps
    weight_new = weight - learn_rate * (corrected / scaled + decay * weight)
    return (weight_new, moment_new, second_new)


def body(
    token_ids,
    token_mask,
    scale_index,
    embed,
    norm_params,
    frozen_bias,
    w_joined,
    w_attn_out,
    w_mlp_in,
    w_mlp_out,
    enc_weight,
    enc_moment,
    enc_second,
    dec_weight,
    dec_moment,
    dec_second,
    enc_bias,
    enc_bias_moment,
    enc_bias_second,
    dec_bias,
    dec_bias_moment,
    dec_bias_second,
):
    lat_size = lax.axis_size("lat")
    lat_index = lax.axis_index("lat")
    group_tokens = token_ids.shape[0]
    tok_local = group_tokens // lat_size
    lat_local = enc_bias.shape[0]
    mask_float = token_mask.astype(jnp.float32)
    enc_low = lax.all_gather(enc_weight.astype(jnp.bfloat16), "rows", axis=0, tiled=True)
    dec_full = lax.all_gather(dec_weight.astype(jnp.bfloat16), "rows", axis=1, tiled=True).astype(
        dec_weight.dtype
    )
    count = lax.psum(jnp.sum(mask_float), "rows")
    vocab_local = embed.shape[0]
    vocab_first = lat_index * vocab_local
    local_ids = token_ids - vocab_first
    inside = ((local_ids >= 0) & (local_ids < vocab_local)).astype(jnp.float32)
    picked = jnp.take(embed, jnp.clip(local_ids, 0, vocab_local - 1), axis=0).astype(jnp.float32)
    embedded = lax.psum_scatter(
        (picked * inside[:, None]).astype(jnp.bfloat16), "lat", scatter_dimension=0, tiled=True
    ).astype(jnp.float32)
    own_first = lat_index * tok_local
    residual = frozen_layer(
        embedded, norm_params, frozen_bias, w_joined, w_attn_out, w_mlp_in, w_mlp_out
    )
    scales = 0.5 + 0.25 * lax.dynamic_slice_in_dim(scale_index, own_first, tok_local).astype(
        jnp.float32
    )
    own_inputs = (residual * scales[:, None]).astype(jnp.bfloat16)
    all_inputs = lax.all_gather(own_inputs, "lat", axis=0, tiled=True)
    preact = jnp.dot(all_inputs, enc_low, preferred_element_type=jnp.float32) + enc_bias
    active = jax.nn.softplus(preact)
    active_low = active.astype(jnp.bfloat16)
    norms = jnp.sqrt(jnp.sum(dec_full * dec_full, axis=1))
    dec_low = dec_full.astype(jnp.bfloat16)
    partial_recon = jnp.dot(active_low, dec_low, preferred_element_type=jnp.float32)
    recon = lax.psum(partial_recon, "lat") + dec_bias
    error_rows = recon - all_inputs.astype(jnp.float32)
    leader = (lat_index == 0).astype(jnp.float32)
    square_part = jnp.sum(mask_float * jnp.sum(error_rows * error_rows, axis=1)) * leader
    recon_grad = (2.0 / count * mask_float[:, None] * error_rows).astype(jnp.bfloat16)
    bias_part = jnp.sum(recon_grad, axis=0, dtype=jnp.float32) * leader
    active_mass = jnp.dot(mask_float, active, precision=lax.Precision.HIGHEST)
    lasso_part = lasso_coef * jnp.sum(active_mass * norms)
    lasso_scale = lasso_coef / count
    grad_dec = (
        contract_rows(active_low, recon_grad)
        + (lasso_scale * active_mass / norms)[:, None] * dec_full
    )
    grad_active = (
        contract_cols(recon_grad, dec_low) + lasso_scale * mask_float[:, None] * norms[None, :]
    )
    grad_preact = (grad_active * jax.nn.sigmoid(preact)).astype(jnp.bfloat16)
    grad_enc = contract_rows(all_inputs, grad_preact)
    enc_bias_part = jnp.sum(grad_preact, axis=0, dtype=jnp.float32)
    placed_bias = lax.dynamic_update_slice(
        jnp.zeros((lat_local * lat_size,), jnp.float32), enc_bias_part, (lat_index * lat_local,)
    )
    loss_sum, grad_dec_bias, placed_sum = lax.psum(
        (square_part + lasso_part, bias_part, placed_bias), ("rows", "lat")
    )
    grad_enc_bias = lax.dynamic_slice_in_dim(placed_sum, lat_index * lat_local, lat_local)
    grad_enc, grad_dec = (
        lax.psum_scatter(grad_enc, "rows", scatter_dimension=0, tiled=True),
        lax.psum_scatter(grad_dec, "rows", scatter_dimension=1, tiled=True),
    )
    local_squares = jnp.sum(grad_enc * grad_enc) + jnp.sum(grad_dec * grad_dec)
    squares = (
        lax.psum(local_squares, ("rows", "lat"))
        + jnp.sum(placed_sum * placed_sum)
        + jnp.sum(grad_dec_bias * grad_dec_bias)
    )
    grad_norm = jnp.sqrt(squares)
    factor = clip_bound / jnp.maximum(grad_norm, clip_bound)
    enc_new = adam_update(enc_weight, enc_moment, enc_second, grad_enc * factor, weight_decay)
    dec_new = adam_update(dec_weight, dec_moment, dec_second, grad_dec * factor, weight_decay)
    enc_bias_new = adam_update(
        enc_bias, enc_bias_moment, enc_bias_second, grad_enc_bias * factor, 0.0
    )
    dec_bias_new = adam_update(
        dec_bias, dec_bias_moment, dec_bias_second, grad_dec_bias * factor, 0.0
    )
    return (
        enc_new[0],
        enc_new[1],
        enc_new[2],
        dec_new[0],
        dec_new[1],
        dec_new[2],
        enc_bias_new[0],
        enc_bias_new[1],
        enc_bias_new[2],
        dec_bias_new[0],
        dec_bias_new[1],
        dec_bias_new[2],
        grad_norm,
        loss_sum,
        count,
    )


def solution(mesh):
    placed = (
        P("rows"),
        P("rows"),
        P("rows"),
        P("lat", None),
        P(),
        P(),
        P(),
        P(),
        P(),
        P(),
        P("rows", "lat"),
        P("rows", "lat"),
        P("rows", "lat"),
        P("lat", "rows"),
        P("lat", "rows"),
        P("lat", "rows"),
        P("lat"),
        P("lat"),
        P("lat"),
        P(),
        P(),
        P(),
    )
    return jax.shard_map(
        body,
        mesh=mesh,
        in_specs=placed,
        out_specs=(
            P("rows", "lat"),
            P("rows", "lat"),
            P("rows", "lat"),
            P("lat", "rows"),
            P("lat", "rows"),
            P("lat", "rows"),
            P("lat"),
            P("lat"),
            P("lat"),
            P(),
            P(),
            P(),
            P(),
            P(),
            P(),
        ),
        check_vma=False,
    )
```

profile of v0, /device:TPU:0, one launch (start us, length us, event | category | flops | bytes accessed | tf_op | source)
XLA Modules:
  0.0 937.0 jit_solution(5071960522933705387)
XLA Ops:
  9.7 23.7 %gather_fusion = bf16[4096,512]{1,0:T(8,128)(2,1)} fusion(bf16[12576,512]{1,0:T(8,128)(2,1)} %param.27, s32[4096]{0:T(1024)S(1)} %fusion.69), kind=kCustom, calls=%fused_computation | custom fusion | bytes 8404992 | tf_op jit(solution)/shard_map/jit(_take)/gather | solution.py:143
  33.4 6.3 multiply_convert_fusion.2
  40.7 2.1 convert_element_type.89
  45.6 41.5 %reduce-scatter.4.cloned.1.call-done = bf16[1024,512]{1,0:T(8,128)(2,1)} async-done(((bf16[4096,512]{1,0:T(8,128)(2,1)}), bf16[1024,512]{1,0:T(8,128)(2,1)}) %reduce-scatter.4.cloned.1.call-update) | async-done | bytes 1048592 | tf_op jit(solution)/shard_map/reduce_scatter | solution.py:144
  87.1 1.4 convert_reduce_fusion.2
  88.6 1.7 fusion.41
  90.3 3.6 convolution_add_fusion
  94.0 2.6 copy-done.2
  96.6 2.5 fusion.107
  99.1 3.1 copy.46
  102.2 2.9 copy.47
  105.1 2.4 slice.112
  107.5 2.1 slice_negate_fusion
  109.7 2.4 slice.113
  112.1 1.7 slice.111
  115.1 1.7 fusion.63
  118.0 2.2 pad_maximum_fusion
  120.2 90.3 %while.11 = (s32[]{:T(128)}, bf16[2,512,8,64]{1,3,2,0:T(8,128)(2,1)}, s32[2]{0:T(128)S(1)}, bf16[1024,8,64]{0,2,1:T(8,128)(2,1)}, bf16[1024,8,64]{0,2,1:T(8,128)...) while((s32[]{:T(128)}, bf16[2,512,8,64]{1,3,2,0:T(8,128)(2,1)}, ...), condition=%wide.region_6.7_spmd.clone, body=%wide.region_3.6_spmd.clone.sunk | while | flops 1107822080 | bytes 71864976 | solution.py:77
  122.8 9.5 %fusion.139 = f32[8,512,1024]{2,1,0:T(8,128)} fusion(bf16[1024,8,64]{0,2,1:T(8,128)(2,1)S(1)} %get-tuple-element.200, bf16[1024,8,64]{0,2,1:T(8,128)(2,1)} %get-tuple-element.199, s32[]{:T(128)S(6)} %select_n.57), kind=kOutput, calls=%fused_computation.14.clone.1 | convolution fusion | flops 536870912 | bytes 18350084 | tf_op jit(solution)/shard_map/while/body/eval_jaxpr/qhd,khd->hqk/dot_general | solution.py:68
  134.1 21.7 %fusion.140 = (f32[8,512]{1,0:T(8,128)S(1)}, f32[8,512,1024]{2,1,0:T(8,128)}) fusion(f32[8,512,1024]{2,1,0:T(8,128)} %fusion.139, pred[512,1024]{1,0:T(8,128)(4,1)} %iota_compare_fusion.2), kind=kOutput, calls=%fused_computation.167.clone.1 | output fusion | flops 25166848 | bytes 34095104 | tf_op jit(solution)/shard_map/while/body/eval_jaxpr/sub | solution.py:73
  155.8 9.6 %fusion.141 = bf16[2,512,8,64]{1,3,2,0:T(8,128)(2,1)} fusion(bf16[2,512,8,64]{1,3,2,0:T(8,128)(2,1)} %get-tuple-element.188, s32[]{:T(128)} %get-tuple-element.187, bf16[1024,8,64]{0,2,1:T(8,128)(2,1)} %get-tuple-element.201, f32[8,512,1024]{2,1,0:T(8,128)} %get-tuple-element.176, f32[8,512]{1,0:T(8,128)S(1)} %get-tuple-element.177), kind=kOutput, calls=%fused_computation.13.clone.1 | convolution fusion | flops 545259520 | bytes 18891264 | tf_op jit(solution)/shard_map/while/body/eval_jaxpr/hqk,khd->qhd/dot_general | solution.py:74
  167.9 9.3 fusion.139
  178.9 21.7 %fusion.140 = (f32[8,512]{1,0:T(8,128)S(1)}, f32[8,512,1024]{2,1,0:T(8,128)}) fusion(f32[8,512,1024]{2,1,0:T(8,128)} %fusion.139, pred[512,1024]{1,0:T(8,128)(4,1)} %iota_compare_fusion.2), kind=kOutput, calls=%fused_computation.167.clone.1 | output fusion | flops 25166848 | bytes 34095104 | tf_op jit(solution)/shard_map/while/body/eval_jaxpr/sub | solution.py:73
  200.6 9.5 %fusion.141 = bf16[2,512,8,64]{1,3,2,0:T(8,128)(2,1)} fusion(bf16[2,512,8,64]{1,3,2,0:T(8,128)(2,1)} %get-tuple-element.188, s32[]{:T(128)} %get-tuple-element.187, bf16[1024,8,64]{0,2,1:T(8,128)(2,1)} %get-tuple-element.201, f32[8,512,1024]{2,1,0:T(8,128)} %get-tuple-element.176, f32[8,512]{1,0:T(8,128)S(1)} %get-tuple-element.177), kind=kOutput, calls=%fused_computation.13.clone.1 | convolution fusion | flops 545259520 | bytes 18891264 | tf_op jit(solution)/shard_map/while/body/eval_jaxpr/hqk,khd->qhd/dot_general | solution.py:74
  210.5 2.3 copy.49
  214.1 23.4 %fusion.29 = f32[1024,512]{1,0:T(8,128)} fusion(bf16[2048,512]{1,0:T(8,128)(2,1)S(1)} %copy-done, f32[2048]{0:T(1024)S(1)} %slice-done.1, bf16[512,2048]{1,0:T(8,128)(2,1)} %param.32, bf16[1024,512]{1,0:T(8,128)(2,1)} %reduce-scatter.4.cloned.1.call-done, f32[512]{0:T(512)S(1)} %bitcast.58, f32[512]{0:T(512)S(1)} %bitcast.59, f32[1024]{0:T(1024)S(1)} %copy-done.24, ...), kind=kOutput, calls=%fused_computation.54 | convolution fusion | flops 4436525056 | bytes 7360512 | tf_op jit(solution)/shard_map/dot_general | solution.py:89
  237.5 4.0 fusion.44
  241.6 3.7 fusion.17
  245.3 30.9 %all-gather.4.cloned.1.call-done = bf16[4096,512]{1,0:T(8,128)(2,1)} async-done(((bf16[1024,512]{1,0:T(8,128)(2,1)}), bf16[4096,512]{1,0:T(8,128)(2,1)}) %all-gather.4.cloned.1.call-update) | async-done | bytes 4194320 | tf_op jit(solution)/shard_map/all_gather | solution.py:155
  276.2 59.8 %fusion.16 = (bf16[4096,4096]{1,0:T(8,128)(2,1)}, f32[4096,4096]{1,0:T(8,128)}) fusion(f32[4096]{0:T(1024)S(1)} %copy-done.17, bf16[4096,512]{1,0:T(8,128)(2,1)} %all-gather.4.cloned.1.call-done, bf16[512,4096]{1,0:T(8,128)(2,1)} %all-gather.6.cloned.1.call-done), kind=kOutput, calls=%fused_computation.24 | convolution fusion | flops 17314086912 | bytes 109068288 | tf_op jit(solution)/shard_map/dot_general | solution.py:156
  336.0 25.0 %fusion.110 = f32[4096,512]{1,0:T(8,128)} fusion(bf16[4096,4096]{1,0:T(8,128)(2,1)} %get-tuple-element.129, bf16[4096,512]{0,1:T(8,128)(2,1)} %all-gather.8.cloned.1.call-done), kind=kOutput, calls=%fused_computation.171 | convolution fusion | flops 17179869184 | bytes 46137344 | tf_op jit(solution)/shard_map/dot_general | solution.py:161
  361.1 74.6 %fusion.15 = f32[1,4096]{1,0:T(1,128)S(1)} fusion(f32[4096,1]{0,1:T(1,128)S(1)} %bitcast.56, f32[4096,4096]{1,0:T(8,128)} %get-tuple-element.130, f32[4096]{0:T(1024)S(1)} %copy-done.17), kind=kOutput, calls=%fused_computation.23 | convolution fusion | flops 318767104 | bytes 67158016 | tf_op jit(solution)/shard_map/dot_general | solution.py:168
  435.7 78.3 %all-reduce.4.cloned.1.call-done = f32[4096,512]{1,0:T(8,128)} async-done(((f32[4096,512]{1,0:T(8,128)}), f32[4096,512]{1,0:T(8,128)}) %all-reduce.4.cloned.1.call-update) | async-done | bytes 8388624 | tf_op jit(solution)/shard_map/psum | solution.py:162
  514.1 6.1 multiply_reduce_fusion
  520.8 22.2 %psum.42 = f32[]{:T(128)} all-reduce(f32[]{:T(128)} %get-tuple-element.74), channel_id=1, replica_groups=mesh['rows'=8,'lat'=4] {'rows'}, use_global_device_ids=true, to_apply=%region_8.9 | all-reduce | flops 1 | bytes 8 | tf_op jit(solution)/shard_map/psum | solution.py:138
  545.0 6.1 convert_reduce_fusion.1
  551.1 2.0 copy-done.5
  553.1 23.1 %fusion.18 = f32[4096,512]{0,1:T(8,128)} fusion(bf16[4096,512]{0,1:T(8,128)(2,1)S(1)} %copy-done.3, bf16[4096,4096]{1,0:T(8,128)(2,1)} %get-tuple-element.129, bf16[4096,512]{1,0:T(8,128)(2,1)S(1)} %get-tuple-element.103, f32[4096]{0:T(1024)S(1)} %get-tuple-element.115), kind=kOutput, calls=%fused_computation.29 | convolution fusion | flops 17186160640 | bytes 50348032 | tf_op jit(solution)/shard_map/dot_general | solution.py:39
  576.2 46.4 %convert_reduce_fusion = (f32[4096]{0:T(1024)S(1)}, bf16[4096,4096]{1,0:T(8,128)(2,1)}) fusion(f32[4096,4096]{1,0:T(8,128)} %get-tuple-element.130, f32[4096]{0:T(1024)S(1)} %copy-done.17, f32[4096]{0:T(1024)S(1)} %get-tuple-element.118, f32[4096]{0:T(1024)S(1)} %get-tuple-element.120, bf16[4096,512]{1,0:T(8,128)(2,1)} %copy-done.5, ...), kind=kOutput, calls=%fused_computation.21 | convolution fusion | flops 17347637248 | bytes 109117440 | tf_op jit(solution)/shard_map/dot_general | solution.py:45
  622.6 24.1 %fusion.111 = f32[512,4096]{1,0:T(8,128)} fusion(bf16[4096,512]{1,0:T(8,128)(2,1)} %all-gather.4.cloned.1.call-done, bf16[4096,4096]{1,0:T(8,128)(2,1)} %get-tuple-element.132), kind=kOutput, calls=%fused_computation.172 | convolution fusion | flops 17179869184 | bytes 46137344 | tf_op jit(solution)/shard_map/dot_general | solution.py:39
  649.3 71.0 %reduce-scatter.8.cloned.1.call-done = f32[4096,64]{0,1:T(8,128)} async-done(((f32[4096,512]{0,1:T(8,128)}), f32[4096,64]{0,1:T(8,128)}) %reduce-scatter.8.cloned.1.call-update) | async-done | bytes 1048592 | tf_op jit(solution)/shard_map/reduce_scatter | solution.py:190
  720.3 2.1 multiply_reduce_fusion.1
  722.4 148.6 %reduce-scatter.6.cloned.1.call-done = f32[64,4096]{1,0:T(8,128)} async-done(((f32[512,4096]{1,0:T(8,128)}), f32[64,4096]{1,0:T(8,128)}) %reduce-scatter.6.cloned.1.call-update) | async-done | bytes 1048592 | tf_op jit(solution)/shard_map/reduce_scatter | solution.py:189
  871.0 2.1 multiply_reduce_fusion.2
  874.4 1.5 multiply_reduce_fusion.3
  875.9 39.2 %all-reduce = (f32[]{:T(128)}, f32[512]{0:T(512)S(1)}, f32[]{:T(128)}) all-reduce(f32[]{:T(128)S(6)} %add.261, f32[512]{0:T(512)S(1)} %broadcast_multiply_fusion.3, f32[]{:T(128)S(6)} %add.285), channel_id=1, replica_groups=mesh['rows'=8,'lat'=4] {'rows','lat'}, use_global_device_ids=true, to_apply=%region_15.16 | all-reduce | flops 514 | bytes 4112 | tf_op jit(solution)/shard_map/psum | solution.py:194
  919.7 4.0 multiply_subtract_fusion
  923.8 4.4 multiply_subtract_fusion.1
  (115 shorter events, 19.2 us)
Async XLA Ops:
  8.0 206.0 %copy-start = (bf16[2048,512]{1,0:T(8,128)(2,1)S(1)}, bf16[2048,512]{1,0:T(8,128)(2,1)}, u32[]{:S(2)}) copy-start(bf16[2048,512]{1,0:T(8,128)(2,1)} %param.33) | copy-start | bytes 6291460
  8.0 79.1 %reduce-scatter.4.cloned.1.call-start = ((), (), s32[]{:S(2)}) async-start(), calls=%async_computation.3 | async-start | bytes 5242880 | tf_op jit(solution)/shard_map/reduce_scatter | solution.py:144
  33.4 6.3 copy-start.6
  33.4 9.5 %copy-start.12 = (f32[4608]{0:T(1024)S(1)}, f32[4608]{0:T(1024)}, u32[]{:S(2)}) copy-start(f32[4608]{0:T(1024)} %param.29) | copy-start | bytes 55300
  33.4 10.1 %copy-start.20 = (f32[4,512]{1,0:T(4,128)S(1)}, f32[4,512]{1,0:T(4,128)}, u32[]{:S(2)}) copy-start(f32[4,512]{1,0:T(4,128)} %param.28) | copy-start | bytes 24580
  33.4 56.9 %slice-start = ((f32[4608]{0:T(1024)}), f32[1536]{0:T(1024)S(1)}, s32[]{:S(2)}) async-start(f32[4608]{0:T(1024)} %param.29), calls=%async_computation.11 | async-start | bytes 16384 | tf_op jit(solution)/shard_map/slice | solution.py:56
  39.7 201.9 %all-gather.8.cloned.1.call-start = ((), (), s32[]{:S(2)}) async-start(), calls=%async_computation.6 | async-start | bytes 4718592 | tf_op jit(solution)/shard_map/all_gather | solution.py:135
  40.6 204.7 %all-gather.6.cloned.1.call-start = ((), (), s32[]{:S(2)}) async-start(), calls=%async_computation.5 | async-start | bytes 4718592 | tf_op jit(solution)/shard_map/all_gather | solution.py:134
  42.8 233.4 %all-gather.4.cloned.1.call-start = ((), (), s32[]{:S(2)}) async-start(), calls=%async_computation.4 | async-start | bytes 5242880 | tf_op jit(solution)/shard_map/all_gather | solution.py:155
  88.6 5.4 copy-start.15
  90.3 3.7 copy-start.23
  94.0 2.6 copy-start.2
  120.2 93.8 %slice-start.1 = ((f32[4608]{0:T(1024)}), f32[2048]{0:T(1024)S(1)}, s32[]{:S(2)}) async-start(f32[4608]{0:T(1024)} %param.29), calls=%async_computation.12 | async-start | bytes 16384 | tf_op jit(solution)/shard_map/slice | solution.py:85
  120.2 93.8 %copy-start.16 = (f32[1024]{0:T(1024)S(1)}, f32[1024]{0:T(1024)}, u32[]{:S(2)}) copy-start(f32[1024]{0:T(1024)} %copy-done.15) | copy-start | bytes 12292
  120.2 93.8 %copy-start.24 = (f32[1024]{0:T(1024)S(1)}, f32[1024]{0:T(1024)}, u32[]{:S(2)}) copy-start(f32[1024]{0:T(1024)} %copy-done.23) | copy-start | bytes 12292
  120.2 93.8 %copy-start.29 = (f32[1,512]{1,0:T(1,128)S(1)}, f32[1,512]{1,0:T(1,128)}, u32[]{:S(2)}) copy-start(f32[1,512]{1,0:T(1,128)} %get-tuple-element.125) | copy-start | bytes 6148
  120.2 93.8 %copy-start.30 = (f32[1,512]{1,0:T(1,128)S(1)}, f32[1,512]{1,0:T(1,128)}, u32[]{:S(2)}) copy-start(f32[1,512]{1,0:T(1,128)} %get-tuple-element.126) | copy-start | bytes 6148
  214.1 23.4 %copy-start.4 = (bf16[1024,512]{1,0:T(8,128)(2,1)S(1)}, bf16[1024,512]{1,0:T(8,128)(2,1)}, u32[]{:S(2)}) copy-start(bf16[1024,512]{1,0:T(8,128)(2,1)} %reduce-scatter.4.cloned.1.call-done) | copy-start | bytes 3145732
  214.1 23.4 %copy-start.22 = (f32[1024]{0:T(1024)S(1)}, f32[1024]{0:T(1024)}, u32[]{:S(2)}) copy-start(f32[1024]{0:T(1024)} %multiply_add_fusion.3) | copy-start | bytes 12292
  214.1 23.4 %copy-start.25 = (f32[512]{0:T(512)S(1)}, f32[512]{0:T(512)}, u32[]{:S(2)}) copy-start(f32[512]{0:T(512)} %get-tuple-element.116) | copy-start | bytes 6148
  214.1 23.4 %copy-start.26 = (f32[512]{0:T(512)S(1)}, f32[512]{0:T(512)}, u32[]{:S(2)}) copy-start(f32[512]{0:T(512)} %get-tuple-element.117) | copy-start | bytes 6148
  214.1 27.5 %copy-start.9 = (s32[4096]{0:T(1024)S(1)}, s32[4096]{0:T(1024)}, u32[]{:S(2)}) copy-start(s32[4096]{0:T(1024)} %param.25) | copy-start | bytes 49156
  237.5 38.7 %copy-start.17 = (f32[4096]{0:T(1024)S(1)}, f32[4096]{0:T(1024)}, u32[]{:S(2)}) copy-start(f32[4096]{0:T(1024)} %param.40) | copy-start | bytes 49156
  241.5 272.5 %all-reduce.4.cloned.1.call-start = ((), (), s32[]{:S(2)}) async-start(), calls=%async_computation.7 | async-start | bytes 16777216 | tf_op jit(solution)/shard_map/psum | solution.py:162
  361.0 359.2 %reduce-scatter.8.cloned.1.call-start = ((), (), s32[]{:S(2)}) async-start(), calls=%async_computation.9 | async-start | bytes 9437184 | tf_op jit(solution)/shard_map/reduce_scatter | solution.py:190
  361.1 153.0 %copy-start.13 = (f32[512]{0:T(512)S(1)}, f32[512]{0:T(512)}, u32[]{:S(2)}) copy-start(f32[512]{0:T(512)} %param.43) | copy-start | bytes 6148
  435.7 84.4 %copy-start.10 = (s32[4096]{0:T(1024)S(1)}, s32[4096]{0:T(1024)}, u32[]{:S(2)}) copy-start(s32[4096]{0:T(1024)} %param.25) | copy-start | bytes 49156
  435.7 108.6 %copy-start.11 = (f32[4096]{0:T(1024)S(1)}, f32[4096]{0:T(1024)}, u32[]{:S(2)}) copy-start(f32[4096]{0:T(1024)} %fusion.17) | copy-start | bytes 49156
  545.0 8.1 copy-start.3
  551.1 2.0 copy-start.5
  576.2 294.8 %reduce-scatter.6.cloned.1.call-start = ((), (), s32[]{:S(2)}) async-start(), calls=%async_computation.8 | async-start | bytes 9437184 | tf_op jit(solution)/shard_map/reduce_scatter | solution.py:189
  646.7 2.0 copy-start.21
  646.7 271.0 %copy-start.14 = (f32[512]{0:T(512)S(1)}, f32[512]{0:T(512)}, u32[]{:S(2)}) copy-start(f32[512]{0:T(512)} %param.43) | copy-start | bytes 6148
  646.7 271.0 %copy-start.27 = (f32[512]{0:T(512)S(1)}, f32[512]{0:T(512)}, u32[]{:S(2)}) copy-start(f32[512]{0:T(512)} %param.44) | copy-start | bytes 6148
  646.7 271.0 %copy-start.28 = (f32[512]{0:T(512)S(1)}, f32[512]{0:T(512)}, u32[]{:S(2)}) copy-start(f32[512]{0:T(512)} %param.45) | copy-start | bytes 6148
  646.7 271.6 %copy-start.18 = (f32[4096]{0:T(1024)S(1)}, f32[4096]{0:T(1024)}, u32[]{:S(2)}) copy-start(f32[4096]{0:T(1024)} %param.41) | copy-start | bytes 49156
  646.7 271.6 %copy-start.19 = (f32[4096]{0:T(1024)S(1)}, f32[4096]{0:T(1024)}, u32[]{:S(2)}) copy-start(f32[4096]{0:T(1024)} %param.42) | copy-start | bytes 49156
  646.8 273.0 %copy-start.7 = (f32[4096,64]{0,1:T(8,128)S(1)}, f32[4096,64]{0,1:T(8,128)}, u32[]{:S(2)}) copy-start(f32[4096,64]{0,1:T(8,128)} %param.37) | copy-start | bytes 3145732
  646.8 227.6 %all-reduce.6.cloned.1.call-start = ((), (), s32[]{:S(2)}) async-start(), calls=%async_computation.10 | async-start | bytes 131072 | tf_op jit(solution)/shard_map/psum | solution.py:184
  648.7 0.6 copy-start.8
  649.3 278.8 %copy-start.1 = (bf16[2048,512]{1,0:T(8,128)(2,1)S(1)}, bf16[2048,512]{1,0:T(8,128)(2,1)}, u32[]{:S(2)}) copy-start(bf16[2048,512]{1,0:T(8,128)(2,1)} %param.33) | copy-start | bytes 6291460
Sparse Core Ops, SparseCore 0:
  39.8 47.2 reduce-scatter.3
  361.2 152.8 all-reduce.3
  654.7 192.7 all-reduce.5
Sparse Core Ops, SparseCore 1:
  42.9 75.6 all-gather.7
  121.1 71.3 all-gather.5
  241.6 34.5 all-gather.3
  576.3 144.0 reduce-scatter.7
  723.9 147.0 reduce-scatter.5
where the time goes:
time: 943 us; the launch traced here: 937 us
  waiting for transfers between devices  370 us (39%)
  matrix products  322 us (34%)
  other arithmetic  103 us (11%)
  blocking collectives  61.4 us (7%)
  local copies, waits for them, and re-layouts  51.7 us (5%)
  between operations  23.6 us (3%)
    reduce_scatter x1, waiting for transfers between devices, body(): lax.psum_scatter(grad_enc, 'rows', scatter_dimension=0, tiled=True)  149 us
    psum x1, waiting for transfers between devices, body(): recon = lax.psum(partial_recon, 'lat') + dec_bias  78.3 us
    dot_general x1, matrix products, body(): active_mass = jnp.dot(mask_float, active, precision=lax.Precision.HIGHEST)  74.6 us
    reduce_scatter x1, waiting for transfers between devices, body(): lax.psum_scatter(grad_dec, 'rows', scatter_dimension=1, tiled=True)  71 us
    dot_general x1, matrix products, body(): jnp.dot(all_inputs, enc_low, preferred_element_type=jnp.float32) + enc_bias  59.8 us
    dot_general x2, matrix products, contract_rows(): lax.dot_general(left, right, (((0,), (0,)), ((), ())), preferred_element_...  47.2 us
    dot_general x1, matrix products, contract_cols(): lax.dot_general(left, right, (((1,), (1,)), ((), ())), preferred_element_...  46.4 us
    sub x2, other arithmetic, attend(): jax.nn.softmax(jnp.where(causal, scores, -1e+30), axis=-1)  43.3 us
  transfers between devices with their start and end apart: 8, of which 5 were waited for; matrix products, arithmetic and copies ran while one was open for 33% of the time, Pallas kernels for 0%

commit v1 on v0

--- a/solution.py
+++ b/solution.py
@@ -1,11 +1,21 @@
+import functools
 import jax
 import jax.numpy as jnp
 from jax import lax
+from jax.experimental import pallas as pl
+from jax.experimental.pallas import tpu as pltpu
 from jax.sharding import PartitionSpec as P
 
 HEADS = 8
 ROT = 16
 STEP = 10
+Z_CHIPS = 4
+CORES = 2
+SLOTS = 6
+CHUNK = 1024
+MESH = pl.DeviceIdType.MESH
+f32 = jnp.float32
+bf16 = jnp.bfloat16
 
 
 lasso_coef = 5.0
@@ -35,18 +45,6 @@
     return jnp.concatenate([head * cosines + turned * sines, values[..., rotated:]], -1)
 
 
-def contract_rows(left, right):
-    return lax.dot_general(
-        left, right, (((0,), (0,)), ((), ())), preferred_element_type=jnp.float32
-    )
-
-
-def contract_cols(left, right):
-    return lax.dot_general(
-        left, right, (((1,), (1,)), ((), ())), preferred_element_type=jnp.float32
-    )
-
-
 def frozen_layer(embedded, norm_params, frozen_bias, w_joined, w_attn_out, w_mlp_in, w_mlp_out):
     length, width = embedded.shape
     head_dim = width // HEADS
@@ -99,6 +97,501 @@
     scaled = jnp.sqrt(second_new / (1.0 - beta_two**STEP)) + adam_eps
     weight_new = weight - learn_rate * (corrected / scaled + decay * weight)
     return (weight_new, moment_new, second_new)
+
+
+def softplus_parts(value):
+    power = jnp.exp(value)
+    grown = jnp.log(1.0 + power)
+    grown = jnp.where(power < 2.0**-8, power * (1.0 - 0.5 * power), grown)
+    active = jnp.where(value > 30.0, value, grown)
+    return active, jnp.exp(value - active)
+
+
+def forward_kernel(
+    lat_size,
+    inputs_ref, enc_ref, dec_ref, enc_bias_ref, mask_ref, dec_bias_ref, scale_ref,
+    active_hbm, slope_hbm, mass_out, back_out, stats_out,
+    active_buf, slope_buf, product, partial, own, send_two, recv_one, recv_two,
+    active_sem, slope_sem, out_one, in_one, out_two, in_two, out_three, in_three, out_four, in_four,
+):
+    tokens, depth = inputs_ref.shape
+    latents = enc_ref.shape[1]
+    chunk, span = product.shape[1:]
+    width = active_hbm.shape[2]
+    chunks, spans = tokens // chunk, latents // span
+    y_size = lat_size // CORES
+    share = chunk // lat_size
+    strip = 16
+    row = lax.axis_index("rows")
+    lat = lax.axis_index("lat")
+    my_y, core = lat // CORES, lax.rem(lat, CORES)
+    other = 1 - core
+
+    def y_peer(step):
+        return lax.rem(my_y + step, y_size)
+
+    def share_rows(y, which_core):
+        return pl.multiple_of((y * CORES + which_core) * share, share)
+
+    def token_rows(block, y, which_core):
+        return pl.ds(pl.multiple_of(block * chunk + (y * CORES + which_core) * share, share), share)
+
+    def remote(src, dst, send, recv, target):
+        return pltpu.make_async_remote_copy(
+            src_ref=src, dst_ref=dst, send_sem=send, recv_sem=recv,
+            device_id=(row, target), device_id_type=MESH)
+
+    def copy_one(block, y):
+        slot = lax.rem(block, 2)
+        return remote(
+            partial.at[slot, pl.ds(share_rows(y, other), share)], recv_one.at[block, y],
+            out_one.at[slot, y], in_one.at[block, y], my_y * CORES + other)
+
+    def copy_two(block, step):
+        slot = lax.rem(block, 2)
+        return remote(
+            send_two.at[slot, step - 1], recv_two.at[block, step - 1],
+            out_two.at[slot, step - 1], in_two.at[block, step - 1], y_peer(step) * CORES + core)
+
+    def copy_three(block, step):
+        mine = back_out.at[token_rows(block, my_y, core)]
+        return remote(
+            mine, mine, out_three.at[block, step - 1], in_three.at[block, step - 1], y_peer(step) * CORES + core)
+
+    def copy_four(block, y):
+        mine = back_out.at[token_rows(block, y, core)]
+        return remote(mine, mine, out_four.at[block, y], in_four.at[block, y], my_y * CORES + other)
+
+    def stores(block, at, slot):
+        rows = pl.ds(pl.multiple_of(block * chunk, chunk), chunk)
+        copies = []
+        for part in range(span // width):
+            lanes = pl.ds(part * width, width)
+            copies.append(pltpu.make_async_copy(
+                active_buf.at[slot, :, lanes], active_hbm.at[at * (span // width) + part, rows], active_sem.at[slot, part]))
+            copies.append(pltpu.make_async_copy(
+                slope_buf.at[slot, :, lanes], slope_hbm.at[at * (span // width) + part, rows], slope_sem.at[slot, part]))
+        return copies
+
+    barrier = pltpu.get_barrier_semaphore()
+    pl.semaphore_signal(barrier, inc=1, device_id=(row, my_y * CORES + other), device_id_type=MESH)
+    for step in range(1, y_size):
+        pl.semaphore_signal(barrier, inc=1, device_id=(row, y_peer(step) * CORES + core), device_id_type=MESH)
+    mass_out[...] = jnp.zeros_like(mass_out)
+    stats_out[...] = jnp.zeros_like(stats_out)
+    pl.semaphore_wait(barrier, y_size)
+
+    def compute(block):
+        place = lax.rem(block, 2)
+        first = pl.multiple_of(block * chunk, chunk)
+
+        @pl.when(block >= 2)
+        def _():
+            for y in range(y_size):
+                copy_one(block - 2, y).wait_send()
+
+        for at in range(spans):
+            slot = at % 2
+            if at >= 2:
+                for copy in stores(block, at - 2, slot):
+                    copy.wait()
+            else:
+                @pl.when(block > 0)
+                def _():
+                    for copy in stores(block - 1, spans - 2 + at, slot):
+                        copy.wait()
+
+            product[slot] = jnp.dot(
+                inputs_ref[pl.ds(first, chunk), :], enc_ref[:, at * span : (at + 1) * span], preferred_element_type=f32)
+            for left in range(0, span, width):
+                lanes = pl.ds(left, width)
+                cols = pl.ds(at * span + left, width)
+                shift = enc_bias_ref[:, cols]
+                total = mass_out[:, cols]
+                for top in range(0, chunk, strip):
+                    rows = pl.ds(top, strip)
+                    mask = mask_ref[pl.ds(first + top, strip), :]
+                    mask = jnp.concatenate([mask] * (width // 128), axis=1)
+                    active, slope = softplus_parts(product[slot, rows, lanes] + shift)
+                    active_buf[slot, rows, lanes] = active.astype(bf16)
+                    slope_buf[slot, rows, lanes] = slope * mask
+                    total = total + (active * mask).reshape(strip // 8, 8, width).sum(0)
+                mass_out[:, cols] = total
+            for copy in stores(block, at, slot):
+                copy.start()
+            part = lax.dot_general(
+                active_buf[slot], dec_ref[:, at * span : (at + 1) * span], (((1,), (1,)), ((), ())),
+                preferred_element_type=f32)
+            partial[place] = part if at == 0 else partial[place] + part
+
+    def exchange(block):
+        slot = lax.rem(block, 2)
+        for y in range(y_size):
+            copy_one(block, y).start()
+        for y in range(y_size):
+            copy_one(block, y).wait_recv()
+        for step in list(range(1, y_size)) + [0]:
+            y = y_peer(step)
+            total = partial[slot, pl.ds(share_rows(y, core), share), :] + recv_one[block, y]
+            if step == 0:
+                own[slot] = total
+            else:
+                @pl.when(block >= 2)
+                def _():
+                    copy_two(block - 2, step).wait_send()
+
+                send_two[slot, step - 1] = total
+                copy_two(block, step).start()
+
+    def settle(block):
+        slot = lax.rem(block, 2)
+        rows = token_rows(block, my_y, core)
+        total = own[slot]
+        for step in range(1, y_size):
+            copy_two(block, step).wait_recv()
+            total = total + recv_two[block, step - 1]
+        error = total + dec_bias_ref[...] - inputs_ref[rows, :].astype(f32)
+        mask = jnp.concatenate([mask_ref[rows, :]] * (depth // 128), axis=1)
+        low = (scale_ref[...] * mask * error).astype(bf16)
+        back_out[rows, :] = low
+        stats_out[0:8, :] += (mask * error * error).reshape(share // 8, 8, depth).sum(0)
+        stats_out[8:16, :] += low.astype(f32).reshape(share // 8, 8, depth).sum(0)
+        for step in range(1, y_size):
+            copy_three(block, step).start()
+
+    def spread(block):
+        for step in range(1, y_size):
+            copy_three(block, step).wait_recv()
+        for y in range(y_size):
+            copy_four(block, y).start()
+
+    def turn(block, carry):
+        @pl.when(block < chunks)
+        def _():
+            compute(block)
+            exchange(block)
+
+        @pl.when((block >= 1) & (block <= chunks))
+        def _():
+            settle(block - 1)
+
+        @pl.when(block >= 2)
+        def _():
+            spread(block - 2)
+
+        return carry
+
+    lax.fori_loop(0, chunks + 2, turn, 0)
+    for slot in range(2):
+        for copy in stores(chunks - 1, spans - 2 + slot, slot):
+            copy.wait()
+    for block in range(chunks - 2, chunks):
+        for y in range(y_size):
+            copy_one(block, y).wait_send()
+        for step in range(1, y_size):
+            copy_two(block, step).wait_send()
+
+    def drain(block, carry):
+        for step in range(1, y_size):
+            copy_three(block, step).wait_send()
+        for y in range(y_size):
+            copy_four(block, y).wait_send()
+            copy_four(block, y).wait_recv()
+        return carry
+
+    lax.fori_loop(0, chunks, drain, 0)
+
+
+def forward(lat_size, inputs, enc_low, dec_cols, enc_bias_row, mask_lanes, dec_bias_row, scale_row):
+    tokens, depth = inputs.shape
+    latents = enc_low.shape[1]
+    chunk, span, width = 512, 1024, (512 if tokens <= 4096 else 256)
+    chunks = tokens // chunk
+    y_size = lat_size // CORES
+    share = chunk // lat_size
+    dma = pltpu.SemaphoreType.DMA
+    vmem = pl.BlockSpec(memory_space=pltpu.VMEM)
+    hbm = pl.BlockSpec(memory_space=pl.ANY)
+    return pl.pallas_call(
+        functools.partial(forward_kernel, lat_size),
+        out_shape=[
+            jax.ShapeDtypeStruct((latents // width, tokens, width), bf16),
+            jax.ShapeDtypeStruct((latents // width, tokens, width), f32),
+            jax.ShapeDtypeStruct((8, latents), f32),
+            jax.ShapeDtypeStruct((tokens, depth), bf16),
+            jax.ShapeDtypeStruct((16, depth), f32),
+        ],
+        in_specs=[vmem] * 7,
+        out_specs=[hbm, hbm, vmem, vmem, vmem],
+        scratch_shapes=[
+            pltpu.VMEM((2, chunk, span), bf16),
+            pltpu.VMEM((2, chunk, span), f32),
+            pltpu.VMEM((2, chunk, span), f32),
+            pltpu.VMEM((2, chunk, depth), f32),
+            pltpu.VMEM((2, share, depth), f32),
+            pltpu.VMEM((2, y_size - 1, share, depth), f32),
+            pltpu.VMEM((chunks, y_size, share, depth), f32),
+            pltpu.VMEM((chunks, y_size - 1, share, depth), f32),
+            dma((2, span // width)), dma((2, span // width)),
+            dma((2, y_size)), dma((chunks, y_size)),
+            dma((2, y_size - 1)), dma((chunks, y_size - 1)),
+            dma((chunks, y_size - 1)), dma((chunks, y_size - 1)),
+            dma((chunks, y_size)), dma((chunks, y_size)),
+        ],
+        compiler_params=pltpu.CompilerParams(
+            collective_id=1, has_side_effects=True, vmem_limit_bytes=60 * 2**20),
+        name="forward",
+    )(inputs, enc_low, dec_cols, enc_bias_row, mask_lanes, dec_bias_row, scale_row)
+
+
+def encode(value):
+    top = jnp.max(jnp.abs(value), axis=0, keepdims=True)
+    unit = jnp.where(top > 0.0, 32766.0 / top, 0.0)
+    shifted = value * unit + 12582912.0
+    return (shifted - 12582912.0).astype(jnp.int32).astype(jnp.int16), top * (1.0 / 32766.0)
+
+
+def decode(code, unit):
+    return code.astype(jnp.int32).astype(f32) * unit
+
+
+def put_units(ref, index, unit):
+    for piece in range(unit.shape[1] // 128):
+        ref[index + (pl.ds(piece, 1), slice(None))] = unit[:, piece * 128 : piece * 128 + 128]
+
+
+def get_units(ref, index, width):
+    return jnp.concatenate(
+        [ref[index + (pl.ds(piece, 1), slice(None))] for piece in range(width // 128)], axis=1)
+
+
+def backward_kernel(
+    rows_size,
+    inputs_ref, back_ref, dec_ref, lasso_ref, active_hbm, slope_hbm,
+    enc_out, dec_out, bias_out,
+    grad_low, active_buf, slope_buf, sums,
+    send_one, units_one, recv_one, got_one,
+    send_two, units_two, recv_two, got_two,
+    active_sem, slope_sem,
+    out_one, in_one, outu_one, inu_one, out_two, in_two, outu_two, inu_two,
+):
+    blocks, tokens, width = active_hbm.shape
+    chunk = slope_buf.shape[1]
+    chunks = tokens // chunk
+    shard = enc_out.shape[0]
+    x_size = rows_size // Z_CHIPS
+    row = lax.axis_index("rows")
+    lat = lax.axis_index("lat")
+    my_z, my_x = row // x_size, lax.rem(row, x_size)
+
+    def x_peer(step):
+        return lax.rem(my_x + step, x_size)
+
+    def z_peer(step):
+        return lax.rem(my_z + step, Z_CHIPS)
+
+    def active_copy(block):
+        slot = lax.rem(block, 2)
+        return pltpu.make_async_copy(active_hbm.at[block], active_buf.at[slot], active_sem.at[slot])
+
+    def slope_copy(index):
+        slot = lax.rem(index, slope_buf.shape[0])
+        return pltpu.make_async_copy(
+            slope_hbm.at[index // chunks, pl.ds(pl.multiple_of(lax.rem(index, chunks) * chunk, chunk), chunk)],
+            slope_buf.at[slot],
+            slope_sem.at[slot],
+        )
+
+    def copies(stage, block, which, step):
+        slot = lax.rem(block, 2)
+        if stage == 0:
+            target = (my_z * x_size + x_peer(step), lat)
+            refs = (send_one, recv_one, out_one, in_one, units_one, got_one, outu_one, inu_one)
+        else:
+            target = (z_peer(step) * x_size + my_x, lat)
+            refs = (send_two, recv_two, out_two, in_two, units_two, got_two, outu_two, inu_two)
+        return [
+            pltpu.make_async_remote_copy(
+                src_ref=refs[at].at[slot, which, step - 1], dst_ref=refs[at + 1].at[block, which, step - 1],
+                send_sem=refs[at + 2].at[slot, which, step - 1], recv_sem=refs[at + 3].at[block, which, step - 1],
+                device_id=target, device_id_type=MESH)
+            for at in (0, 4)
+        ]
+
+    barrier = pltpu.get_barrier_semaphore()
+    for step in range(1, x_size):
+        pl.semaphore_signal(barrier, inc=1, device_id=(my_z * x_size + x_peer(step), lat), device_id_type=MESH)
+    for step in range(1, Z_CHIPS):
+        pl.semaphore_signal(barrier, inc=1, device_id=(z_peer(step) * x_size + my_x, lat), device_id_type=MESH)
+    active_copy(0).start()
+    ahead = slope_buf.shape[0] - 1
+    for index in range(ahead):
+        slope_copy(index).start()
+    pl.semaphore_wait(barrier, x_size + Z_CHIPS - 2)
+
+    def columns(block):
+        return pl.ds(pl.multiple_of(block * width, width), width)
+
+    over_tokens = (((0,), (0,)), ((), ()))
+
+    def compute_dec(block):
+        slot = lax.rem(block, 2)
+
+        @pl.when(block + 1 < blocks)
+        def _():
+            active_copy(block + 1).start()
+
+        active_copy(block).wait()
+        sums[slot, 1] = lax.dot_general(back_ref[...], active_buf[slot], over_tokens, preferred_element_type=f32)
+
+    def compute_enc(block):
+        slot = lax.rem(block, 2)
+        cols = columns(block)
+
+        def piece(index, total):
+            at = block * chunks + index
+
+            @pl.when(at + ahead < blocks * chunks)
+            def _():
+                slope_copy(at + ahead).start()
+
+            slope_copy(at).wait()
+            rows = pl.ds(pl.multiple_of(index * chunk, chunk), chunk)
+            back = jnp.dot(back_ref[rows, :], dec_ref[:, cols], preferred_element_type=f32)
+            low = ((back + lasso_ref[:, cols]) * slope_buf[lax.rem(at, ahead + 1)]).astype(bf16)
+            grad_low[rows, :] = low
+            return total + low.astype(f32).reshape(chunk // 8, 8, width).sum(0)
+
+        bias_out[:, cols] = lax.fori_loop(0, chunks, piece, jnp.zeros((8, width), f32))
+        sums[slot, 0] = lax.dot_general(inputs_ref[...], grad_low[...], over_tokens, preferred_element_type=f32)
+
+    def send_x(block, which):
+        slot = lax.rem(block, 2)
+        for step in range(1, x_size):
+            @pl.when(block >= 2)
+            def _():
+                for copy in copies(0, block - 2, which, step):
+                    copy.wait_send()
+
+            parts = []
+            for z in range(Z_CHIPS):
+                first = pl.multiple_of((z * x_size + x_peer(step)) * shard, shard)
+                parts.append(sums[slot, which, pl.ds(first, shard), :])
+            code, unit = encode(jnp.concatenate(parts, axis=0))
+            for z in range(Z_CHIPS):
+                send_one[slot, which, step - 1, z] = code[z * shard : (z + 1) * shard]
+            put_units(units_one, (slot, which, step - 1), unit)
+            for copy in copies(0, block, which, step):
+                copy.start()
+
+    def send_z(block, which):
+        slot = lax.rem(block, 2)
+        for step in range(1, x_size):
+            for copy in copies(0, block, which, step):
+                copy.wait_recv()
+        for step in range(Z_CHIPS):
+            z = z_peer(step)
+            if step:
+                @pl.when(block >= 2)
+                def _():
+                    for copy in copies(1, block - 2, which, step):
+                        copy.wait_send()
+
+            first = pl.multiple_of((z * x_size + my_x) * shard, shard)
+            total = sums[slot, which, pl.ds(first, shard), :]
+            for x_step in range(1, x_size):
+                total = total + decode(
+                    recv_one[block, which, x_step - 1, z], get_units(got_one, (block, which, x_step - 1), width))
+            if step == 0:
+                (enc_out, dec_out)[which][:, columns(block)] = total
+            else:
+                code, unit = encode(total)
+                send_two[slot, which, step - 1] = code
+                put_units(units_two, (slot, which, step - 1), unit)
+                for copy in copies(1, block, which, step):
+                    copy.start()
+
+    def finish(block, which):
+        slot = lax.rem(block, 2)
+        for step in range(1, Z_CHIPS):
+            for copy in copies(1, block, which, step):
+                copy.wait_recv()
+        out, cols = (enc_out, dec_out)[which], columns(block)
+        total = out[:, cols]
+        for step in range(1, Z_CHIPS):
+            total = total + decode(
+                recv_two[block, which, step - 1], get_units(got_two, (block, which, step - 1), width))
+        out[:, cols] = total
+
+    def turn(block, carry):
+        for which, compute in ((1, compute_dec), (0, compute_enc)):
+            @pl.when(block < blocks)
+            def _():
+                compute(block)
+                send_x(block, which)
+
+            @pl.when((block >= 1) & (block <= blocks))
+            def _():
+                send_z(block - 1, which)
+
+            @pl.when(block >= 2)
+            def _():
+                finish(block - 2, which)
+
+        return carry
+
+    lax.fori_loop(0, blocks + 2, turn, 0)
+    for block in range(max(blocks - 2, 0), blocks):
+        for which in range(2):
+            for stage, size in ((0, x_size), (1, Z_CHIPS)):
+                for step in range(1, size):
+                    for copy in copies(stage, block, which, step):
+                        copy.wait_send()
+
+
+def backward(rows_size, inputs, back, dec_cols, lasso_row, active, slope):
+    blocks, tokens, width = active.shape
+    depth = inputs.shape[1]
+    shard = depth // rows_size
+    latents = dec_cols.shape[1]
+    x_size = rows_size // Z_CHIPS
+    chunk = min(CHUNK, tokens)
+    i16 = jnp.int16
+    dma = pltpu.SemaphoreType.DMA
+    vmem = pl.BlockSpec(memory_space=pltpu.VMEM)
+    hbm = pl.BlockSpec(memory_space=pl.ANY)
+    return pl.pallas_call(
+        functools.partial(backward_kernel, rows_size),
+        out_shape=[
+            jax.ShapeDtypeStruct((shard, latents), f32),
+            jax.ShapeDtypeStruct((shard, latents), f32),
+            jax.ShapeDtypeStruct((8, latents), f32),
+        ],
+        in_specs=[vmem] * 4 + [hbm] * 2,
+        out_specs=[vmem] * 3,
+        scratch_shapes=[
+            pltpu.VMEM((tokens, width), bf16),
+            pltpu.VMEM((2, tokens, width), bf16),
+            pltpu.VMEM((SLOTS, chunk, width), f32),
+            pltpu.VMEM((2, 2, depth, width), f32),
+            pltpu.VMEM((2, 2, x_size - 1, Z_CHIPS, shard, width), i16),
+            pltpu.VMEM((2, 2, x_size - 1, 8, 128), f32),
+            pltpu.VMEM((blocks, 2, x_size - 1, Z_CHIPS, shard, width), i16),
+            pltpu.VMEM((blocks, 2, x_size - 1, 8, 128), f32),
+            pltpu.VMEM((2, 2, Z_CHIPS - 1, shard, width), i16),
+            pltpu.VMEM((2, 2, Z_CHIPS - 1, 8, 128), f32),
+            pltpu.VMEM((blocks, 2, Z_CHIPS - 1, shard, width), i16),
+            pltpu.VMEM((blocks, 2, Z_CHIPS - 1, 8, 128), f32),
+            dma((2,)), dma((SLOTS,)),
+            dma((2, 2, x_size - 1)), dma((blocks, 2, x_size - 1)),
+            dma((2, 2, x_size - 1)), dma((blocks, 2, x_size - 1)),
+            dma((2, 2, Z_CHIPS - 1)), dma((blocks, 2, Z_CHIPS - 1)),
+            dma((2, 2, Z_CHIPS - 1)), dma((blocks, 2, Z_CHIPS - 1)),
+        ],
+        compiler_params=pltpu.CompilerParams(
+            collective_id=2, has_side_effects=True, vmem_limit_bytes=60 * 2**20),
+        name="backward",
+    )(inputs, back, dec_cols, lasso_row, active, slope)
 
 
 def body(
@@ -129,76 +622,51 @@
     lat_index = lax.axis_index("lat")
     group_tokens = token_ids.shape[0]
     tok_local = group_tokens // lat_size
-    lat_local = enc_bias.shape[0]
-    mask_float = token_mask.astype(jnp.float32)
-    enc_low = lax.all_gather(enc_weight.astype(jnp.bfloat16), "rows", axis=0, tiled=True)
-    dec_full = lax.all_gather(dec_weight.astype(jnp.bfloat16), "rows", axis=1, tiled=True).astype(
-        dec_weight.dtype
-    )
+    rows_size = lax.axis_size("rows")
+    depth = enc_weight.shape[0] * rows_size
+    mask_float = token_mask.astype(f32)
+    dec_master = dec_weight.T
+    enc_low = lax.all_gather(enc_weight.astype(bf16), "rows", axis=0, tiled=True)
+    dec_cols = lax.all_gather(dec_master.astype(bf16), "rows", axis=0, tiled=True)
     count = lax.psum(jnp.sum(mask_float), "rows")
+    norms = jnp.sqrt(lax.psum(jnp.sum(dec_master * dec_master, axis=0), "rows"))
     vocab_local = embed.shape[0]
     vocab_first = lat_index * vocab_local
     local_ids = token_ids - vocab_first
-    inside = ((local_ids >= 0) & (local_ids < vocab_local)).astype(jnp.float32)
-    picked = jnp.take(embed, jnp.clip(local_ids, 0, vocab_local - 1), axis=0).astype(jnp.float32)
+    inside = ((local_ids >= 0) & (local_ids < vocab_local)).astype(f32)
+    picked = jnp.take(embed, jnp.clip(local_ids, 0, vocab_local - 1), axis=0).astype(f32)
     embedded = lax.psum_scatter(
-        (picked * inside[:, None]).astype(jnp.bfloat16), "lat", scatter_dimension=0, tiled=True
-    ).astype(jnp.float32)
+        (picked * inside[:, None]).astype(bf16), "lat", scatter_dimension=0, tiled=True
+    ).astype(f32)
     own_first = lat_index * tok_local
     residual = frozen_layer(
         embedded, norm_params, frozen_bias, w_joined, w_attn_out, w_mlp_in, w_mlp_out
     )
-    scales = 0.5 + 0.25 * lax.dynamic_slice_in_dim(scale_index, own_first, tok_local).astype(
-        jnp.float32
-    )
-    own_inputs = (residual * scales[:, None]).astype(jnp.bfloat16)
+    scales = 0.5 + 0.25 * lax.dynamic_slice_in_dim(scale_index, own_first, tok_local).astype(f32)
+    own_inputs = (residual * scales[:, None]).astype(bf16)
     all_inputs = lax.all_gather(own_inputs, "lat", axis=0, tiled=True)
-    preact = jnp.dot(all_inputs, enc_low, preferred_element_type=jnp.float32) + enc_bias
-    active = jax.nn.softplus(preact)
-    active_low = active.astype(jnp.bfloat16)
-    norms = jnp.sqrt(jnp.sum(dec_full * dec_full, axis=1))
-    dec_low = dec_full.astype(jnp.bfloat16)
-    partial_recon = jnp.dot(active_low, dec_low, preferred_element_type=jnp.float32)
-    recon = lax.psum(partial_recon, "lat") + dec_bias
-    error_rows = recon - all_inputs.astype(jnp.float32)
-    leader = (lat_index == 0).astype(jnp.float32)
-    square_part = jnp.sum(mask_float * jnp.sum(error_rows * error_rows, axis=1)) * leader
-    recon_grad = (2.0 / count * mask_float[:, None] * error_rows).astype(jnp.bfloat16)
-    bias_part = jnp.sum(recon_grad, axis=0, dtype=jnp.float32) * leader
-    active_mass = jnp.dot(mask_float, active, precision=lax.Precision.HIGHEST)
-    lasso_part = lasso_coef * jnp.sum(active_mass * norms)
+    mask_lanes = jnp.broadcast_to(mask_float[:, None], (group_tokens, 128))
+    scale_row = jnp.full((1, depth), 2.0 / count, f32)
     lasso_scale = lasso_coef / count
-    grad_dec = (
-        contract_rows(active_low, recon_grad)
-        + (lasso_scale * active_mass / norms)[:, None] * dec_full
-    )
-    grad_active = (
-        contract_cols(recon_grad, dec_low) + lasso_scale * mask_float[:, None] * norms[None, :]
-    )
-    grad_preact = (grad_active * jax.nn.sigmoid(preact)).astype(jnp.bfloat16)
-    grad_enc = contract_rows(all_inputs, grad_preact)
-    enc_bias_part = jnp.sum(grad_preact, axis=0, dtype=jnp.float32)
-    placed_bias = lax.dynamic_update_slice(
-        jnp.zeros((lat_local * lat_size,), jnp.float32), enc_bias_part, (lat_index * lat_local,)
-    )
-    loss_sum, grad_dec_bias, placed_sum = lax.psum(
-        (square_part + lasso_part, bias_part, placed_bias), ("rows", "lat")
-    )
-    grad_enc_bias = lax.dynamic_slice_in_dim(placed_sum, lat_index * lat_local, lat_local)
-    grad_enc, grad_dec = (
-        lax.psum_scatter(grad_enc, "rows", scatter_dimension=0, tiled=True),
-        lax.psum_scatter(grad_dec, "rows", scatter_dimension=1, tiled=True),
-    )
-    local_squares = jnp.sum(grad_enc * grad_enc) + jnp.sum(grad_dec * grad_dec)
-    squares = (
-        lax.psum(local_squares, ("rows", "lat"))
-        + jnp.sum(placed_sum * placed_sum)
-        + jnp.sum(grad_dec_bias * grad_dec_bias)
-    )
+    active, slope, mass_rows, recon_grad, stats = forward(
+        lat_size, all_inputs, enc_low, dec_cols, enc_bias[None, :], mask_lanes, dec_bias[None, :], scale_row)
+    grad_enc, grad_dec, bias_rows = backward(
+        rows_size, all_inputs, recon_grad, dec_cols, (lasso_scale * norms)[None, :], active, slope)
+    bias_mass = jnp.stack([bias_rows.sum(0), mass_rows.sum(0)])
+    grad_enc_bias, active_mass = lax.psum(bias_mass, "rows")
+    leader = (lax.axis_index("rows") == 0).astype(f32)
+    lasso_part = lasso_coef * jnp.sum(active_mass * norms) * leader
+    loss_sum, grad_dec_bias = lax.psum((jnp.sum(stats[:8]) + lasso_part, stats[8:].sum(0)), ("rows", "lat"))
+    grad_dec = grad_dec + (lasso_scale * active_mass / norms)[None, :] * dec_master
+    local_squares = (
+        jnp.sum(grad_enc * grad_enc) + jnp.sum(grad_dec * grad_dec)
+        + jnp.sum(grad_enc_bias * grad_enc_bias) * leader
+    )
+    squares = lax.psum(local_squares, ("rows", "lat")) + jnp.sum(grad_dec_bias * grad_dec_bias)
     grad_norm = jnp.sqrt(squares)
     factor = clip_bound / jnp.maximum(grad_norm, clip_bound)
     enc_new = adam_update(enc_weight, enc_moment, enc_second, grad_enc * factor, weight_decay)
-    dec_new = adam_update(dec_weight, dec_moment, dec_second, grad_dec * factor, weight_decay)
+    dec_new = adam_update(dec_weight, dec_moment, dec_second, grad_dec.T * factor, weight_decay)
     enc_bias_new = adam_update(
         enc_bias, enc_bias_moment, enc_bias_second, grad_enc_bias * factor, 0.0
     )

time: 943 us -> 618 us (0.66)
  waiting for transfers between devices: 370 us -> 41 us
  matrix products: 322 us -> 68.8 us
  Pallas kernels: 0 us -> 222 us
  blocking collectives: 61.4 us -> 110 us
  other arithmetic: 103 us -> 89.7 us
    dot_general x6 -> x0, matrix products: 253 us -> none  [the longest x1 74.6 us: body(): active_mass = jnp.dot(mask_float, active, precision=lax.Precision.HIGHEST)]
    pallas_call x0 -> x2, Pallas kernels: none -> 222 us  [the longest x1 120 us: backward(): pl.pallas_call(functools.partial(backward_kernel, rows_size), out_shape=[...]
    reduce_scatter x3 -> x1, waiting for transfers between devices: 261 us -> 40.9 us  [body(): lax.psum_scatter((picked * inside[:, None]).astype(bf16), 'lat', scatter_...]
    psum x2 -> x0, waiting for transfers between devices: 78.3 us -> none  [the longest x1 78.3 us: body(): recon = lax.psum(partial_recon, 'lat') + dec_bias]
    psum x1 -> x2, blocking collectives: 39.2 us -> 71.5 us  [the longest x1 36.9 us: body(): lax.psum(local_squares, ('rows', 'lat'))]
    all_gather x1, waiting for transfers between devices: 30.9 us -> 0.01 us  [body(): all_inputs = lax.all_gather(own_inputs, 'lat', axis=0, tiled=True)]
    psum x1, blocking collectives: 22.2 us -> 38.8 us  [body(): count = lax.psum(jnp.sum(mask_float), 'rows')]
    reduce_sum x8 -> x9, other arithmetic: 22.8 us -> 10 us  [the longest x1 3 us: body(): jnp.sum(grad_dec * grad_dec)]
  transfers between devices with their start and end apart: 8 -> 4, of which waited for: 5 -> 1; matrix products, arithmetic and copies ran while one was open for 33% -> 25% of each run, Pallas kernels for 0% -> 0%
where the time goes in v1:
time: 618 us; the launch traced here: 611 us
  Pallas kernels  222 us (36%)
  blocking collectives  110 us (18%)
  other arithmetic  89.7 us (15%)
  matrix products  68.8 us (11%)
  local copies, waits for them, and re-layouts  51.6 us (8%)
  waiting for transfers between devices  41 us (7%)
  between operations  23.5 us (4%)
    pallas_call x1, Pallas kernels, backward(): pl.pallas_call(functools.partial(backward_kernel, rows_size), out_shape=[...  120 us
    pallas_call x1, Pallas kernels, forward(): pl.pallas_call(functools.partial(forward_kernel, lat_size), out_shape=[ja...  102 us
    sub x2, other arithmetic, attend(): jax.nn.softmax(jnp.where(causal, scores, -1e+30), axis=-1)  43.4 us
    reduce_scatter x1, waiting for transfers between devices, body(): lax.psum_scatter((picked * inside[:, None]).astype(bf16), 'lat', scatter_...  40.9 us
    psum x1, blocking collectives, body(): count = lax.psum(jnp.sum(mask_float), 'rows')  38.8 us
    psum x1, blocking collectives, body(): lax.psum(local_squares, ('rows', 'lat'))  36.9 us
    psum x1, blocking collectives, body(): grad_enc_bias, active_mass = lax.psum(bias_mass, 'rows')  34.6 us
    gather x1, local copies, waits for them, and re-layouts, body(): jnp.take(embed, jnp.clip(local_ids, 0, vocab_local - 1), axis=0).astype(f32)  23.8 us
  transfers between devices with their start and end apart: 4, of which 1 were waited for; matrix products, arithmetic and copies ran while one was open for 25% of the time, Pallas kernels for 0%

profile of v1, /device:TPU:0, one launch (start us, length us, event | category | flops | bytes accessed | tf_op | source)
XLA Modules:
  0.0 611.1 jit_solution(17923213106324332557)
XLA Ops:
  8.1 0.9 compare_and_fusion
  9.0 0.7 fusion.66
  9.7 23.8 %gather_fusion = bf16[4096,512]{1,0:T(8,128)(2,1)} fusion(bf16[12576,512]{1,0:T(8,128)(2,1)} %param.27, s32[4096]{0:T(1024)S(1)} %fusion.66), kind=kCustom, calls=%fused_computation | custom fusion | bytes 8404992 | tf_op jit(solution)/shard_map/jit(_take)/gather | solution.py:637
  33.5 6.2 %multiply_convert_fusion = bf16[4096,512]{1,0:T(8,128)(2,1)} fusion(f32[4096]{0:T(1024)S(1)} %get-tuple-element.141, bf16[4096,512]{1,0:T(8,128)(2,1)} %gather_fusion, pred[4096]{0:T(1024)(128)(4,1)S(1)} %get-tuple-element.140), kind=kLoop, calls=%fused_computation.37 | loop fusion | flops 8388608 | bytes 8409088 | tf_op jit(solution)/shard_map/convert_element_type | solution.py:639
  39.8 1.5 multiply_reduce_fusion.2
  41.4 2.1 convert_element_type.67
  45.0 1.3 multiply_add_fusion.2
  46.3 40.9 %reduce-scatter.2.cloned.1.call-done = bf16[1024,512]{1,0:T(8,128)(2,1)} async-done(((bf16[4096,512]{1,0:T(8,128)(2,1)}), bf16[1024,512]{1,0:T(8,128)(2,1)}) %reduce-scatter.2.cloned.1.call-update) | async-done | bytes 1048592 | tf_op jit(solution)/shard_map/reduce_scatter | solution.py:638
  87.1 1.4 convert_reduce_fusion
  88.6 1.7 fusion.37
  90.3 3.6 convolution_add_fusion
  94.0 2.7 copy-done.3
  96.7 2.4 fusion.104
  99.1 3.4 copy.50
  102.5 2.9 copy.51
  105.5 2.4 slice.122
  107.9 2.1 slice_negate_fusion
  110.0 2.4 slice.123
  112.4 1.7 slice.121
  114.1 1.3 copy.52
  115.4 1.7 fusion.60
  117.1 1.2 pad_maximum_fusion.1
  118.3 2.2 pad_maximum_fusion
  120.5 90.1 %while.11 = (s32[]{:T(128)}, bf16[2,512,8,64]{1,3,2,0:T(8,128)(2,1)}, s32[2]{0:T(128)S(1)}, bf16[1024,8,64]{0,2,1:T(8,128)(2,1)}, bf16[1024,8,64]{0,2,1:T(8,128)...) while((s32[]{:T(128)}, bf16[2,512,8,64]{1,3,2,0:T(8,128)(2,1)}, ...), condition=%wide.region_6.7_spmd.clone, body=%wide.region_3.6_spmd.clone.sunk | while | flops 1107822080 | bytes 71864976 | solution.py:75
  123.1 9.5 %fusion.123 = f32[8,512,1024]{2,1,0:T(8,128)} fusion(bf16[1024,8,64]{0,2,1:T(8,128)(2,1)S(1)} %get-tuple-element.215, bf16[1024,8,64]{0,2,1:T(8,128)(2,1)} %get-tuple-element.214, s32[]{:T(128)S(6)} %select_n.43), kind=kOutput, calls=%fused_computation.14.clone.1 | convolution fusion | flops 536870912 | bytes 18350084 | tf_op jit(solution)/shard_map/while/body/eval_jaxpr/qhd,khd->hqk/dot_general | solution.py:66
  132.6 0.6 iota_add_fusion.2
  133.2 1.2 iota_compare_fusion.2
  134.4 21.7 %fusion.124 = (f32[8,512]{1,0:T(8,128)S(1)}, f32[8,512,1024]{2,1,0:T(8,128)}) fusion(f32[8,512,1024]{2,1,0:T(8,128)} %fusion.123, pred[512,1024]{1,0:T(8,128)(4,1)} %iota_compare_fusion.2), kind=kOutput, calls=%fused_computation.157.clone.1 | output fusion | flops 25166848 | bytes 34095104 | tf_op jit(solution)/shard_map/while/body/eval_jaxpr/sub | solution.py:71
  156.1 9.6 %fusion.125 = bf16[2,512,8,64]{1,3,2,0:T(8,128)(2,1)} fusion(bf16[2,512,8,64]{1,3,2,0:T(8,128)(2,1)} %get-tuple-element.203, s32[]{:T(128)} %get-tuple-element.202, bf16[1024,8,64]{0,2,1:T(8,128)(2,1)} %get-tuple-element.216, f32[8,512,1024]{2,1,0:T(8,128)} %get-tuple-element.191, f32[8,512]{1,0:T(8,128)S(1)} %get-tuple-element.192), kind=kOutput, calls=%fused_computation.13.clone.1 | convolution fusion | flops 545259520 | bytes 18891264 | tf_op jit(solution)/shard_map/while/body/eval_jaxpr/hqk,khd->qhd/dot_general | solution.py:72
  168.2 9.3 %fusion.123 = f32[8,512,1024]{2,1,0:T(8,128)} fusion(bf16[1024,8,64]{0,2,1:T(8,128)(2,1)S(1)} %get-tuple-element.215, bf16[1024,8,64]{0,2,1:T(8,128)(2,1)} %get-tuple-element.214, s32[]{:T(128)S(6)} %select_n.43), kind=kOutput, calls=%fused_computation.14.clone.1 | convolution fusion | flops 536870912 | bytes 18350084 | tf_op jit(solution)/shard_map/while/body/eval_jaxpr/qhd,khd->hqk/dot_general | solution.py:66
  178.1 1.2 iota_compare_fusion.2
  179.2 21.7 %fusion.124 = (f32[8,512]{1,0:T(8,128)S(1)}, f32[8,512,1024]{2,1,0:T(8,128)}) fusion(f32[8,512,1024]{2,1,0:T(8,128)} %fusion.123, pred[512,1024]{1,0:T(8,128)(4,1)} %iota_compare_fusion.2), kind=kOutput, calls=%fused_computation.157.clone.1 | output fusion | flops 25166848 | bytes 34095104 | tf_op jit(solution)/shard_map/while/body/eval_jaxpr/sub | solution.py:71
  200.9 9.5 %fusion.125 = bf16[2,512,8,64]{1,3,2,0:T(8,128)(2,1)} fusion(bf16[2,512,8,64]{1,3,2,0:T(8,128)(2,1)} %get-tuple-element.203, s32[]{:T(128)} %get-tuple-element.202, bf16[1024,8,64]{0,2,1:T(8,128)(2,1)} %get-tuple-element.216, f32[8,512,1024]{2,1,0:T(8,128)} %get-tuple-element.191, f32[8,512]{1,0:T(8,128)S(1)} %get-tuple-element.192), kind=kOutput, calls=%fused_computation.13.clone.1 | convolution fusion | flops 545259520 | bytes 18891264 | tf_op jit(solution)/shard_map/while/body/eval_jaxpr/hqk,khd->qhd/dot_general | solution.py:72
  210.6 2.3 copy.53
  212.9 1.2 copy.54
  214.2 23.4 %fusion.25 = f32[1024,512]{1,0:T(8,128)} fusion(bf16[2048,512]{1,0:T(8,128)(2,1)S(1)} %copy-done, f32[2048]{0:T(1024)S(1)} %slice-done.1, bf16[512,2048]{1,0:T(8,128)(2,1)} %param.32, bf16[1024,512]{1,0:T(8,128)(2,1)} %reduce-scatter.2.cloned.1.call-done, f32[512]{0:T(512)S(1)} %bitcast.69, f32[512]{0:T(512)S(1)} %bitcast.70, f32[1024]{0:T(1024)S(1)} %copy-done.19, ...), kind=kOutput, calls=%fused_computation.41 | convolution fusion | flops 4436525056 | bytes 7360512 | tf_op jit(solution)/shard_map/dot_general | solution.py:87
  237.7 4.0 fusion.40
  242.3 38.8 %all-reduce.1 = (f32[]{:T(128)}, f32[4096]{0:T(1024)S(1)}) all-reduce(f32[]{:T(128)} %convert_reduce_fusion.1, f32[4096]{0:T(1024)S(1)} %copy-done.7), channel_id=1, replica_groups=mesh['rows'=8,'lat'=4] {'rows'}, use_global_device_ids=true, to_apply=%region_8.9 | all-reduce | flops 4097 | bytes 32776 | tf_op jit(solution)/shard_map/psum | solution.py:631
  283.7 1.9 broadcast_in_dim.49.mask_ref
  285.6 101.8 %forward.1 = (bf16[8,4096,512]{2,1,0:T(8,128)(2,1)}, f32[8,4096,512]{2,1,0:T(8,128)}, f32[8,4096]{1,0:T(8,128)}, bf16[4096,512]{1,0:T(8,128)(2,1)}, f32[16,512]{1,0:T(8,128)}) custom-call(bf16[4096,512]{1,0:T(8,128)(2,1)} %all-gather.4.cloned.1.call-done.inputs_ref, bf16[512,4096]{1,0:T(8,128)(2,1)} %all-gather.6.cloned.1.call-done.enc_ref, ...), custom_call_target="tpu_custom_call" | custom-call | tf_op jit(solution)/shard_map/forward/pallas_call | solution.py:315
  387.4 120.2 %backward.1 = (f32[64,4096]{1,0:T(8,128)}, f32[64,4096]{1,0:T(8,128)}, f32[8,4096]{1,0:T(8,128)}) custom-call(bf16[4096,512]{1,0:T(8,128)(2,1)} %all-gather.4.cloned.1.call-done.inputs_ref, bf16[4096,512]{1,0:T(8,128)(2,1)} %get-tuple-element.61.back_ref, bf16[512,4096]{1,0:T(8,128)(2,1)} %all-gather.8.cloned.1.call-done.dec_ref, f32[1,4096]{1,0:T(1,128)} %bitcast.67, ...), custom_call_target="tpu_custom_call" | custom-call | tf_op jit(solution)/shard_map/backward/pallas_call | solution.py:563
  507.7 0.9 reduce_sum.139
  508.8 34.6 %psum.44 = f32[2,4096]{1,0:T(2,128)S(1)} all-reduce(f32[2,4096]{1,0:T(2,128)S(1)} %pad_maximum_fusion.4), channel_id=1, replica_groups=mesh['rows'=8,'lat'=4] {'rows'}, use_global_device_ids=true, to_apply=%region_14.15 | all-reduce | flops 8192 | bytes 65536 | tf_op jit(solution)/shard_map/psum | solution.py:656
  545.9 2.1 multiply_reduce_fusion.1
  549.3 3.0 multiply_reduce_fusion
  553.6 36.9 %all-reduce = (f32[]{:T(128)}, f32[512]{0:T(512)S(1)}, f32[]{:T(128)}) all-reduce(f32[]{:T(128)S(6)} %add.221, f32[512]{0:T(512)S(1)} %get-tuple-element.90, f32[]{:T(128)S(6)} %add.243), channel_id=1, replica_groups=mesh['rows'=8,'lat'=4] {'rows','lat'}, use_global_device_ids=true, to_apply=%region_17.18 | all-reduce | flops 514 | bytes 4112 | tf_op jit(solution)/shard_map/psum | solution.py:665
  593.1 4.4 multiply_subtract_fusion.1
  598.2 4.0 multiply_subtract_fusion
  (91 shorter events, 9.2 us)
Async XLA Ops:
  8.0 206.1 %copy-start = (bf16[2048,512]{1,0:T(8,128)(2,1)S(1)}, bf16[2048,512]{1,0:T(8,128)(2,1)}, u32[]{:S(2)}) copy-start(bf16[2048,512]{1,0:T(8,128)(2,1)} %param.33) | copy-start | bytes 6291460
  8.0 79.1 %reduce-scatter.2.cloned.1.call-start = ((), (), s32[]{:S(2)}) async-start(), calls=%async_computation.1 | async-start | bytes 5242880 | tf_op jit(solution)/shard_map/reduce_scatter | solution.py:638
  33.5 6.3 %copy-start.1 = (f32[4096,64]{0,1:T(8,128)S(1)}, f32[4096,64]{0,1:T(8,128)}, u32[]{:S(2)}) copy-start(f32[4096,64]{0,1:T(8,128)} %param.37) | copy-start | bytes 3145732
  33.5 10.1 %copy-start.10 = (f32[4608]{0:T(1024)S(1)}, f32[4608]{0:T(1024)}, u32[]{:S(2)}) copy-start(f32[4608]{0:T(1024)} %param.29) | copy-start | bytes 55300
  33.5 10.7 %copy-start.16 = (f32[4,512]{1,0:T(4,128)S(1)}, f32[4,512]{1,0:T(4,128)}, u32[]{:S(2)}) copy-start(f32[4,512]{1,0:T(4,128)} %param.28) | copy-start | bytes 24580
  33.5 56.9 %slice-start = ((f32[4608]{0:T(1024)}), f32[1536]{0:T(1024)S(1)}, s32[]{:S(2)}) async-start(f32[4608]{0:T(1024)} %param.29), calls=%async_computation.5 | async-start | bytes 16384 | tf_op jit(solution)/shard_map/slice | solution.py:54
  39.7 243.4 %all-gather.8.cloned.1.call-start = ((), (), s32[]{:S(2)}) async-start(), calls=%async_computation.4 | async-start | bytes 4718592 | tf_op jit(solution)/shard_map/all_gather | solution.py:630
  41.3 241.8 %all-gather.6.cloned.1.call-start = ((), (), s32[]{:S(2)}) async-start(), calls=%async_computation.3 | async-start | bytes 4718592 | tf_op jit(solution)/shard_map/all_gather | solution.py:629
  43.5 239.7 %all-gather.4.cloned.1.call-start = ((), (), s32[]{:S(2)}) async-start(), calls=%async_computation.2 | async-start | bytes 5242880 | tf_op jit(solution)/shard_map/all_gather | solution.py:647
  88.6 5.4 copy-start.11
  90.3 3.7 copy-start.18
  94.0 2.7 copy-start.3
  120.5 93.6 %slice-start.1 = ((f32[4608]{0:T(1024)}), f32[2048]{0:T(1024)S(1)}, s32[]{:S(2)}) async-start(f32[4608]{0:T(1024)} %param.29), calls=%async_computation.6 | async-start | bytes 16384 | tf_op jit(solution)/shard_map/slice | solution.py:83
  120.5 93.6 %copy-start.12 = (f32[1024]{0:T(1024)S(1)}, f32[1024]{0:T(1024)}, u32[]{:S(2)}) copy-start(f32[1024]{0:T(1024)} %copy-done.11) | copy-start | bytes 12292
  120.5 93.6 %copy-start.19 = (f32[1024]{0:T(1024)S(1)}, f32[1024]{0:T(1024)}, u32[]{:S(2)}) copy-start(f32[1024]{0:T(1024)} %copy-done.18) | copy-start | bytes 12292
  120.5 93.6 %copy-start.24 = (f32[1,512]{1,0:T(1,128)S(1)}, f32[1,512]{1,0:T(1,128)}, u32[]{:S(2)}) copy-start(f32[1,512]{1,0:T(1,128)} %get-tuple-element.144) | copy-start | bytes 6148
  120.5 93.6 %copy-start.25 = (f32[1,512]{1,0:T(1,128)S(1)}, f32[1,512]{1,0:T(1,128)}, u32[]{:S(2)}) copy-start(f32[1,512]{1,0:T(1,128)} %get-tuple-element.145) | copy-start | bytes 6148
  214.2 23.5 %copy-start.4 = (bf16[1024,512]{1,0:T(8,128)(2,1)S(1)}, bf16[1024,512]{1,0:T(8,128)(2,1)}, u32[]{:S(2)}) copy-start(bf16[1024,512]{1,0:T(8,128)(2,1)} %reduce-scatter.2.cloned.1.call-done) | copy-start | bytes 3145732
  214.2 23.5 %copy-start.17 = (f32[1024]{0:T(1024)S(1)}, f32[1024]{0:T(1024)}, u32[]{:S(2)}) copy-start(f32[1024]{0:T(1024)} %multiply_add_fusion.2) | copy-start | bytes 12292
  214.2 23.5 %copy-start.20 = (f32[512]{0:T(512)S(1)}, f32[512]{0:T(512)}, u32[]{:S(2)}) copy-start(f32[512]{0:T(512)} %get-tuple-element.138) | copy-start | bytes 6148
  214.2 23.5 %copy-start.21 = (f32[512]{0:T(512)S(1)}, f32[512]{0:T(512)}, u32[]{:S(2)}) copy-start(f32[512]{0:T(512)} %get-tuple-element.139) | copy-start | bytes 6148
  214.2 27.5 %copy-start.8 = (s32[4096]{0:T(1024)S(1)}, s32[4096]{0:T(1024)}, u32[]{:S(2)}) copy-start(s32[4096]{0:T(1024)} %param.25) | copy-start | bytes 49156
  214.2 28.1 %copy-start.7 = (f32[4096]{0:T(1024)S(1)}, f32[4096]{0:T(1024)}, u32[]{:S(2)}) copy-start(f32[4096]{0:T(1024)} %get-tuple-element.130) | copy-start | bytes 49156
  387.4 121.3 %copy-start.5 = (f32[8,4096]{1,0:T(8,128)S(1)}, f32[8,4096]{1,0:T(8,128)}, u32[]{:S(2)}) copy-start(f32[8,4096]{1,0:T(8,128)} %get-tuple-element.67) | copy-start | bytes 393220
  387.4 157.9 %copy-start.9 = (f32[16,512]{1,0:T(8,128)S(1)}, f32[16,512]{1,0:T(8,128)}, u32[]{:S(2)}) copy-start(f32[16,512]{1,0:T(8,128)} %get-tuple-element.68) | copy-start | bytes 98308
  387.4 161.9 %copy-start.2 = (f32[4096,64]{0,1:T(8,128)S(1)}, f32[4096,64]{0,1:T(8,128)}, u32[]{:S(2)}) copy-start(f32[4096,64]{0,1:T(8,128)} %param.37) | copy-start | bytes 3145732
  387.4 205.1 %copy-start.15 = (f32[512]{0:T(512)S(1)}, f32[512]{0:T(512)}, u32[]{:S(2)}) copy-start(f32[512]{0:T(512)} %param.43) | copy-start | bytes 6148
  387.4 205.1 %copy-start.22 = (f32[512]{0:T(512)S(1)}, f32[512]{0:T(512)}, u32[]{:S(2)}) copy-start(f32[512]{0:T(512)} %param.44) | copy-start | bytes 6148
  387.4 205.1 %copy-start.23 = (f32[512]{0:T(512)S(1)}, f32[512]{0:T(512)}, u32[]{:S(2)}) copy-start(f32[512]{0:T(512)} %param.45) | copy-start | bytes 6148
  507.7 89.8 %copy-start.6 = (f32[4096]{0:T(1024)S(1)}, f32[4096]{0:T(1024)}, u32[]{:S(2)}) copy-start(f32[4096]{0:T(1024)} %param.40) | copy-start | bytes 49156
  507.7 89.8 %copy-start.13 = (f32[4096]{0:T(1024)S(1)}, f32[4096]{0:T(1024)}, u32[]{:S(2)}) copy-start(f32[4096]{0:T(1024)} %param.41) | copy-start | bytes 49156
  507.7 89.8 %copy-start.14 = (f32[4096]{0:T(1024)S(1)}, f32[4096]{0:T(1024)}, u32[]{:S(2)}) copy-start(f32[4096]{0:T(1024)} %param.42) | copy-start | bytes 49156
Sparse Core Ops, SparseCore 0:
  39.9 47.2 reduce-scatter.1
Sparse Core Ops, SparseCore 1:
  42.9 75.6 all-gather.7
  121.2 71.3 all-gather.5
  241.8 34.6 all-gather.3

commit v2 on v1

--- a/solution.py
+++ b/solution.py
@@ -27,69 +27,6 @@
 weight_decay = 0.01
 
 
-def layer_norm(values, gain, shift):
-    centred = values - jnp.mean(values, axis=-1, keepdims=True)
-    spread = jnp.mean(centred * centred, axis=-1, keepdims=True)
-    return centred * lax.rsqrt(spread + 1e-05) * gain + shift
-
-
-def rotary(values, rotated):
-    length = values.shape[0]
-    half = rotated // 2
-    freqs = 10000.0 ** (-2.0 * jnp.arange(half, dtype=jnp.float32) / rotated)
-    angles = jnp.arange(length, dtype=jnp.float32)[:, None] * freqs[None, :]
-    cosines = jnp.concatenate([jnp.cos(angles), jnp.cos(angles)], -1)[:, None, :]
-    sines = jnp.concatenate([jnp.sin(angles), jnp.sin(angles)], -1)[:, None, :]
-    head = values[..., :rotated]
-    turned = jnp.concatenate([-head[..., half:], head[..., :half]], -1)
-    return jnp.concatenate([head * cosines + turned * sines, values[..., rotated:]], -1)
-
-
-def frozen_layer(embedded, norm_params, frozen_bias, w_joined, w_attn_out, w_mlp_in, w_mlp_out):
-    length, width = embedded.shape
-    head_dim = width // HEADS
-    hidden_units = w_mlp_in.shape[1]
-    attn_in = layer_norm(embedded, norm_params[0], norm_params[1]).astype(jnp.bfloat16)
-    joined = (
-        jnp.dot(attn_in, w_joined, preferred_element_type=jnp.float32) + frozen_bias[: 3 * width]
-    )
-    queries = rotary(joined[:, :width].reshape(length, HEADS, head_dim), ROT).astype(jnp.bfloat16)
-    keys = rotary(joined[:, width : 2 * width].reshape(length, HEADS, head_dim), ROT).astype(
-        jnp.bfloat16
-    )
-    values = joined[:, 2 * width :].reshape(length, HEADS, head_dim).astype(jnp.bfloat16)
-    block_rows = min(512, length)
-    key_places = jnp.arange(length)
-
-    def attend(block_start):
-        block_queries = lax.dynamic_slice_in_dim(queries, block_start, block_rows, 0)
-        scores = jnp.einsum(
-            "qhd,khd->hqk", block_queries, keys, preferred_element_type=jnp.float32
-        ) * head_dim ** (-0.5)
-        query_places = block_start + jnp.arange(block_rows)
-        causal = query_places[None, :, None] >= key_places[None, None, :]
-        probs = jax.nn.softmax(jnp.where(causal, scores, -1e30), axis=-1).astype(jnp.bfloat16)
-        return jnp.einsum("hqk,khd->qhd", probs, values, preferred_element_type=jnp.float32)
-
-    starts = jnp.arange(0, length, block_rows)
-    context = lax.map(attend, starts).reshape(length, width).astype(jnp.bfloat16)
-    attended = (
-        jnp.dot(context, w_attn_out, preferred_element_type=jnp.float32)
-        + frozen_bias[3 * width : 4 * width]
-    )
-    mlp_in = layer_norm(embedded, norm_params[2], norm_params[3]).astype(jnp.bfloat16)
-    inner = (
-        jnp.dot(mlp_in, w_mlp_in, preferred_element_type=jnp.float32)
-        + frozen_bias[4 * width : 4 * width + hidden_units]
-    )
-    inner = jax.nn.gelu(inner, approximate=False).astype(jnp.bfloat16)
-    mlp_out = (
-        jnp.dot(inner, w_mlp_out, preferred_element_type=jnp.float32)
-        + frozen_bias[4 * width + hidden_units :]
-    )
-    return embedded + attended + mlp_out
-
-
 def adam_update(weight, moment, second, grad, decay):
     moment_new = beta_one * moment + (1.0 - beta_one) * grad
     second_new = beta_two * second + (1.0 - beta_two) * grad * grad
@@ -97,6 +34,342 @@
     scaled = jnp.sqrt(second_new / (1.0 - beta_two**STEP)) + adam_eps
     weight_new = weight - learn_rate * (corrected / scaled + decay * weight)
     return (weight_new, moment_new, second_new)
+
+
+ROWS = 512
+PIECE = 256
+HEAD = 64
+PAIR = 128
+
+
+def front_kernel(
+    rows_size, lat_size,
+    picked_ref, norm_ref, bias_ref, joined_ref, attn_ref, mlp_in_ref, mlp_out_ref,
+    turn_ref, level_ref, mask_ref, enc_ref, dec_ref,
+    inputs_out, enc_out, dec_out, norms_out, count_out,
+    from_core, from_y, base, queries, keys, values, context, facts, got_facts,
+    out_right, in_left, out_left, in_right, out_x, in_x, out_fact, in_fact,
+    out_core, in_core, out_y, in_y, out_own, in_own, out_near, in_near,
+):
+    tokens, depth = base.shape
+    shard = enc_ref.shape[0]
+    latents = enc_ref.shape[1]
+    hidden = mlp_in_ref.shape[1]
+    x_size = rows_size // Z_CHIPS
+    y_size = lat_size // CORES
+    pieces = tokens // PIECE
+    row = lax.axis_index("rows")
+    lat = lax.axis_index("lat")
+    my_z, my_x = row // x_size, lax.rem(row, x_size)
+    my_y, core = lat // CORES, lax.rem(lat, CORES)
+    other = 1 - core
+
+    def remote(src, dst, send, recv, to_row, to_lat):
+        return pltpu.make_async_remote_copy(
+            src_ref=src, dst_ref=dst, send_sem=send, recv_sem=recv,
+            device_id=(to_row, to_lat), device_id_type=MESH)
+
+    def peer_row(step):
+        return lax.rem(row + step, rows_size)
+
+    def x_row(step):
+        return my_z * x_size + lax.rem(my_x + step, x_size)
+
+    def y_peer(step):
+        return lax.rem(my_y + step, y_size)
+
+    barrier = pltpu.get_barrier_semaphore()
+    for step in range(1, rows_size):
+        pl.semaphore_signal(barrier, inc=1, device_id=(peer_row(step), lat), device_id_type=MESH)
+    for step in range(1, y_size):
+        pl.semaphore_signal(barrier, inc=1, device_id=(row, y_peer(step) * CORES + core), device_id_type=MESH)
+    pl.semaphore_signal(barrier, inc=1, device_id=(row, my_y * CORES + other), device_id_type=MESH)
+
+    mine = pl.ds(pl.multiple_of(row * shard, shard), shard)
+    enc_out[mine, :] = enc_ref[...].astype(bf16)
+    dec_out[mine, :] = dec_ref[...].astype(bf16)
+    square = jnp.sum(dec_ref[...] * dec_ref[...], axis=0, keepdims=True)
+    part = latents // 8
+    for at in range(8):
+        facts[pl.ds(at, 1), :] = square[:, at * part : (at + 1) * part]
+    facts[8:16, :] = jnp.broadcast_to(jnp.sum(mask_ref[...], keepdims=True), (8, part))
+    pl.semaphore_wait(barrier, rows_size + y_size - 1)
+
+    weights = (enc_out, dec_out)
+
+    def weight_rows(z):
+        return pl.ds(pl.multiple_of((z * x_size + my_x) * shard, shard), shard)
+
+    def right_copy(hop, which, received=False):
+        area = weights[which].at[weight_rows(jnp.maximum(my_z - hop - (1 if received else 0), 0))]
+        return remote(area, area, out_right.at[hop, which], in_left.at[hop, which],
+                      jnp.minimum(my_z + 1, Z_CHIPS - 1) * x_size + my_x, lat)
+
+    def left_copy(hop, which, received=False):
+        area = weights[which].at[weight_rows(jnp.minimum(my_z + hop + (1 if received else 0), Z_CHIPS - 1))]
+        return remote(area, area, out_left.at[hop, which], in_right.at[hop, which],
+                      jnp.maximum(my_z - 1, 0) * x_size + my_x, lat)
+
+    def x_copy(z, which, step):
+        area = weights[which].at[weight_rows(z)]
+        return remote(area, area, out_x.at[z, which, step - 1], in_x.at[z, which, step - 1], x_row(step), lat)
+
+    def pass_on(hop, which):
+        if hop == 0:
+            @pl.when(my_z < Z_CHIPS - 1)
+            def _():
+                right_copy(0, which).start()
+
+            @pl.when(my_z > 0)
+            def _():
+                left_copy(0, which).start()
+
+            for step in range(1, x_size):
+                x_copy(my_z, which, step).start()
+            return
+
+        @pl.when(my_z >= hop)
+        def _():
+            right_copy(hop - 1, which, True).wait_recv()
+            if hop < Z_CHIPS - 1:
+                @pl.when(my_z < Z_CHIPS - 1)
+                def _():
+                    right_copy(hop, which).start()
+            for step in range(1, x_size):
+                x_copy(my_z - hop, which, step).start()
+
+        @pl.when(my_z + hop <= Z_CHIPS - 1)
+        def _():
+            left_copy(hop - 1, which, True).wait_recv()
+            if hop < Z_CHIPS - 1:
+                @pl.when(my_z > 0)
+                def _():
+                    left_copy(hop, which).start()
+            for step in range(1, x_size):
+                x_copy(my_z + hop, which, step).start()
+
+    def fact_copy(step):
+        return remote(facts, got_facts.at[step - 1], out_fact.at[step - 1], in_fact.at[step - 1], peer_row(step), lat)
+
+    def block_rows(y, which_core, piece):
+        return pl.ds(pl.multiple_of((y * CORES + which_core) * tokens + piece * PIECE, PIECE), PIECE)
+
+    def core_copy(step, piece):
+        return remote(
+            picked_ref.at[block_rows(y_peer(step), other, piece)], from_core.at[step, pl.ds(piece * PIECE, PIECE)],
+            out_core.at[step, piece], in_core.at[step, piece], row, my_y * CORES + other)
+
+    def y_copy(step, piece):
+        here = pl.ds(piece * PIECE, PIECE)
+        return remote(
+            from_core.at[step, here], from_y.at[step - 1, here],
+            out_y.at[step - 1, piece], in_y.at[step - 1, piece], row, y_peer(step) * CORES + core)
+
+    for piece in range(pieces):
+        for step in list(range(1, y_size)) + [0]:
+            core_copy(step, piece).start()
+    for which in range(2):
+        pass_on(0, which)
+    for step in range(1, rows_size):
+        fact_copy(step).start()
+    for piece in range(pieces):
+        here = pl.ds(piece * PIECE, PIECE)
+        for step in list(range(1, y_size)) + [0]:
+            core_copy(step, piece).wait_recv()
+            total = picked_ref[block_rows(y_peer(step), core, piece), :].astype(f32) + from_core[step, here, :].astype(f32)
+            if step == 0:
+                base[here, :] = total
+            else:
+                from_core[step, here, :] = total.astype(bf16)
+                y_copy(step, piece).start()
+    pass_on(1, 0)
+
+    def normed(value, gain, shift):
+        centred = value - jnp.mean(value, axis=1, keepdims=True)
+        spread = jnp.mean(centred * centred, axis=1, keepdims=True)
+        return (centred * lax.rsqrt(spread + 1e-05) * gain + shift).astype(bf16)
+
+    def dot(left, right):
+        return jnp.dot(left, right, preferred_element_type=f32)
+
+    def rotated(value, rows):
+        cosine, low, high = turn_ref[0, rows, :], turn_ref[1, rows, :], turn_ref[2, rows, :]
+        parts = []
+        for at in range(depth // PAIR):
+            tile = value[:, at * PAIR : (at + 1) * PAIR]
+            parts.append(
+                tile * cosine + pltpu.roll(tile, PAIR - ROT // 2, 1) * low + pltpu.roll(tile, ROT // 2, 1) * high)
+        return jnp.concatenate(parts, axis=1)
+
+    for block in range(tokens // ROWS):
+        rows = pl.ds(block * ROWS, ROWS)
+        for piece in range(block * ROWS // PIECE, (block + 1) * ROWS // PIECE):
+            for step in range(1, y_size):
+                y_copy(step, piece).wait_recv()
+        embedded = base[rows, :]
+        for step in range(1, y_size):
+            embedded = embedded + from_y[step - 1, rows, :].astype(f32)
+        attn_in = normed(embedded, norm_ref[0:1, :], norm_ref[1:2, :])
+        joined = dot(attn_in, joined_ref[...]) + bias_ref[:, : 3 * depth]
+        queries[rows, :] = (rotated(joined[:, :depth], rows).astype(bf16) * HEAD**-0.5).astype(bf16)
+        keys[rows, :] = rotated(joined[:, depth : 2 * depth], rows).astype(bf16)
+        values[rows, :] = joined[:, 2 * depth :].astype(bf16)
+        mlp_in = normed(embedded, norm_ref[2:3, :], norm_ref[3:4, :])
+        inner = dot(mlp_in, mlp_in_ref[...]) + bias_ref[:, 4 * depth : 4 * depth + hidden]
+        inner = (0.5 * inner * (1.0 + lax.erf(inner * 0.5**0.5))).astype(bf16)
+        base[rows, :] = embedded + (dot(inner, mlp_out_ref[...]) + bias_ref[:, 4 * depth + hidden :])
+        if block == 0:
+            pass_on(1, 1)
+    pass_on(2, 0)
+
+    def own_rows(y, which_core, piece):
+        return pl.ds(pl.multiple_of((y * CORES + which_core) * tokens + piece * PIECE, PIECE), PIECE)
+
+    def own_copy(step, piece):
+        area = inputs_out.at[own_rows(my_y, core, piece)]
+        return remote(area, area, out_own.at[step - 1, piece], in_own.at[step - 1, piece], row, y_peer(step) * CORES + core)
+
+    def near_copy(step, piece):
+        area = inputs_out.at[own_rows(y_peer(step), core, piece)]
+        return remote(area, area, out_near.at[step, piece], in_near.at[step, piece], row, my_y * CORES + other)
+
+    lanes = lax.broadcasted_iota(jnp.int32, (PIECE, PAIR), 1)
+    for piece in range(pieces):
+        here = pl.ds(piece * PIECE, PIECE)
+        reach = (piece + 1) * PIECE
+        visible = (
+            lax.broadcasted_iota(jnp.int32, (PIECE, reach), 0) + piece * PIECE
+            >= lax.broadcasted_iota(jnp.int32, (PIECE, reach), 1)
+        )
+
+        def attend(pair, carry):
+            cols = pl.ds(pl.multiple_of(pair * PAIR, PAIR), PAIR)
+            both = queries[here, cols]
+            found = []
+            for first in (True, False):
+                chosen = jnp.where((lanes < HEAD) == first, both, jnp.zeros_like(both))
+                scores = lax.dot_general(
+                    chosen, keys[0:reach, cols], (((1,), (1,)), ((), ())), preferred_element_type=f32)
+                scores = jnp.where(visible, scores, -1e30)
+                powers = jnp.exp(scores - jnp.max(scores, axis=1, keepdims=True))
+                probs = (powers * (1.0 / jnp.sum(powers, axis=1, keepdims=True))).astype(bf16)
+                found.append(dot(probs, values[0:reach, cols]))
+            context[here, cols] = jnp.where(lanes < HEAD, found[0], found[1]).astype(bf16)
+            return carry
+
+        lax.fori_loop(0, depth // PAIR, attend, 0)
+        attended = dot(context[here, :], attn_ref[...]) + bias_ref[:, 3 * depth : 4 * depth]
+        level = jnp.concatenate([level_ref[here, :]] * (depth // 128), axis=1)
+        inputs_out[own_rows(my_y, core, piece), :] = ((base[here, :] + attended) * level).astype(bf16)
+        for step in range(1, y_size):
+            own_copy(step, piece).start()
+        near_copy(0, piece).start()
+        if piece == 1:
+            pass_on(2, 1)
+        if piece >= 2:
+            for step in range(1, y_size):
+                own_copy(step, piece - 2).wait_recv()
+                near_copy(step, piece - 2).start()
+
+    total = facts[...]
+    for step in range(1, rows_size):
+        fact_copy(step).wait_recv()
+        total = total + got_facts[step - 1]
+    count_out[...] = total[8:16, 0:128]
+    norms = jnp.sqrt(total[0:8, :])
+    for at in range(8):
+        norms_out[:, at * part : (at + 1) * part] = norms[at : at + 1, :]
+    pass_on(3, 0)
+    for piece in range(pieces - 2, pieces):
+        for step in range(1, y_size):
+            own_copy(step, piece).wait_recv()
+            near_copy(step, piece).start()
+    pass_on(3, 1)
+
+    for which in range(2):
+        for hop in range(Z_CHIPS - 1):
+            @pl.when((my_z < Z_CHIPS - 1) & (my_z >= hop))
+            def _():
+                right_copy(hop, which).wait_send()
+
+            @pl.when((my_z > 0) & (my_z + hop <= Z_CHIPS - 1))
+            def _():
+                left_copy(hop, which).wait_send()
+
+        for z in range(Z_CHIPS):
+            for step in range(1, x_size):
+                x_copy(z, which, step).wait_send()
+                x_copy(z, which, step).wait_recv()
+    for step in range(1, rows_size):
+        fact_copy(step).wait_send()
+    for piece in range(pieces):
+        for step in range(y_size):
+            core_copy(step, piece).wait_send()
+            near_copy(step, piece).wait_send()
+            near_copy(step, piece).wait_recv()
+        for step in range(1, y_size):
+            y_copy(step, piece).wait_send()
+            own_copy(step, piece).wait_send()
+
+
+def front(rows_size, lat_size, picked, norm_params, bias_row, w_joined, w_attn_out, w_mlp_in, w_mlp_out,
+          turns, level_lanes, mask_tiles, enc_shard, dec_shard):
+    group, depth = picked.shape
+    tokens = group // lat_size
+    shard, latents = enc_shard.shape
+    x_size = rows_size // Z_CHIPS
+    y_size = lat_size // CORES
+    pieces = tokens // PIECE
+    dma = pltpu.SemaphoreType.DMA
+    vmem = pl.BlockSpec(memory_space=pltpu.VMEM)
+    hops = Z_CHIPS - 1
+    return pl.pallas_call(
+        functools.partial(front_kernel, rows_size, lat_size),
+        out_shape=[
+            jax.ShapeDtypeStruct((group, depth), bf16),
+            jax.ShapeDtypeStruct((depth, latents), bf16),
+            jax.ShapeDtypeStruct((depth, latents), bf16),
+            jax.ShapeDtypeStruct((1, latents), f32),
+            jax.ShapeDtypeStruct((8, 128), f32),
+        ],
+        in_specs=[vmem] * 12,
+        out_specs=[vmem] * 5,
+        scratch_shapes=[
+            pltpu.VMEM((y_size, tokens, depth), bf16),
+            pltpu.VMEM((y_size - 1, tokens, depth), bf16),
+            pltpu.VMEM((tokens, depth), f32),
+            pltpu.VMEM((tokens, depth), bf16),
+            pltpu.VMEM((tokens, depth), bf16),
+            pltpu.VMEM((tokens, depth), bf16),
+            pltpu.VMEM((tokens, depth), bf16),
+            pltpu.VMEM((16, latents // 8), f32),
+            pltpu.VMEM((rows_size - 1, 16, latents // 8), f32),
+            dma((hops, 2)), dma((hops, 2)), dma((hops, 2)), dma((hops, 2)),
+            dma((Z_CHIPS, 2, x_size - 1)), dma((Z_CHIPS, 2, x_size - 1)),
+            dma((rows_size - 1,)), dma((rows_size - 1,)),
+            dma((y_size, pieces)), dma((y_size, pieces)),
+            dma((y_size - 1, pieces)), dma((y_size - 1, pieces)),
+            dma((y_size - 1, pieces)), dma((y_size - 1, pieces)),
+            dma((y_size, pieces)), dma((y_size, pieces)),
+        ],
+        compiler_params=pltpu.CompilerParams(
+            collective_id=3, has_side_effects=True, vmem_limit_bytes=60 * 2**20),
+        name="front",
+    )(picked, norm_params, bias_row, w_joined, w_attn_out, w_mlp_in, w_mlp_out,
+      turns, level_lanes, mask_tiles, enc_shard, dec_shard)
+
+
+def turn_tables(length):
+    half = ROT // 2
+    freqs = 10000.0 ** (-2.0 * jnp.arange(half, dtype=f32) / ROT)
+    angles = jnp.arange(length, dtype=f32)[:, None] * jnp.tile(freqs, PAIR // half)[None, :]
+    place = jnp.arange(PAIR) % HEAD
+    cosines, sines = jnp.cos(angles), jnp.sin(angles)
+    return jnp.stack([
+        jnp.where(place < ROT, cosines, 1.0),
+        jnp.where(place < half, -sines, 0.0),
+        jnp.where((place >= half) & (place < ROT), sines, 0.0),
+    ])
 
 
 def softplus_parts(value):
@@ -626,32 +899,28 @@
     depth = enc_weight.shape[0] * rows_size
     mask_float = token_mask.astype(f32)
     dec_master = dec_weight.T
-    enc_low = lax.all_gather(enc_weight.astype(bf16), "rows", axis=0, tiled=True)
-    dec_cols = lax.all_gather(dec_master.astype(bf16), "rows", axis=0, tiled=True)
-    count = lax.psum(jnp.sum(mask_float), "rows")
-    norms = jnp.sqrt(lax.psum(jnp.sum(dec_master * dec_master, axis=0), "rows"))
+    bias_row = frozen_bias[None, :]
     vocab_local = embed.shape[0]
     vocab_first = lat_index * vocab_local
     local_ids = token_ids - vocab_first
     inside = ((local_ids >= 0) & (local_ids < vocab_local)).astype(f32)
     picked = jnp.take(embed, jnp.clip(local_ids, 0, vocab_local - 1), axis=0).astype(f32)
-    embedded = lax.psum_scatter(
-        (picked * inside[:, None]).astype(bf16), "lat", scatter_dimension=0, tiled=True
-    ).astype(f32)
+    picked = (picked * inside[:, None]).astype(bf16)
     own_first = lat_index * tok_local
-    residual = frozen_layer(
-        embedded, norm_params, frozen_bias, w_joined, w_attn_out, w_mlp_in, w_mlp_out
-    )
     scales = 0.5 + 0.25 * lax.dynamic_slice_in_dim(scale_index, own_first, tok_local).astype(f32)
-    own_inputs = (residual * scales[:, None]).astype(bf16)
-    all_inputs = lax.all_gather(own_inputs, "lat", axis=0, tiled=True)
+    level_lanes = jnp.broadcast_to(scales[:, None], (tok_local, 128))
+    all_inputs, enc_low, dec_cols, norms_row, counts = front(
+        rows_size, lat_size, picked, norm_params, bias_row, w_joined, w_attn_out, w_mlp_in, w_mlp_out,
+        turn_tables(tok_local), level_lanes, mask_float.reshape(-1, 128), enc_weight, dec_master)
+    count = counts[0, 0]
+    norms = norms_row[0]
     mask_lanes = jnp.broadcast_to(mask_float[:, None], (group_tokens, 128))
     scale_row = jnp.full((1, depth), 2.0 / count, f32)
     lasso_scale = lasso_coef / count
     active, slope, mass_rows, recon_grad, stats = forward(
         lat_size, all_inputs, enc_low, dec_cols, enc_bias[None, :], mask_lanes, dec_bias[None, :], scale_row)
     grad_enc, grad_dec, bias_rows = backward(
-        rows_size, all_inputs, recon_grad, dec_cols, (lasso_scale * norms)[None, :], active, slope)
+        rows_size, all_inputs, recon_grad, dec_cols, lasso_scale * norms_row, active, slope)
     bias_mass = jnp.stack([bias_rows.sum(0), mass_rows.sum(0)])
     grad_enc_bias, active_mass = lax.psum(bias_mass, "rows")
     leader = (lax.axis_index("rows") == 0).astype(f32)

time: 618 us -> 471 us (0.76)
  Pallas kernels: 222 us -> 332 us
  matrix products: 68.8 us -> 0 us
  other arithmetic: 89.7 us -> 25.7 us
  waiting for transfers between devices: 41 us -> 0 us
  blocking collectives: 110 us -> 74.1 us
  local copies, waits for them, and re-layouts: 51.6 us -> 29.3 us
  between operations: 23.5 us -> 8.06 us
    pallas_call x0 -> x1, Pallas kernels: none -> 110 us  [front(): pl.pallas_call(functools.partial(front_kernel, rows_size, lat_size), out_...]
    dot_general x7 -> x0, matrix products: 68.8 us -> none  [the longest x1 23.4 us: frozen_layer(): jnp.dot(inner, w_mlp_out, preferred_element_type=jnp.float32)]
    sub x2 -> x0, other arithmetic: 43.4 us -> none  [attend(): jax.nn.softmax(jnp.where(causal, scores, -1e+30), axis=-1)]
    reduce_scatter x1 -> x0, waiting for transfers between devices: 40.9 us -> none  [body(): lax.psum_scatter((picked * inside[:, None]).astype(bf16), 'lat', scatter_...]
    psum x1 -> x0, blocking collectives: 38.8 us -> none  [body(): count = lax.psum(jnp.sum(mask_float), 'rows')]
    slice x13 -> x1, local copies, waits for them, and re-layouts: 17.8 us -> 1.19 us  [body(): count = counts[0, 0]]
  transfers between devices with their start and end apart: 4 -> 0, of which waited for: 1 -> 0; matrix products, arithmetic and copies ran while one was open for 25% -> 0% of each run, Pallas kernels for 0% -> 0%
where the time goes in v2:
time: 471 us; the launch traced here: 469 us
  Pallas kernels  332 us (70%)
  blocking collectives  74.1 us (16%)
  local copies, waits for them, and re-layouts  29.3 us (6%)
  other arithmetic  25.7 us (5%)
  between operations  8.06 us (2%)
    pallas_call x1, Pallas kernels, backward(): pl.pallas_call(functools.partial(backward_kernel, rows_size), out_shape=[...  120 us
    pallas_call x1, Pallas kernels, front(): pl.pallas_call(functools.partial(front_kernel, rows_size, lat_size), out_...  110 us
    pallas_call x1, Pallas kernels, forward(): pl.pallas_call(functools.partial(forward_kernel, lat_size), out_shape=[ja...  102 us
    psum x1, blocking collectives, body(): grad_enc_bias, active_mass = lax.psum(bias_mass, 'rows')  37.2 us
    psum x1, blocking collectives, body(): lax.psum(local_squares, ('rows', 'lat'))  36.9 us
    gather x1, local copies, waits for them, and re-layouts, body(): jnp.take(embed, jnp.clip(local_ids, 0, vocab_local - 1), axis=0).astype(f32)  23.9 us

profile of v2, /device:TPU:0, one launch (start us, length us, event | category | flops | bytes accessed | tf_op | source)
XLA Modules:
  0.0 469.5 jit_solution(7203916504999486602)
XLA Ops:
  0.6 0.0 copy-start.7
  0.7 0.1 mul.305
  0.8 2.0 cosine_select_fusion
  2.8 1.3 pad_maximum_fusion.turn_ref
  4.1 0.7 multiply_add_fusion.3
  4.8 1.0 broadcast_in_dim.66.level_ref
  5.8 0.0 copy-done.7
  5.8 23.9 %gather_fusion = bf16[4096,512]{1,0:T(8,128)(2,1)} fusion(bf16[12576,512]{1,0:T(8,128)(2,1)} %param.25, s32[4096]{0:T(1024)S(1)} %fusion.6), kind=kCustom, calls=%fused_computation | custom fusion | bytes 8404992 | tf_op jit(solution)/shard_map/jit(_take)/gather | solution.py:907
  29.7 6.1 %multiply_convert_fusion.picked_ref = bf16[4096,512]{1,0:T(8,128)(2,1)} fusion(f32[4096]{0:T(1024)S(1)} %get-tuple-element.66, bf16[4096,512]{1,0:T(8,128)(2,1)} %gather_fusion, pred[4096]{0:T(1024)(128)(4,1)S(1)} %get-tuple-element.65), kind=kLoop, calls=%fused_computation.1 | loop fusion | flops 8388608 | bytes 8409088 | tf_op jit(solution)/shard_map/convert_element_type | solution.py:908
  35.8 0.0 copy-done.11
  35.8 0.6 fusion.13
  36.5 0.0 copy-done.10
  36.5 0.6 broadcast_in_dim.60.bias_ref
  37.1 110.4 %front.1 = (bf16[4096,512]{1,0:T(8,128)(2,1)}, bf16[512,4096]{1,0:T(8,128)(2,1)}, bf16[512,4096]{1,0:T(8,128)(2,1)}, f32[1,4096]{1,0:T(1,128)}, f32[8,128]{1,0:T(8,128)}) custom-call(bf16[4096,512]{1,0:T(8,128)(2,1)} %multiply_convert_fusion.picked_ref, f32[4,512]{1,0:T(4,128)} %norm_ref.1, f32[1,4608]{1,0:T(1,128)} %broadcast_in_dim.60.bias_ref, ...), custom_call_target="tpu_custom_call" | custom-call | tf_op jit(solution)/shard_map/front/pallas_call | solution.py:326
  147.5 1.2 slice.9
  149.4 0.6 broadcast_in_dim.70.scale_ref
  150.0 1.9 broadcast_in_dim.68.mask_ref
  151.9 102.2 %forward.1 = (bf16[8,4096,512]{2,1,0:T(8,128)(2,1)}, f32[8,4096,512]{2,1,0:T(8,128)}, f32[8,4096]{1,0:T(8,128)}, bf16[4096,512]{1,0:T(8,128)(2,1)}, f32[16,512]{1,0:T(8,128)}) custom-call(bf16[4096,512]{1,0:T(8,128)(2,1)} %get-tuple-element.28.inputs_ref, bf16[512,4096]{1,0:T(8,128)(2,1)} %get-tuple-element.29.enc_ref, ...), custom_call_target="tpu_custom_call" | custom-call | tf_op jit(solution)/shard_map/forward/pallas_call | solution.py:588
  254.8 0.0 copy-done.8
  254.8 0.6 broadcast_multiply_fusion.lasso_ref
  255.4 119.7 %backward.1 = (f32[64,4096]{1,0:T(8,128)}, f32[64,4096]{1,0:T(8,128)}, f32[8,4096]{1,0:T(8,128)}) custom-call(bf16[4096,512]{1,0:T(8,128)(2,1)} %get-tuple-element.28.inputs_ref, bf16[4096,512]{1,0:T(8,128)(2,1)} %get-tuple-element.32.back_ref, bf16[512,4096]{1,0:T(8,128)(2,1)} %get-tuple-element.30.dec_ref, f32[1,4096]{1,0:T(1,128)} %broadcast_multiply_fusion.lasso_ref, ...), custom_call_target="tpu_custom_call" | custom-call | tf_op jit(solution)/shard_map/backward/pallas_call | solution.py:836
  375.1 0.0 copy-start.2
  375.1 0.0 copy-start.14
  375.1 0.0 copy-start.15
  375.1 0.0 copy-start.16
  375.1 0.0 copy-start.6
  375.1 0.0 copy-start.12
  375.1 0.0 copy-start.13
  375.1 1.0 reduce_sum.82
  376.2 0.0 copy-done.5
  376.2 37.2 %psum.28 = f32[2,4096]{1,0:T(2,128)S(1)} all-reduce(f32[2,4096]{1,0:T(2,128)S(1)} %pad_maximum_fusion.1), channel_id=1, replica_groups=mesh['rows'=8,'lat'=4] {'rows'}, use_global_device_ids=true, to_apply=%region_3.4 | all-reduce | flops 8192 | bytes 65536 | tf_op jit(solution)/shard_map/psum | solution.py:925
  413.4 0.7 multiply_reduce_fusion.2
  414.7 0.0 copy-done.9
  414.7 0.6 slice_reduce_fusion
  416.0 0.0 copy-done
  416.0 3.0 multiply_reduce_fusion
  419.0 0.9 multiply_reduce_fusion.1
  421.8 36.9 %all-reduce = (f32[]{:T(128)}, f32[512]{0:T(512)S(1)}, f32[]{:T(128)}) all-reduce(f32[]{:T(128)S(6)} %add.118, f32[512]{0:T(512)S(1)} %get-tuple-element.44, f32[]{:T(128)S(6)} %add.140), channel_id=1, replica_groups=mesh['rows'=8,'lat'=4] {'rows','lat'}, use_global_device_ids=true, to_apply=%region_6.7 | all-reduce | flops 514 | bytes 4112 | tf_op jit(solution)/shard_map/psum | solution.py:934
  458.7 0.6 multiply_reduce_fusion.4
  460.8 0.0 copy-start.3
  460.8 0.0 copy-start.4
  460.8 0.6 multiply_subtract_fusion.3
  461.4 0.0 copy-done.6
  461.4 0.0 copy-done.12
  461.4 0.0 copy-done.13
  461.4 0.6 multiply_subtract_fusion.2
  462.1 4.0 multiply_subtract_fusion
  466.1 2.2 multiply_subtract_fusion.1
  (23 shorter events, 0.2 us)
Async XLA Ops:
  0.6 5.1 %copy-start.7 = (s32[4096]{0:T(1024)S(1)}, s32[4096]{0:T(1024)}, u32[]{:S(2)}) copy-start(s32[4096]{0:T(1024)} %param.22) | copy-start | bytes 49156
  29.7 6.1 %copy-start.11 = (s32[4096]{0:T(1024)S(1)}, s32[4096]{0:T(1024)}, u32[]{:S(2)}) copy-start(s32[4096]{0:T(1024)} %param.23) | copy-start | bytes 49156
  29.7 6.8 %copy-start.10 = (f32[4608]{0:T(1024)S(1)}, f32[4608]{0:T(1024)}, u32[]{:S(2)}) copy-start(f32[4608]{0:T(1024)} %param.27) | copy-start | bytes 55300
  151.9 102.9 %copy-start.8 = (f32[1,4096]{1,0:T(1,128)S(1)}, f32[1,4096]{1,0:T(1,128)}, u32[]{:S(2)}) copy-start(f32[1,4096]{1,0:T(1,128)} %get-tuple-element.33) | copy-start | bytes 49156
  255.4 120.8 %copy-start.5 = (f32[8,4096]{1,0:T(8,128)S(1)}, f32[8,4096]{1,0:T(8,128)}, u32[]{:S(2)}) copy-start(f32[8,4096]{1,0:T(8,128)} %get-tuple-element.39) | copy-start | bytes 393220
  255.4 159.3 %copy-start.9 = (f32[16,512]{1,0:T(8,128)S(1)}, f32[16,512]{1,0:T(8,128)}, u32[]{:S(2)}) copy-start(f32[16,512]{1,0:T(8,128)} %get-tuple-element.40) | copy-start | bytes 98308
  255.4 160.6 %copy-start = (f32[4096,64]{0,1:T(8,128)S(1)}, f32[4096,64]{0,1:T(8,128)}, u32[]{:S(2)}) copy-start(f32[4096,64]{0,1:T(8,128)} %param.35) | copy-start | bytes 3145732
  375.1 44.0 %copy-start.2 = (f32[64,4096]{1,0:T(8,128)S(1)}, f32[64,4096]{1,0:T(8,128)}, u32[]{:S(2)}) copy-start(f32[64,4096]{1,0:T(8,128)} %get-tuple-element.36) | copy-start | bytes 3145732
  375.1 85.7 %copy-start.14 = (f32[512]{0:T(512)S(1)}, f32[512]{0:T(512)}, u32[]{:S(2)}) copy-start(f32[512]{0:T(512)} %param.41) | copy-start | bytes 6148
  375.1 85.7 %copy-start.15 = (f32[512]{0:T(512)S(1)}, f32[512]{0:T(512)}, u32[]{:S(2)}) copy-start(f32[512]{0:T(512)} %param.42) | copy-start | bytes 6148
  375.1 85.7 %copy-start.16 = (f32[512]{0:T(512)S(1)}, f32[512]{0:T(512)}, u32[]{:S(2)}) copy-start(f32[512]{0:T(512)} %param.43) | copy-start | bytes 6148
  375.1 86.3 %copy-start.6 = (f32[4096]{0:T(1024)S(1)}, f32[4096]{0:T(1024)}, u32[]{:S(2)}) copy-start(f32[4096]{0:T(1024)} %param.38) | copy-start | bytes 49156
  375.1 86.3 %copy-start.12 = (f32[4096]{0:T(1024)S(1)}, f32[4096]{0:T(1024)}, u32[]{:S(2)}) copy-start(f32[4096]{0:T(1024)} %param.39) | copy-start | bytes 49156
  375.1 86.3 %copy-start.13 = (f32[4096]{0:T(1024)S(1)}, f32[4096]{0:T(1024)}, u32[]{:S(2)}) copy-start(f32[4096]{0:T(1024)} %param.40) | copy-start | bytes 49156
  419.0 47.1 %copy-start.1 = (f32[64,4096]{1,0:T(8,128)S(1)}, f32[64,4096]{1,0:T(8,128)}, u32[]{:S(2)}) copy-start(f32[64,4096]{1,0:T(8,128)} %enc_ref.1) | copy-start | bytes 3145732
  460.8 5.4 %copy-start.3 = (f32[64,4096]{1,0:T(8,128)S(1)}, f32[64,4096]{1,0:T(8,128)}, u32[]{:S(2)}) copy-start(f32[64,4096]{1,0:T(8,128)} %param.33) | copy-start | bytes 3145732
  460.8 5.4 %copy-start.4 = (f32[64,4096]{1,0:T(8,128)S(1)}, f32[64,4096]{1,0:T(8,128)}, u32[]{:S(2)}) copy-start(f32[64,4096]{1,0:T(8,128)} %param.34) | copy-start | bytes 3145732

commit v3 on v2

--- a/solution.py
+++ b/solution.py
@@ -639,14 +639,16 @@
 
 
 def backward_kernel(
-    rows_size,
-    inputs_ref, back_ref, dec_ref, lasso_ref, active_hbm, slope_hbm,
-    enc_out, dec_out, bias_out,
+    rows_size, lat_size,
+    inputs_ref, back_ref, dec_ref, lasso_ref, norms_ref, pull_ref, mass_ref, stats_ref, master_ref,
+    active_hbm, slope_hbm,
+    enc_out, dec_out, bias_out, center_out, totals_out,
     grad_low, active_buf, slope_buf, sums,
     send_one, units_one, recv_one, got_one,
     send_two, units_two, recv_two, got_two,
+    bias_rows, pull_cols, facts, tiles,
     active_sem, slope_sem,
-    out_one, in_one, outu_one, inu_one, out_two, in_two, outu_two, inu_two,
+    out_one, in_one, outu_one, inu_one, out_two, in_two, outu_two, inu_two, out_facts, in_facts, out_tiles, in_tiles,
 ):
     blocks, tokens, width = active_hbm.shape
     chunk = slope_buf.shape[1]
@@ -691,16 +693,95 @@
             for at in (0, 4)
         ]
 
+    devices = rows_size * lat_size
+    me = row * lat_size + lat
+    latents = dec_ref.shape[1]
+    depth = inputs_ref.shape[1]
+    part = latents // 8
+
+    def fact_copy(kind, step):
+        area = facts.at[kind, row]
+        return pltpu.make_async_remote_copy(
+            src_ref=area, dst_ref=area, send_sem=out_facts.at[kind, step], recv_sem=in_facts.at[kind, row],
+            device_id=(lax.rem(row + step, rows_size), lat), device_id_type=MESH)
+
+    def fact_arrival(kind, step):
+        source = lax.rem(row + step, rows_size)
+        area = facts.at[kind, source]
+        return pltpu.make_async_remote_copy(
+            src_ref=area, dst_ref=area, send_sem=out_facts.at[kind, step], recv_sem=in_facts.at[kind, source],
+            device_id=(source, lat), device_id_type=MESH)
+
+    def tile_copy(kind, step):
+        area = tiles.at[kind, me]
+        target = lax.rem(me + step, devices)
+        return pltpu.make_async_remote_copy(
+            src_ref=area, dst_ref=area, send_sem=out_tiles.at[kind, step], recv_sem=in_tiles.at[kind, me],
+            device_id=(target // lat_size, lax.rem(target, lat_size)), device_id_type=MESH)
+
+    def tile_arrival(kind, step):
+        source = lax.rem(me + step, devices)
+        area = tiles.at[kind, source]
+        return pltpu.make_async_remote_copy(
+            src_ref=area, dst_ref=area, send_sem=out_tiles.at[kind, step], recv_sem=in_tiles.at[kind, source],
+            device_id=(source // lat_size, lax.rem(source, lat_size)), device_id_type=MESH)
+
+    def over_devices(action):
+        def turn(step, carry):
+            action(step)
+            return carry
+
+        lax.fori_loop(1, devices, turn, 0)
+
+    def share_row(kind, value):
+        for at in range(8):
+            facts[kind, row, pl.ds(at, 1), :] = value[:, at * part : (at + 1) * part]
+        for step in range(1, rows_size):
+            fact_copy(kind, step).start()
+
+    def shared_row(kind):
+        for step in range(1, rows_size):
+            fact_arrival(kind, step).wait_recv()
+        total = facts[kind, 0]
+        for source in range(1, rows_size):
+            total = total + facts[kind, source]
+        return jnp.concatenate([total[at : at + 1, :] for at in range(8)], axis=1)
+
+    def share_tile(kind, value):
+        tiles[kind, me] = value
+
+        def start(step):
+            tile_copy(kind, step).start()
+
+        over_devices(start)
+
+    def shared_tile(kind):
+        def wait(step):
+            tile_arrival(kind, step).wait_recv()
+
+        over_devices(wait)
+        return lax.fori_loop(1, devices, lambda source, total: total + tiles[kind, source], tiles[kind, 0])
+
     barrier = pltpu.get_barrier_semaphore()
-    for step in range(1, x_size):
-        pl.semaphore_signal(barrier, inc=1, device_id=(my_z * x_size + x_peer(step), lat), device_id_type=MESH)
-    for step in range(1, Z_CHIPS):
-        pl.semaphore_signal(barrier, inc=1, device_id=(z_peer(step) * x_size + my_x, lat), device_id_type=MESH)
+
+    def greet(step):
+        target = lax.rem(me + step, devices)
+        pl.semaphore_signal(
+            barrier, inc=1, device_id=(target // lat_size, lax.rem(target, lat_size)), device_id_type=MESH)
+
+    over_devices(greet)
     active_copy(0).start()
     ahead = slope_buf.shape[0] - 1
     for index in range(ahead):
         slope_copy(index).start()
-    pl.semaphore_wait(barrier, x_size + Z_CHIPS - 2)
+    pl.semaphore_wait(barrier, devices - 1)
+    share_row(0, jnp.sum(mass_ref[...], axis=0, keepdims=True))
+    center = jnp.sum(stats_ref[8:16, :], axis=0, keepdims=True)
+    square = jnp.sum(stats_ref[0:8, :], keepdims=True)
+    quarter = depth // 4
+    share_tile(0, jnp.concatenate(
+        [center[:, at * quarter : (at + 1) * quarter] for at in range(4)]
+        + [jnp.broadcast_to(square, (4, quarter))], axis=0))
 
     def columns(block):
         return pl.ds(pl.multiple_of(block * width, width), width)
@@ -735,7 +816,7 @@
             grad_low[rows, :] = low
             return total + low.astype(f32).reshape(chunk // 8, 8, width).sum(0)
 
-        bias_out[:, cols] = lax.fori_loop(0, chunks, piece, jnp.zeros((8, width), f32))
+        bias_rows[:, cols] = lax.fori_loop(0, chunks, piece, jnp.zeros((8, width), f32))
         sums[slot, 0] = lax.dot_general(inputs_ref[...], grad_low[...], over_tokens, preferred_element_type=f32)
 
     def send_x(block, which):
@@ -813,7 +894,43 @@
 
         return carry
 
-    lax.fori_loop(0, blocks + 2, turn, 0)
+    lax.fori_loop(0, blocks, turn, 0)
+    share_row(1, jnp.sum(bias_rows[...], axis=0, keepdims=True))
+    lax.fori_loop(blocks, blocks + 2, turn, 0)
+
+    mass = shared_row(0)
+    bias = shared_row(1)
+    bias_out[...] = bias
+    pull = mass * pull_ref[...]
+
+    def squares(block, total):
+        cols = columns(block)
+        gain = dec_out[:, cols] + pull_cols[:, cols] * master_ref[:, cols]
+        dec_out[:, cols] = gain
+        other = enc_out[:, cols]
+        return total + gain * gain + other * other
+
+    pull_cols[...] = pull
+    total = jnp.sum(lax.fori_loop(0, blocks, squares, jnp.zeros((shard, width), f32)), keepdims=True)
+    leads = jnp.where(row == 0, 1.0, 0.0)
+    total = total + leads * jnp.sum(bias * bias, keepdims=True)
+    lasso = leads * lasso_coef * jnp.sum(mass * norms_ref[...], keepdims=True)
+    share_tile(1, jnp.concatenate(
+        [jnp.broadcast_to(total, (4, quarter)), jnp.broadcast_to(lasso, (4, quarter))], axis=0))
+    first = shared_tile(0)
+    center = jnp.concatenate([first[at : at + 1, :] for at in range(4)], axis=1)
+    center_out[...] = center
+    second = shared_tile(1)
+    squared = second[0:4, :] + jnp.sum(center * center, keepdims=True)
+    totals_out[...] = jnp.concatenate([squared, first[4:8, :] + second[4:8, :]], axis=0)
+    for kind in range(2):
+        for step in range(1, rows_size):
+            fact_copy(kind, step).wait_send()
+
+        def sent(step, kind=kind):
+            tile_copy(kind, step).wait_send()
+
+        over_devices(sent)
     for block in range(max(blocks - 2, 0), blocks):
         for which in range(2):
             for stage, size in ((0, x_size), (1, Z_CHIPS)):
@@ -822,26 +939,30 @@
                         copy.wait_send()
 
 
-def backward(rows_size, inputs, back, dec_cols, lasso_row, active, slope):
+def backward(rows_size, lat_size, inputs, back, dec_cols, lasso_row, norms_row, pull_row, mass_rows, stats, master,
+             active, slope):
     blocks, tokens, width = active.shape
     depth = inputs.shape[1]
     shard = depth // rows_size
     latents = dec_cols.shape[1]
     x_size = rows_size // Z_CHIPS
+    devices = rows_size * lat_size
     chunk = min(CHUNK, tokens)
     i16 = jnp.int16
     dma = pltpu.SemaphoreType.DMA
     vmem = pl.BlockSpec(memory_space=pltpu.VMEM)
     hbm = pl.BlockSpec(memory_space=pl.ANY)
     return pl.pallas_call(
-        functools.partial(backward_kernel, rows_size),
+        functools.partial(backward_kernel, rows_size, lat_size),
         out_shape=[
             jax.ShapeDtypeStruct((shard, latents), f32),
             jax.ShapeDtypeStruct((shard, latents), f32),
-            jax.ShapeDtypeStruct((8, latents), f32),
+            jax.ShapeDtypeStruct((1, latents), f32),
+            jax.ShapeDtypeStruct((1, depth), f32),
+            jax.ShapeDtypeStruct((8, 128), f32),
         ],
-        in_specs=[vmem] * 4 + [hbm] * 2,
-        out_specs=[vmem] * 3,
+        in_specs=[vmem] * 9 + [hbm] * 2,
+        out_specs=[vmem] * 5,
         scratch_shapes=[
             pltpu.VMEM((tokens, width), bf16),
             pltpu.VMEM((2, tokens, width), bf16),
@@ -855,16 +976,21 @@
             pltpu.VMEM((2, 2, Z_CHIPS - 1, 8, 128), f32),
             pltpu.VMEM((blocks, 2, Z_CHIPS - 1, shard, width), i16),
             pltpu.VMEM((blocks, 2, Z_CHIPS - 1, 8, 128), f32),
+            pltpu.VMEM((8, latents), f32),
+            pltpu.VMEM((1, latents), f32),
+            pltpu.VMEM((2, rows_size, 8, latents // 8), f32),
+            pltpu.VMEM((2, devices, 8, 128), f32),
             dma((2,)), dma((SLOTS,)),
             dma((2, 2, x_size - 1)), dma((blocks, 2, x_size - 1)),
             dma((2, 2, x_size - 1)), dma((blocks, 2, x_size - 1)),
             dma((2, 2, Z_CHIPS - 1)), dma((blocks, 2, Z_CHIPS - 1)),
             dma((2, 2, Z_CHIPS - 1)), dma((blocks, 2, Z_CHIPS - 1)),
+            dma((2, rows_size)), dma((2, rows_size)), dma((2, devices)), dma((2, devices)),
         ],
         compiler_params=pltpu.CompilerParams(
-            collective_id=2, has_side_effects=True, vmem_limit_bytes=60 * 2**20),
+            collective_id=2, has_side_effects=True, vmem_limit_bytes=61 * 2**20),
         name="backward",
-    )(inputs, back, dec_cols, lasso_row, active, slope)
+    )(inputs, back, dec_cols, lasso_row, norms_row, pull_row, mass_rows, stats, master, active, slope)
 
 
 def body(
@@ -913,26 +1039,17 @@
         rows_size, lat_size, picked, norm_params, bias_row, w_joined, w_attn_out, w_mlp_in, w_mlp_out,
         turn_tables(tok_local), level_lanes, mask_float.reshape(-1, 128), enc_weight, dec_master)
     count = counts[0, 0]
-    norms = norms_row[0]
     mask_lanes = jnp.broadcast_to(mask_float[:, None], (group_tokens, 128))
     scale_row = jnp.full((1, depth), 2.0 / count, f32)
     lasso_scale = lasso_coef / count
     active, slope, mass_rows, recon_grad, stats = forward(
         lat_size, all_inputs, enc_low, dec_cols, enc_bias[None, :], mask_lanes, dec_bias[None, :], scale_row)
-    grad_enc, grad_dec, bias_rows = backward(
-        rows_size, all_inputs, recon_grad, dec_cols, lasso_scale * norms_row, active, slope)
-    bias_mass = jnp.stack([bias_rows.sum(0), mass_rows.sum(0)])
-    grad_enc_bias, active_mass = lax.psum(bias_mass, "rows")
-    leader = (lax.axis_index("rows") == 0).astype(f32)
-    lasso_part = lasso_coef * jnp.sum(active_mass * norms) * leader
-    loss_sum, grad_dec_bias = lax.psum((jnp.sum(stats[:8]) + lasso_part, stats[8:].sum(0)), ("rows", "lat"))
-    grad_dec = grad_dec + (lasso_scale * active_mass / norms)[None, :] * dec_master
-    local_squares = (
-        jnp.sum(grad_enc * grad_enc) + jnp.sum(grad_dec * grad_dec)
-        + jnp.sum(grad_enc_bias * grad_enc_bias) * leader
-    )
-    squares = lax.psum(local_squares, ("rows", "lat")) + jnp.sum(grad_dec_bias * grad_dec_bias)
-    grad_norm = jnp.sqrt(squares)
+    grad_enc, grad_dec, bias_total, center, totals = backward(
+        rows_size, lat_size, all_inputs, recon_grad, dec_cols, lasso_scale * norms_row, norms_row,
+        lasso_scale / norms_row, mass_rows, stats, dec_master, active, slope)
+    grad_enc_bias, grad_dec_bias = bias_total[0], center[0]
+    grad_norm = jnp.sqrt(totals[0, 0])
+    loss_sum = totals[4, 0]
     factor = clip_bound / jnp.maximum(grad_norm, clip_bound)
     enc_new = adam_update(enc_weight, enc_moment, enc_second, grad_enc * factor, weight_decay)
     dec_new = adam_update(dec_weight, dec_moment, dec_second, grad_dec.T * factor, weight_decay)

time: 471 us -> 405 us (0.86)
  blocking collectives: 74.1 us -> 0 us
  Pallas kernels: 332 us -> 345 us
  other arithmetic: 25.7 us -> 20.2 us
    psum x2 -> x0, blocking collectives: 74.1 us -> none  [the longest x1 37.2 us: body(): grad_enc_bias, active_mass = lax.psum(bias_mass, 'rows')]
    pallas_call x1, Pallas kernels: 120 us -> 133 us  [backward(): pl.pallas_call(functools.partial(backward_kernel, rows_size, lat_size), o...]
    reduce_sum x7 -> x0, other arithmetic: 6.77 us -> none  [the longest x1 3 us: body(): jnp.sum(grad_dec * grad_dec)]
where the time goes in v3:
time: 405 us; the launch traced here: 401 us
  Pallas kernels  345 us (85%)
  local copies, waits for them, and re-layouts  31.1 us (8%)
  other arithmetic  20.2 us (5%)
  between operations  4.36 us (1%)
    pallas_call x1, Pallas kernels, backward(): pl.pallas_call(functools.partial(backward_kernel, rows_size, lat_size), o...  133 us
    pallas_call x1, Pallas kernels, front(): pl.pallas_call(functools.partial(front_kernel, rows_size, lat_size), out_...  110 us
    pallas_call x1, Pallas kernels, forward(): pl.pallas_call(functools.partial(forward_kernel, lat_size), out_shape=[ja...  102 us
    gather x1, local copies, waits for them, and re-layouts, body(): jnp.take(embed, jnp.clip(local_ids, 0, vocab_local - 1), axis=0).astype(f32)  24.3 us

profile of v3, /device:TPU:0, one launch (start us, length us, event | category | flops | bytes accessed | tf_op | source)
XLA Modules:
  0.0 400.8 jit_solution(11512190026165485848)
XLA Ops:
  0.6 0.0 copy-start.8
  0.7 0.1 mul.267
  0.8 2.0 cosine_select_fusion
  2.8 1.3 pad_maximum_fusion.turn_ref
  4.1 0.7 multiply_add_fusion.2
  4.8 1.0 broadcast_in_dim.65.level_ref
  5.8 0.0 copy-done.8
  5.8 24.3 %gather_fusion = bf16[4096,512]{1,0:T(8,128)(2,1)} fusion(bf16[12576,512]{1,0:T(8,128)(2,1)} %param.25, s32[4096]{0:T(1024)S(1)} %fusion.6), kind=kCustom, calls=%fused_computation | custom fusion | bytes 8404992 | tf_op jit(solution)/shard_map/jit(_take)/gather | solution.py:1033
  30.2 6.2 %multiply_convert_fusion.picked_ref = bf16[4096,512]{1,0:T(8,128)(2,1)} fusion(f32[4096]{0:T(1024)S(1)} %get-tuple-element.62, bf16[4096,512]{1,0:T(8,128)(2,1)} %gather_fusion, pred[4096]{0:T(1024)(128)(4,1)S(1)} %get-tuple-element.61), kind=kLoop, calls=%fused_computation.1 | loop fusion | flops 8388608 | bytes 8409088 | tf_op jit(solution)/shard_map/convert_element_type | solution.py:1034
  36.3 0.0 copy-done.10
  36.3 0.6 fusion.13
  36.9 0.0 copy-done.9
  36.9 0.6 broadcast_in_dim.59.bias_ref
  37.6 110.4 %front.1 = (bf16[4096,512]{1,0:T(8,128)(2,1)}, bf16[512,4096]{1,0:T(8,128)(2,1)}, bf16[512,4096]{1,0:T(8,128)(2,1)}, f32[1,4096]{1,0:T(1,128)}, f32[8,128]{1,0:T(8,128)}) custom-call(bf16[4096,512]{1,0:T(8,128)(2,1)} %multiply_convert_fusion.picked_ref, f32[4,512]{1,0:T(4,128)} %norm_ref.1, f32[1,4608]{1,0:T(1,128)} %broadcast_in_dim.59.bias_ref, ...), custom_call_target="tpu_custom_call" | custom-call | tf_op jit(solution)/shard_map/front/pallas_call | solution.py:326
  148.0 1.2 slice.9
  149.9 0.6 broadcast_in_dim.69.scale_ref
  150.5 1.9 broadcast_in_dim.67.mask_ref
  152.4 102.2 %forward.1 = (bf16[8,4096,512]{2,1,0:T(8,128)(2,1)}, f32[8,4096,512]{2,1,0:T(8,128)}, f32[8,4096]{1,0:T(8,128)}, bf16[4096,512]{1,0:T(8,128)(2,1)}, f32[16,512]{1,0:T(8,128)}) custom-call(bf16[4096,512]{1,0:T(8,128)(2,1)} %get-tuple-element.30.inputs_ref, bf16[512,4096]{1,0:T(8,128)(2,1)} %get-tuple-element.31.enc_ref, ...), custom_call_target="tpu_custom_call" | custom-call | tf_op jit(solution)/shard_map/forward/pallas_call | solution.py:588
  255.3 0.0 copy-done.7
  255.3 0.6 broadcast_divide_fusion
  255.9 0.0 copy-start.11
  256.0 0.0 copy-start.12
  256.0 0.0 copy-start
  256.0 0.0 copy-start.2
  256.0 132.5 %backward.1 = (f32[64,4096]{1,0:T(8,128)}, f32[64,4096]{1,0:T(8,128)}, f32[1,4096]{1,0:T(1,128)}, f32[1,512]{1,0:T(1,128)}, f32[8,128]{1,0:T(8,128)}) custom-call(bf16[4096,512]{1,0:T(8,128)(2,1)} %get-tuple-element.30.inputs_ref, bf16[4096,512]{1,0:T(8,128)(2,1)} %get-tuple-element.34.back_ref, bf16[512,4096]{1,0:T(8,128)(2,1)} %get-tuple-element.32.dec_ref, ...), custom_call_target="tpu_custom_call" | custom-call | tf_op jit(solution)/shard_map/backward/pallas_call | solution.py:955
  388.5 0.0 copy-start.1
  388.5 1.3 fusion.14
  390.6 0.0 copy-start.3
  390.6 0.0 copy-start.4
  390.6 0.0 copy-start.5
  390.6 0.8 broadcast_multiply_fusion.2
  391.4 0.0 copy-done.13
  391.4 0.0 copy-done.14
  391.4 0.0 copy-done.15
  391.4 0.6 multiply_subtract_fusion.3
  392.0 0.7 broadcast_multiply_fusion
  392.8 0.0 copy-done.6
  392.8 0.0 copy-done.11
  392.8 0.0 copy-done.12
  392.8 0.6 multiply_subtract_fusion.2
  393.4 0.0 copy-done
  393.4 0.0 copy-done.2
  393.4 3.7 multiply_subtract_fusion
  397.2 0.0 copy-done.1
  397.2 0.0 copy-done.3
  397.2 0.0 copy-done.4
  397.2 0.0 copy-done.5
  397.2 2.2 multiply_subtract_fusion.1
  (13 shorter events, 0.1 us)
Async XLA Ops:
  0.6 5.1 %copy-start.8 = (s32[4096]{0:T(1024)S(1)}, s32[4096]{0:T(1024)}, u32[]{:S(2)}) copy-start(s32[4096]{0:T(1024)} %param.22) | copy-start | bytes 49156
  30.2 6.2 %copy-start.10 = (s32[4096]{0:T(1024)S(1)}, s32[4096]{0:T(1024)}, u32[]{:S(2)}) copy-start(s32[4096]{0:T(1024)} %param.23) | copy-start | bytes 49156
  30.2 6.8 %copy-start.9 = (f32[4608]{0:T(1024)S(1)}, f32[4608]{0:T(1024)}, u32[]{:S(2)}) copy-start(f32[4608]{0:T(1024)} %param.27) | copy-start | bytes 55300
  152.4 102.9 %copy-start.7 = (f32[1,4096]{1,0:T(1,128)S(1)}, f32[1,4096]{1,0:T(1,128)}, u32[]{:S(2)}) copy-start(f32[1,4096]{1,0:T(1,128)} %get-tuple-element.35.norms_ref) | copy-start | bytes 49156
  255.9 135.5 %copy-start.13 = (f32[512]{0:T(512)S(1)}, f32[512]{0:T(512)}, u32[]{:S(2)}) copy-start(f32[512]{0:T(512)} %param.41) | copy-start | bytes 6148
  255.9 135.5 %copy-start.14 = (f32[512]{0:T(512)S(1)}, f32[512]{0:T(512)}, u32[]{:S(2)}) copy-start(f32[512]{0:T(512)} %param.42) | copy-start | bytes 6148
  255.9 135.5 %copy-start.15 = (f32[512]{0:T(512)S(1)}, f32[512]{0:T(512)}, u32[]{:S(2)}) copy-start(f32[512]{0:T(512)} %param.43) | copy-start | bytes 6148
  255.9 136.8 %copy-start.6 = (f32[4096]{0:T(1024)S(1)}, f32[4096]{0:T(1024)}, u32[]{:S(2)}) copy-start(f32[4096]{0:T(1024)} %param.38) | copy-start | bytes 49156
  255.9 136.8 %copy-start.11 = (f32[4096]{0:T(1024)S(1)}, f32[4096]{0:T(1024)}, u32[]{:S(2)}) copy-start(f32[4096]{0:T(1024)} %param.39) | copy-start | bytes 49156
  256.0 136.8 %copy-start.12 = (f32[4096]{0:T(1024)S(1)}, f32[4096]{0:T(1024)}, u32[]{:S(2)}) copy-start(f32[4096]{0:T(1024)} %param.40) | copy-start | bytes 49156
  256.0 137.5 %copy-start = (f32[4096,64]{0,1:T(8,128)S(1)}, f32[4096,64]{0,1:T(8,128)}, u32[]{:S(2)}) copy-start(f32[4096,64]{0,1:T(8,128)} %param.35) | copy-start | bytes 3145732
  256.0 137.4 %copy-start.2 = (f32[4096,64]{0,1:T(8,128)S(1)}, f32[4096,64]{0,1:T(8,128)}, u32[]{:S(2)}) copy-start(f32[4096,64]{0,1:T(8,128)} %param.36) | copy-start | bytes 3145732
  388.5 8.6 %copy-start.1 = (f32[64,4096]{1,0:T(8,128)S(1)}, f32[64,4096]{1,0:T(8,128)}, u32[]{:S(2)}) copy-start(f32[64,4096]{1,0:T(8,128)} %enc_ref.1) | copy-start | bytes 3145732
  390.6 6.6 %copy-start.3 = (f32[64,4096]{1,0:T(8,128)S(1)}, f32[64,4096]{1,0:T(8,128)}, u32[]{:S(2)}) copy-start(f32[64,4096]{1,0:T(8,128)} %param.33) | copy-start | bytes 3145732
  390.6 6.6 %copy-start.4 = (f32[64,4096]{1,0:T(8,128)S(1)}, f32[64,4096]{1,0:T(8,128)}, u32[]{:S(2)}) copy-start(f32[64,4096]{1,0:T(8,128)} %param.34) | copy-start | bytes 3145732
  390.6 6.6 %copy-start.5 = (f32[64,4096]{1,0:T(8,128)S(1)}, f32[64,4096]{1,0:T(8,128)}, u32[]{:S(2)}) copy-start(f32[64,4096]{1,0:T(8,128)} %get-tuple-element.40) | copy-start | bytes 3145732

commit v4 on v3

--- a/solution.py
+++ b/solution.py
@@ -45,15 +45,15 @@
 def front_kernel(
     rows_size, lat_size,
     picked_ref, norm_ref, bias_ref, joined_ref, attn_ref, mlp_in_ref, mlp_out_ref,
-    turn_ref, level_ref, mask_ref, enc_ref, dec_ref,
-    inputs_out, enc_out, dec_out, norms_out, count_out,
-    from_core, from_y, base, queries, keys, values, context, facts, got_facts,
+    turn_ref, level_ref, mask_ref, dec_ref, own_ref, left_ref, right_ref, across_ref,
+    inputs_out, enc_out, dec_out, norms_out, lasso_out, pull_out, scale_out,
+    from_core, from_y, base, queries, keys, values, context, ready, facts, got_facts,
+    place_sem,
     out_right, in_left, out_left, in_right, out_x, in_x, out_fact, in_fact,
     out_core, in_core, out_y, in_y, out_own, in_own, out_near, in_near,
 ):
     tokens, depth = base.shape
-    shard = enc_ref.shape[0]
-    latents = enc_ref.shape[1]
+    shard, latents = dec_ref.shape
     hidden = mlp_in_ref.shape[1]
     x_size = rows_size // Z_CHIPS
     y_size = lat_size // CORES
@@ -85,9 +85,6 @@
         pl.semaphore_signal(barrier, inc=1, device_id=(row, y_peer(step) * CORES + core), device_id_type=MESH)
     pl.semaphore_signal(barrier, inc=1, device_id=(row, my_y * CORES + other), device_id_type=MESH)
 
-    mine = pl.ds(pl.multiple_of(row * shard, shard), shard)
-    enc_out[mine, :] = enc_ref[...].astype(bf16)
-    dec_out[mine, :] = dec_ref[...].astype(bf16)
     square = jnp.sum(dec_ref[...] * dec_ref[...], axis=0, keepdims=True)
     part = latents // 8
     for at in range(8):
@@ -102,51 +99,66 @@
 
     def right_copy(hop, which, received=False):
         area = weights[which].at[weight_rows(jnp.maximum(my_z - hop - (1 if received else 0), 0))]
-        return remote(area, area, out_right.at[hop, which], in_left.at[hop, which],
+        source = left_ref.at[which] if hop == 1 and not received else area
+        return remote(source, area, out_right.at[hop, which], in_left.at[hop, which],
                       jnp.minimum(my_z + 1, Z_CHIPS - 1) * x_size + my_x, lat)
 
     def left_copy(hop, which, received=False):
         area = weights[which].at[weight_rows(jnp.minimum(my_z + hop + (1 if received else 0), Z_CHIPS - 1))]
-        return remote(area, area, out_left.at[hop, which], in_right.at[hop, which],
+        source = right_ref.at[which] if hop == 1 and not received else area
+        return remote(source, area, out_left.at[hop, which], in_right.at[hop, which],
                       jnp.maximum(my_z - 1, 0) * x_size + my_x, lat)
 
-    def x_copy(z, which, step):
+    def x_copy(z, which, step, source=None):
         area = weights[which].at[weight_rows(z)]
-        return remote(area, area, out_x.at[z, which, step - 1], in_x.at[z, which, step - 1], x_row(step), lat)
+        return remote(area if source is None else source.at[which], area,
+                      out_x.at[z, which, step - 1], in_x.at[z, which, step - 1], x_row(step), lat)
+
+    def place(index, which):
+        sources = [(own_ref, row), (left_ref, row - x_size), (right_ref, row + x_size)]
+        sources += [(across_ref.at[step - 1], x_row(step)) for step in range(1, x_size)]
+        source, owner = sources[index]
+        owner = jnp.clip(owner, 0, rows_size - 1)
+        return pltpu.make_async_copy(
+            source.at[which], weights[which].at[pl.ds(pl.multiple_of(owner * shard, shard), shard)],
+            place_sem.at[index, which])
+
+    def place_all(action):
+        for which in range(2):
+            for index in range(x_size + 2):
+                if index == 1:
+                    @pl.when(my_z > 0)
+                    def _():
+                        action(place(1, which))
+                elif index == 2:
+                    @pl.when(my_z < Z_CHIPS - 1)
+                    def _():
+                        action(place(2, which))
+                else:
+                    action(place(index, which))
 
     def pass_on(hop, which):
-        if hop == 0:
-            @pl.when(my_z < Z_CHIPS - 1)
-            def _():
-                right_copy(0, which).start()
-
-            @pl.when(my_z > 0)
-            def _():
-                left_copy(0, which).start()
-
-            for step in range(1, x_size):
-                x_copy(my_z, which, step).start()
-            return
-
         @pl.when(my_z >= hop)
         def _():
-            right_copy(hop - 1, which, True).wait_recv()
+            if hop > 1:
+                right_copy(hop - 1, which, True).wait_recv()
             if hop < Z_CHIPS - 1:
                 @pl.when(my_z < Z_CHIPS - 1)
                 def _():
                     right_copy(hop, which).start()
             for step in range(1, x_size):
-                x_copy(my_z - hop, which, step).start()
+                x_copy(my_z - hop, which, step, left_ref if hop == 1 else None).start()
 
         @pl.when(my_z + hop <= Z_CHIPS - 1)
         def _():
-            left_copy(hop - 1, which, True).wait_recv()
+            if hop > 1:
+                left_copy(hop - 1, which, True).wait_recv()
             if hop < Z_CHIPS - 1:
                 @pl.when(my_z > 0)
                 def _():
                     left_copy(hop, which).start()
             for step in range(1, x_size):
-                x_copy(my_z + hop, which, step).start()
+                x_copy(my_z + hop, which, step, right_ref if hop == 1 else None).start()
 
     def fact_copy(step):
         return remote(facts, got_facts.at[step - 1], out_fact.at[step - 1], in_fact.at[step - 1], peer_row(step), lat)
@@ -168,10 +180,6 @@
     for piece in range(pieces):
         for step in list(range(1, y_size)) + [0]:
             core_copy(step, piece).start()
-    for which in range(2):
-        pass_on(0, which)
-    for step in range(1, rows_size):
-        fact_copy(step).start()
     for piece in range(pieces):
         here = pl.ds(piece * PIECE, PIECE)
         for step in list(range(1, y_size)) + [0]:
@@ -182,7 +190,13 @@
             else:
                 from_core[step, here, :] = total.astype(bf16)
                 y_copy(step, piece).start()
+
     pass_on(1, 0)
+    for step in range(1, rows_size):
+        fact_copy(step).start()
+    place_all(lambda copy: copy.start())
+    pass_on(1, 1)
+    pass_on(2, 0)
 
     def normed(value, gain, shift):
         centred = value - jnp.mean(value, axis=1, keepdims=True)
@@ -219,19 +233,24 @@
         inner = (0.5 * inner * (1.0 + lax.erf(inner * 0.5**0.5))).astype(bf16)
         base[rows, :] = embedded + (dot(inner, mlp_out_ref[...]) + bias_ref[:, 4 * depth + hidden :])
         if block == 0:
-            pass_on(1, 1)
-    pass_on(2, 0)
+            pass_on(2, 1)
+    pass_on(3, 0)
 
     def own_rows(y, which_core, piece):
         return pl.ds(pl.multiple_of((y * CORES + which_core) * tokens + piece * PIECE, PIECE), PIECE)
 
     def own_copy(step, piece):
         area = inputs_out.at[own_rows(my_y, core, piece)]
-        return remote(area, area, out_own.at[step - 1, piece], in_own.at[step - 1, piece], row, y_peer(step) * CORES + core)
+        return remote(ready.at[pl.ds(piece * PIECE, PIECE)], area, out_own.at[step - 1, piece], in_own.at[step - 1, piece], row, y_peer(step) * CORES + core)
 
     def near_copy(step, piece):
         area = inputs_out.at[own_rows(y_peer(step), core, piece)]
-        return remote(area, area, out_near.at[step, piece], in_near.at[step, piece], row, my_y * CORES + other)
+        source = area if step else ready.at[pl.ds(piece * PIECE, PIECE)]
+        return remote(source, area, out_near.at[step, piece], in_near.at[step, piece], row, my_y * CORES + other)
+
+    def keep_copy(piece):
+        return pltpu.make_async_copy(
+            ready.at[pl.ds(piece * PIECE, PIECE)], inputs_out.at[own_rows(my_y, core, piece)], place_sem.at[x_size + 2, piece])
 
     lanes = lax.broadcasted_iota(jnp.int32, (PIECE, PAIR), 1)
     for piece in range(pieces):
@@ -260,12 +279,13 @@
         lax.fori_loop(0, depth // PAIR, attend, 0)
         attended = dot(context[here, :], attn_ref[...]) + bias_ref[:, 3 * depth : 4 * depth]
         level = jnp.concatenate([level_ref[here, :]] * (depth // 128), axis=1)
-        inputs_out[own_rows(my_y, core, piece), :] = ((base[here, :] + attended) * level).astype(bf16)
+        ready[here, :] = ((base[here, :] + attended) * level).astype(bf16)
+        keep_copy(piece).start()
         for step in range(1, y_size):
             own_copy(step, piece).start()
         near_copy(0, piece).start()
         if piece == 1:
-            pass_on(2, 1)
+            pass_on(3, 1)
         if piece >= 2:
             for step in range(1, y_size):
                 own_copy(step, piece - 2).wait_recv()
@@ -275,19 +295,23 @@
     for step in range(1, rows_size):
         fact_copy(step).wait_recv()
         total = total + got_facts[step - 1]
-    count_out[...] = total[8:16, 0:128]
+    count = total[8:9, 0:1]
     norms = jnp.sqrt(total[0:8, :])
-    for at in range(8):
-        norms_out[:, at * part : (at + 1) * part] = norms[at : at + 1, :]
-    pass_on(3, 0)
+    norms = jnp.concatenate([norms[at : at + 1, :] for at in range(8)], axis=1)
+    lasso_scale = lasso_coef / count
+    norms_out[...] = norms
+    lasso_out[...] = lasso_scale * norms
+    pull_out[...] = lasso_scale / norms
+    scale_out[0:1, :] = jnp.broadcast_to(2.0 / count, (1, depth))
+    scale_out[1:8, :] = jnp.broadcast_to(count, (7, depth))
     for piece in range(pieces - 2, pieces):
         for step in range(1, y_size):
             own_copy(step, piece).wait_recv()
             near_copy(step, piece).start()
-    pass_on(3, 1)
+    place_all(lambda copy: copy.wait())
 
     for which in range(2):
-        for hop in range(Z_CHIPS - 1):
+        for hop in range(1, Z_CHIPS - 1):
             @pl.when((my_z < Z_CHIPS - 1) & (my_z >= hop))
             def _():
                 right_copy(hop, which).wait_send()
@@ -297,12 +321,15 @@
                 left_copy(hop, which).wait_send()
 
         for z in range(Z_CHIPS):
-            for step in range(1, x_size):
-                x_copy(z, which, step).wait_send()
-                x_copy(z, which, step).wait_recv()
+            @pl.when(z != my_z)
+            def _():
+                for step in range(1, x_size):
+                    x_copy(z, which, step).wait_send()
+                    x_copy(z, which, step).wait_recv()
     for step in range(1, rows_size):
         fact_copy(step).wait_send()
     for piece in range(pieces):
+        keep_copy(piece).wait()
         for step in range(y_size):
             core_copy(step, piece).wait_send()
             near_copy(step, piece).wait_send()
@@ -313,15 +340,16 @@
 
 
 def front(rows_size, lat_size, picked, norm_params, bias_row, w_joined, w_attn_out, w_mlp_in, w_mlp_out,
-          turns, level_lanes, mask_tiles, enc_shard, dec_shard):
+          turns, level_lanes, mask_tiles, dec_shard, own, left, right, across):
     group, depth = picked.shape
     tokens = group // lat_size
-    shard, latents = enc_shard.shape
+    shard, latents = dec_shard.shape
     x_size = rows_size // Z_CHIPS
     y_size = lat_size // CORES
     pieces = tokens // PIECE
     dma = pltpu.SemaphoreType.DMA
     vmem = pl.BlockSpec(memory_space=pltpu.VMEM)
+    hbm = pl.BlockSpec(memory_space=pl.ANY)
     hops = Z_CHIPS - 1
     return pl.pallas_call(
         functools.partial(front_kernel, rows_size, lat_size),
@@ -330,10 +358,12 @@
             jax.ShapeDtypeStruct((depth, latents), bf16),
             jax.ShapeDtypeStruct((depth, latents), bf16),
             jax.ShapeDtypeStruct((1, latents), f32),
-            jax.ShapeDtypeStruct((8, 128), f32),
+            jax.ShapeDtypeStruct((1, latents), f32),
+            jax.ShapeDtypeStruct((1, latents), f32),
+            jax.ShapeDtypeStruct((8, depth), f32),
         ],
-        in_specs=[vmem] * 12,
-        out_specs=[vmem] * 5,
+        in_specs=[vmem] * 15,
+        out_specs=[hbm] * 3 + [vmem] * 4,
         scratch_shapes=[
             pltpu.VMEM((y_size, tokens, depth), bf16),
             pltpu.VMEM((y_size - 1, tokens, depth), bf16),
@@ -342,8 +372,10 @@
             pltpu.VMEM((tokens, depth), bf16),
             pltpu.VMEM((tokens, depth), bf16),
             pltpu.VMEM((tokens, depth), bf16),
+            pltpu.VMEM((tokens, depth), bf16),
             pltpu.VMEM((16, latents // 8), f32),
             pltpu.VMEM((rows_size - 1, 16, latents // 8), f32),
+            dma((x_size + 3, max(pieces, 2))),
             dma((hops, 2)), dma((hops, 2)), dma((hops, 2)), dma((hops, 2)),
             dma((Z_CHIPS, 2, x_size - 1)), dma((Z_CHIPS, 2, x_size - 1)),
             dma((rows_size - 1,)), dma((rows_size - 1,)),
@@ -356,7 +388,7 @@
             collective_id=3, has_side_effects=True, vmem_limit_bytes=60 * 2**20),
         name="front",
     )(picked, norm_params, bias_row, w_joined, w_attn_out, w_mlp_in, w_mlp_out,
-      turns, level_lanes, mask_tiles, enc_shard, dec_shard)
+      turns, level_lanes, mask_tiles, dec_shard, own, left, right, across)
 
 
 def turn_tables(length):
@@ -525,7 +557,7 @@
             total = total + recv_two[block, step - 1]
         error = total + dec_bias_ref[...] - inputs_ref[rows, :].astype(f32)
         mask = jnp.concatenate([mask_ref[rows, :]] * (depth // 128), axis=1)
-        low = (scale_ref[...] * mask * error).astype(bf16)
+        low = (scale_ref[0:1, :] * mask * error).astype(bf16)
         back_out[rows, :] = low
         stats_out[0:8, :] += (mask * error * error).reshape(share // 8, 8, depth).sum(0)
         stats_out[8:16, :] += low.astype(f32).reshape(share // 8, 8, depth).sum(0)
@@ -575,7 +607,7 @@
     lax.fori_loop(0, chunks, drain, 0)
 
 
-def forward(lat_size, inputs, enc_low, dec_cols, enc_bias_row, mask_lanes, dec_bias_row, scale_row):
+def forward(lat_size, inputs, enc_low, dec_cols, enc_bias_row, mask_lanes, dec_bias_row, scale_rows):
     tokens, depth = inputs.shape
     latents = enc_low.shape[1]
     chunk, span, width = 512, 1024, (512 if tokens <= 4096 else 256)
@@ -614,7 +646,7 @@
         compiler_params=pltpu.CompilerParams(
             collective_id=1, has_side_effects=True, vmem_limit_bytes=60 * 2**20),
         name="forward",
-    )(inputs, enc_low, dec_cols, enc_bias_row, mask_lanes, dec_bias_row, scale_row)
+    )(inputs, enc_low, dec_cols, enc_bias_row, mask_lanes, dec_bias_row, scale_rows)
 
 
 def encode(value):
@@ -640,7 +672,7 @@
 
 def backward_kernel(
     rows_size, lat_size,
-    inputs_ref, back_ref, dec_ref, lasso_ref, norms_ref, pull_ref, mass_ref, stats_ref, master_ref,
+    inputs_ref, back_ref, dec_ref, norms_ref, lasso_ref, pull_ref, mass_ref, stats_ref, master_ref,
     active_hbm, slope_hbm,
     enc_out, dec_out, bias_out, center_out, totals_out,
     grad_low, active_buf, slope_buf, sums,
@@ -939,7 +971,7 @@
                         copy.wait_send()
 
 
-def backward(rows_size, lat_size, inputs, back, dec_cols, lasso_row, norms_row, pull_row, mass_rows, stats, master,
+def backward(rows_size, lat_size, inputs, back, dec_cols, norms_row, lasso_row, pull_row, mass_rows, stats, master,
              active, slope):
     blocks, tokens, width = active.shape
     depth = inputs.shape[1]
@@ -990,7 +1022,7 @@
         compiler_params=pltpu.CompilerParams(
             collective_id=2, has_side_effects=True, vmem_limit_bytes=61 * 2**20),
         name="backward",
-    )(inputs, back, dec_cols, lasso_row, norms_row, pull_row, mass_rows, stats, master, active, slope)
+    )(inputs, back, dec_cols, norms_row, lasso_row, pull_row, mass_rows, stats, master, active, slope)
 
 
 def body(
@@ -1029,27 +1061,35 @@
     vocab_local = embed.shape[0]
     vocab_first = lat_index * vocab_local
     local_ids = token_ids - vocab_first
-    inside = ((local_ids >= 0) & (local_ids < vocab_local)).astype(f32)
-    picked = jnp.take(embed, jnp.clip(local_ids, 0, vocab_local - 1), axis=0).astype(f32)
-    picked = (picked * inside[:, None]).astype(bf16)
+    inside = (local_ids >= 0) & (local_ids < vocab_local)
+    picked = jnp.take(embed, jnp.clip(local_ids, 0, vocab_local - 1), axis=0)
+    picked = jnp.where(inside[:, None], picked, jnp.zeros((), bf16))
+    own = jnp.stack([enc_weight.astype(bf16), dec_master.astype(bf16)])
+    x_size = rows_size // Z_CHIPS
+    right_pairs = [(i, i + x_size) for i in range(rows_size - x_size)]
+    left_pairs = [(i + x_size, i) for i in range(rows_size - x_size)]
+    from_left = lax.ppermute(own, "rows", right_pairs)
+    from_right = lax.ppermute(own, "rows", left_pairs)
+    across = []
+    for step in range(1, x_size):
+        pairs = [(i // x_size * x_size + (i + step) % x_size, i) for i in range(rows_size)]
+        across.append(lax.ppermute(own, "rows", pairs))
     own_first = lat_index * tok_local
     scales = 0.5 + 0.25 * lax.dynamic_slice_in_dim(scale_index, own_first, tok_local).astype(f32)
     level_lanes = jnp.broadcast_to(scales[:, None], (tok_local, 128))
-    all_inputs, enc_low, dec_cols, norms_row, counts = front(
+    mask_lanes = jnp.broadcast_to(mask_float[:, None], (group_tokens, 128))
+    all_inputs, enc_low, dec_cols, norms_row, lasso_row, pull_row, scale_rows = front(
         rows_size, lat_size, picked, norm_params, bias_row, w_joined, w_attn_out, w_mlp_in, w_mlp_out,
-        turn_tables(tok_local), level_lanes, mask_float.reshape(-1, 128), enc_weight, dec_master)
-    count = counts[0, 0]
-    mask_lanes = jnp.broadcast_to(mask_float[:, None], (group_tokens, 128))
-    scale_row = jnp.full((1, depth), 2.0 / count, f32)
-    lasso_scale = lasso_coef / count
+        turn_tables(tok_local), level_lanes, mask_float.reshape(-1, 128), dec_master,
+        own, from_left, from_right, jnp.stack(across))
     active, slope, mass_rows, recon_grad, stats = forward(
-        lat_size, all_inputs, enc_low, dec_cols, enc_bias[None, :], mask_lanes, dec_bias[None, :], scale_row)
+        lat_size, all_inputs, enc_low, dec_cols, enc_bias[None, :], mask_lanes, dec_bias[None, :], scale_rows)
     grad_enc, grad_dec, bias_total, center, totals = backward(
-        rows_size, lat_size, all_inputs, recon_grad, dec_cols, lasso_scale * norms_row, norms_row,
-        lasso_scale / norms_row, mass_rows, stats, dec_master, active, slope)
+        rows_size, lat_size, all_inputs, recon_grad, dec_cols, norms_row, lasso_row, pull_row, mass_rows, stats, dec_master, active, slope)
     grad_enc_bias, grad_dec_bias = bias_total[0], center[0]
     grad_norm = jnp.sqrt(totals[0, 0])
     loss_sum = totals[4, 0]
+    count = scale_rows[1, 0]
     factor = clip_bound / jnp.maximum(grad_norm, clip_bound)
     enc_new = adam_update(enc_weight, enc_moment, enc_second, grad_enc * factor, weight_decay)
     dec_new = adam_update(dec_weight, dec_moment, dec_second, grad_dec.T * factor, weight_decay)

time: 405 us -> 389 us (0.960)
  Pallas kernels: 345 us -> 323 us
  starting transfers between devices: 0 us -> 7.83 us
    pallas_call x1, Pallas kernels: 110 us -> 88.5 us  [front(): pl.pallas_call(functools.partial(front_kernel, rows_size, lat_size), out_...]
    ppermute x0 -> x3, starting transfers between devices: none -> 7.83 us  [the longest x1 3.53 us: body(): from_left = lax.ppermute(own, 'rows', right_pairs)]
    convert_element_type x1 -> x0, other arithmetic: 6.16 us -> none  [body(): picked = (picked * inside[:, None]).astype(bf16)]
    select_n x0 -> x1, other arithmetic: none -> 4.48 us  [body(): picked = jnp.where(inside[:, None], picked, jnp.zeros((), bf16))]
  transfers between devices with their start and end apart: 0 -> 3, of which waited for: 0 -> 0; matrix products, arithmetic and copies ran while one was open for 0% -> 9% of each run, Pallas kernels for 0% -> 0%
where the time goes in v4:
time: 389 us; the launch traced here: 386 us
  Pallas kernels  323 us (83%)
  local copies, waits for them, and re-layouts  30.9 us (8%)
  other arithmetic  20.6 us (5%)
  starting transfers between devices  7.83 us (2%)
    pallas_call x1, Pallas kernels, backward(): pl.pallas_call(functools.partial(backward_kernel, rows_size, lat_size), o...  131 us
    pallas_call x1, Pallas kernels, forward(): pl.pallas_call(functools.partial(forward_kernel, lat_size), out_shape=[ja...  104 us
    pallas_call x1, Pallas kernels, front(): pl.pallas_call(functools.partial(front_kernel, rows_size, lat_size), out_...  88.5 us
    gather x1, local copies, waits for them, and re-layouts, body(): picked = jnp.take(embed, jnp.clip(local_ids, 0, vocab_local - 1), axis=0)  24.3 us
  transfers between devices with their start and end apart: 3, of which 0 were waited for; matrix products, arithmetic and copies ran while one was open for 9% of the time, Pallas kernels for 0%

profile of v4, /device:TPU:0, one launch (start us, length us, event | category | flops | bytes accessed | tf_op | source)
XLA Modules:
  0.0 385.9 jit_solution(6735496935320189181)
XLA Ops:
  0.7 1.3 convert_bitcast_fusion
  2.0 1.3 convert_bitcast_fusion.1
  3.3 0.1 pad_maximum_fusion.1.own_ref
  3.4 0.0 copy-start.2
  3.4 3.0 collective-permute-start.2
  6.4 3.5 collective-permute-start
  9.9 1.3 collective-permute-start.1
  11.3 0.0 copy-done.10
  11.3 0.1 mul.251
  11.4 0.6 fusion.13
  12.0 0.0 copy-done.12
  12.0 0.6 broadcast_in_dim.70.bias_ref
  12.7 0.7 multiply_add_fusion.2
  13.4 24.3 %gather_fusion = bf16[4096,512]{1,0:T(8,128)(2,1)} fusion(bf16[12576,512]{1,0:T(8,128)(2,1)} %param.25, s32[4096]{0:T(1024)S(1)} %fusion.6), kind=kCustom, calls=%fused_computation | custom fusion | bytes 8404992 | tf_op jit(solution)/shard_map/jit(_take)/gather | solution.py:1065
  37.6 2.0 cosine_select_fusion
  39.7 1.3 pad_maximum_fusion.turn_ref
  40.9 4.5 %select_select_fusion.picked_ref = bf16[4096,512]{1,0:T(8,128)(2,1)} fusion(bf16[4096,512]{1,0:T(8,128)(2,1)S(1)} %copy-done.1, pred[4096]{0:T(1024)(128)(4,1)S(1)} %get-tuple-element.64, pred[4096]{0:T(1024)(128)(4,1)S(1)} %get-tuple-element.63), kind=kLoop, calls=%fused_computation.1 | loop fusion | flops 4194304 | bytes 8396800 | tf_op jit(solution)/shard_map/jit(_where)/select_n | solution.py:1066
  45.4 0.0 collective-permute-done.2
  45.4 0.0 collective-permute-done.left_ref
  45.4 0.0 copy-start.5
  45.4 0.0 collective-permute-done.1.right_ref
  45.4 1.2 broadcast_in_dim.76.level_ref
  46.6 0.3 copy-done.5
  46.9 88.5 %front.1 = (bf16[4096,512]{1,0:T(8,128)(2,1)}, bf16[512,4096]{1,0:T(8,128)(2,1)}, bf16[512,4096]{1,0:T(8,128)(2,1)}, f32[1,4096]{1,0:T(1,128)}, f32[1,4096]{1,0:...) custom-call(bf16[4096,512]{1,0:T(8,128)(2,1)} %select_select_fusion.picked_ref, f32[4,512]{1,0:T(4,128)} %norm_ref.1, ...), custom_call_target="tpu_custom_call" | custom-call | tf_op jit(solution)/shard_map/front/pallas_call | solution.py:354
  135.4 1.2 slice.11
  136.6 1.9 broadcast_in_dim.78.mask_ref
  138.5 103.7 %forward.1 = (bf16[8,4096,512]{2,1,0:T(8,128)(2,1)}, f32[8,4096,512]{2,1,0:T(8,128)}, f32[8,4096]{1,0:T(8,128)}, bf16[4096,512]{1,0:T(8,128)(2,1)}, f32[16,512]{1,0:T(8,128)}) custom-call(bf16[4096,512]{1,0:T(8,128)(2,1)} %get-tuple-element.32.inputs_ref, bf16[512,4096]{1,0:T(8,128)(2,1)} %get-tuple-element.33.enc_ref, ...), custom_call_target="tpu_custom_call" | custom-call | tf_op jit(solution)/shard_map/forward/pallas_call | solution.py:620
  242.2 0.0 copy-start.16
  242.2 0.0 copy-start.17
  242.2 0.0 copy-start.18
  242.2 0.0 copy-start.11
  242.3 0.0 copy-start.14
  242.3 0.0 copy-start.15
  242.3 0.0 copy-start
  242.3 0.0 copy-start.6
  242.3 131.2 %backward.1 = (f32[64,4096]{1,0:T(8,128)}, f32[64,4096]{1,0:T(8,128)}, f32[1,4096]{1,0:T(1,128)}, f32[1,512]{1,0:T(1,128)}, f32[8,128]{1,0:T(8,128)}) custom-call(bf16[4096,512]{1,0:T(8,128)(2,1)} %get-tuple-element.32.inputs_ref, bf16[4096,512]{1,0:T(8,128)(2,1)} %get-tuple-element.36.back_ref, bf16[512,4096]{1,0:T(8,128)(2,1)} %get-tuple-element.34.dec_ref, ...), custom_call_target="tpu_custom_call" | custom-call | tf_op jit(solution)/shard_map/backward/pallas_call | solution.py:987
  373.6 0.0 copy-start.3
  373.6 1.3 fusion.14
  375.6 0.0 copy-start.7
  375.6 0.0 copy-start.8
  375.6 0.8 broadcast_multiply_fusion.1
  376.5 0.8 broadcast_multiply_fusion
  377.3 0.6 multiply_subtract_fusion.3
  377.9 0.0 copy-done.14
  377.9 0.6 multiply_subtract_fusion.2
  378.6 3.7 multiply_subtract_fusion
  382.3 0.0 copy-done.9
  382.3 2.2 multiply_subtract_fusion.1
  (26 shorter events, 0.1 us)
Async XLA Ops:
  0.6 10.6 %copy-start.10 = (s32[4096]{0:T(1024)S(1)}, s32[4096]{0:T(1024)}, u32[]{:S(2)}) copy-start(s32[4096]{0:T(1024)} %param.22) | copy-start | bytes 49156
  0.7 10.8 %copy-start.13 = (s32[4096]{0:T(1024)S(1)}, s32[4096]{0:T(1024)}, u32[]{:S(2)}) copy-start(s32[4096]{0:T(1024)} %param.23) | copy-start | bytes 49156
  0.7 11.4 %copy-start.12 = (f32[4608]{0:T(1024)S(1)}, f32[4608]{0:T(1024)}, u32[]{:S(2)}) copy-start(f32[4608]{0:T(1024)} %param.27) | copy-start | bytes 55300
  3.4 34.3 %copy-start.2 = (bf16[2,64,4096]{2,1,0:T(8,128)(2,1)}, bf16[2,64,4096]{2,1,0:T(8,128)(2,1)S(1)}, u32[]{:S(2)}) copy-start(bf16[2,64,4096]{2,1,0:T(8,128)(2,1)S(1)} %pad_maximum_fusion.1.own_ref) | copy-start | bytes 3145732
  3.4 42.0 %collective-permute-start.2 = (bf16[2,64,4096]{2,1,0:T(8,128)(2,1)S(1)}, bf16[2,64,4096]{2,1,0:T(8,128)(2,1)S(1)}, u32[]{:S(2)}, u32[]{:S(2)}) collective-permute-start(bf16[2,64,4096]{2,1,0:T(8,128)(2,1)S(1)} %pad_maximum_fusion.1.own_ref), channel_id=1, source_target_pairs={{4,0},{0,4},{12,8},{8,12},{20,16},{16,20},{28,24},{24,28},{5,1},{1... | collective-permute-start | bytes 3145736 | tf_op jit(solution)/shard_map/ppermute | solution.py:1076
  6.4 39.0 %collective-permute-start = (bf16[2,64,4096]{2,1,0:T(8,128)(2,1)S(1)}, bf16[2,64,4096]{2,1,0:T(8,128)(2,1)S(1)}, u32[]{:S(2)}, u32[]{:S(2)}) collective-permute-start(bf16[2,64,4096]{2,1,0:T(8,128)(2,1)S(1)} %pad_maximum_fusion.1.own_ref), channel_id=1, source_target_pairs={{0,8},{4,12},{8,16},{12,20},{16,24},{20,28},{1,9},{5,13},{9,17},{1... | collective-permute-start | bytes 3145736 | tf_op jit(solution)/shard_map/ppermute | solution.py:1071
  9.9 35.5 %collective-permute-start.1 = (bf16[2,64,4096]{2,1,0:T(8,128)(2,1)S(1)}, bf16[2,64,4096]{2,1,0:T(8,128)(2,1)}, u32[]{:S(2)}, u32[]{:S(2)}) collective-permute-start(bf16[2,64,4096]{2,1,0:T(8,128)(2,1)S(1)} %pad_maximum_fusion.1.own_ref), channel_id=1, source_target_pairs={{8,0},{12,4},{16,8},{20,12},{24,16},{28,20},{9,1},{13,5},{17,9},{2... | collective-permute-start | bytes 3145736 | tf_op jit(solution)/shard_map/ppermute | solution.py:1072
  37.6 3.3 copy-start.1
  45.4 1.2 copy-start.4
  45.4 1.5 copy-start.5
  242.2 135.1 %copy-start.16 = (f32[512]{0:T(512)S(1)}, f32[512]{0:T(512)}, u32[]{:S(2)}) copy-start(f32[512]{0:T(512)} %param.41) | copy-start | bytes 6148
  242.2 135.1 %copy-start.17 = (f32[512]{0:T(512)S(1)}, f32[512]{0:T(512)}, u32[]{:S(2)}) copy-start(f32[512]{0:T(512)} %param.42) | copy-start | bytes 6148
  242.2 135.1 %copy-start.18 = (f32[512]{0:T(512)S(1)}, f32[512]{0:T(512)}, u32[]{:S(2)}) copy-start(f32[512]{0:T(512)} %param.43) | copy-start | bytes 6148
  242.2 135.7 %copy-start.11 = (f32[4096]{0:T(1024)S(1)}, f32[4096]{0:T(1024)}, u32[]{:S(2)}) copy-start(f32[4096]{0:T(1024)} %param.38) | copy-start | bytes 49156
  242.3 135.7 %copy-start.14 = (f32[4096]{0:T(1024)S(1)}, f32[4096]{0:T(1024)}, u32[]{:S(2)}) copy-start(f32[4096]{0:T(1024)} %param.39) | copy-start | bytes 49156
  242.3 135.6 %copy-start.15 = (f32[4096]{0:T(1024)S(1)}, f32[4096]{0:T(1024)}, u32[]{:S(2)}) copy-start(f32[4096]{0:T(1024)} %param.40) | copy-start | bytes 49156
  242.3 136.3 %copy-start = (f32[4096,64]{0,1:T(8,128)S(1)}, f32[4096,64]{0,1:T(8,128)}, u32[]{:S(2)}) copy-start(f32[4096,64]{0,1:T(8,128)} %param.35) | copy-start | bytes 3145732
  242.3 136.3 %copy-start.6 = (f32[4096,64]{0,1:T(8,128)S(1)}, f32[4096,64]{0,1:T(8,128)}, u32[]{:S(2)}) copy-start(f32[4096,64]{0,1:T(8,128)} %param.36) | copy-start | bytes 3145732
  373.6 8.7 %copy-start.3 = (f32[64,4096]{1,0:T(8,128)S(1)}, f32[64,4096]{1,0:T(8,128)}, u32[]{:S(2)}) copy-start(f32[64,4096]{1,0:T(8,128)} %param.32) | copy-start | bytes 3145732
  375.6 6.7 %copy-start.7 = (f32[64,4096]{1,0:T(8,128)S(1)}, f32[64,4096]{1,0:T(8,128)}, u32[]{:S(2)}) copy-start(f32[64,4096]{1,0:T(8,128)} %param.33) | copy-start | bytes 3145732
  375.6 6.7 %copy-start.8 = (f32[64,4096]{1,0:T(8,128)S(1)}, f32[64,4096]{1,0:T(8,128)}, u32[]{:S(2)}) copy-start(f32[64,4096]{1,0:T(8,128)} %param.34) | copy-start | bytes 3145732
  375.6 6.7 %copy-start.9 = (f32[64,4096]{1,0:T(8,128)S(1)}, f32[64,4096]{1,0:T(8,128)}, u32[]{:S(2)}) copy-start(f32[64,4096]{1,0:T(8,128)} %get-tuple-element.44) | copy-start | bytes 3145732

commit v5 on v4

--- a/solution.py
+++ b/solution.py
@@ -44,17 +44,26 @@
 
 def front_kernel(
     rows_size, lat_size,
-    picked_ref, norm_ref, bias_ref, joined_ref, attn_ref, mlp_in_ref, mlp_out_ref,
-    turn_ref, level_ref, mask_ref, dec_ref, own_ref, left_ref, right_ref, across_ref,
+    picked_ref, norm_ref, bias_ref, mask_ref, dec_ref,
+    joined_hbm, attn_hbm, mlp_in_hbm, mlp_out_hbm, turn_hbm, level_hbm, own_ref, left_ref, right_ref, across_ref,
     inputs_out, enc_out, dec_out, norms_out, lasso_out, pull_out, scale_out,
     from_core, from_y, base, queries, keys, values, context, ready, facts, got_facts,
-    place_sem,
+    joined_ref, attn_ref, mlp_in_ref, mlp_out_ref, turn_ref, level_ref,
+    load_sem, place_sem,
     out_right, in_left, out_left, in_right, out_x, in_x, out_fact, in_fact,
     out_core, in_core, out_y, in_y, out_own, in_own, out_near, in_near,
 ):
     tokens, depth = base.shape
     shard, latents = dec_ref.shape
     hidden = mlp_in_ref.shape[1]
+    loads = [
+        pltpu.make_async_copy(source, target, load_sem.at[at])
+        for at, (source, target) in enumerate((
+            (joined_hbm, joined_ref), (turn_hbm, turn_ref), (mlp_in_hbm, mlp_in_ref),
+            (mlp_out_hbm, mlp_out_ref), (attn_hbm, attn_ref), (level_hbm, level_ref)))
+    ]
+    for load in loads:
+        load.start()
     x_size = rows_size // Z_CHIPS
     y_size = lat_size // CORES
     pieces = tokens // PIECE
@@ -215,6 +224,8 @@
                 tile * cosine + pltpu.roll(tile, PAIR - ROT // 2, 1) * low + pltpu.roll(tile, ROT // 2, 1) * high)
         return jnp.concatenate(parts, axis=1)
 
+    for load in loads:
+        load.wait()
     for block in range(tokens // ROWS):
         rows = pl.ds(block * ROWS, ROWS)
         for piece in range(block * ROWS // PIECE, (block + 1) * ROWS // PIECE):
@@ -362,7 +373,7 @@
             jax.ShapeDtypeStruct((1, latents), f32),
             jax.ShapeDtypeStruct((8, depth), f32),
         ],
-        in_specs=[vmem] * 15,
+        in_specs=[vmem] * 5 + [hbm] * 6 + [vmem] * 4,
         out_specs=[hbm] * 3 + [vmem] * 4,
         scratch_shapes=[
             pltpu.VMEM((y_size, tokens, depth), bf16),
@@ -375,7 +386,8 @@
             pltpu.VMEM((tokens, depth), bf16),
             pltpu.VMEM((16, latents // 8), f32),
             pltpu.VMEM((rows_size - 1, 16, latents // 8), f32),
-            dma((x_size + 3, max(pieces, 2))),
+            *[pltpu.VMEM(a.shape, a.dtype) for a in (w_joined, w_attn_out, w_mlp_in, w_mlp_out, turns, level_lanes)],
+            dma((6,)), dma((x_size + 3, max(pieces, 2))),
             dma((hops, 2)), dma((hops, 2)), dma((hops, 2)), dma((hops, 2)),
             dma((Z_CHIPS, 2, x_size - 1)), dma((Z_CHIPS, 2, x_size - 1)),
             dma((rows_size - 1,)), dma((rows_size - 1,)),
@@ -387,8 +399,8 @@
         compiler_params=pltpu.CompilerParams(
             collective_id=3, has_side_effects=True, vmem_limit_bytes=60 * 2**20),
         name="front",
-    )(picked, norm_params, bias_row, w_joined, w_attn_out, w_mlp_in, w_mlp_out,
-      turns, level_lanes, mask_tiles, dec_shard, own, left, right, across)
+    )(picked, norm_params, bias_row, mask_tiles, dec_shard,
+      w_joined, w_attn_out, w_mlp_in, w_mlp_out, turns, level_lanes, own, left, right, across)
 
 
 def turn_tables(length):
@@ -414,14 +426,23 @@
 
 def forward_kernel(
     lat_size,
-    inputs_ref, enc_ref, dec_ref, enc_bias_ref, mask_ref, dec_bias_ref, scale_ref,
+    inputs_hbm, enc_hbm, dec_hbm, mask_hbm, enc_bias_ref, dec_bias_ref, scale_ref,
     active_hbm, slope_hbm, mass_out, back_out, stats_out,
-    active_buf, slope_buf, product, partial, own, send_two, recv_one, recv_two,
-    active_sem, slope_sem, out_one, in_one, out_two, in_two, out_three, in_three, out_four, in_four,
+    active_buf, slope_buf, product, partial, own, send_two, units_two, recv_one, recv_two, got_two,
+    inputs_ref, enc_ref, dec_ref, mask_ref, load_sem,
+    active_sem, slope_sem, out_one, in_one, out_two, in_two, outu_two, inu_two, out_three, in_three, out_four, in_four,
 ):
     tokens, depth = inputs_ref.shape
     latents = enc_ref.shape[1]
     chunk, span = product.shape[1:]
+    halves = [pl.ds(at * span, span) for at in range(latents // span)]
+    loads = [pltpu.make_async_copy(inputs_hbm, inputs_ref, load_sem.at[0]), pltpu.make_async_copy(mask_hbm, mask_ref, load_sem.at[1])]
+    for at, cols in enumerate(halves):
+        loads.append(pltpu.make_async_copy(enc_hbm.at[:, cols], enc_ref.at[:, cols], load_sem.at[2 + 2 * at]))
+        loads.append(pltpu.make_async_copy(dec_hbm.at[:, cols], dec_ref.at[:, cols], load_sem.at[3 + 2 * at]))
+    for load in loads:
+        load.start()
+
     width = active_hbm.shape[2]
     chunks, spans = tokens // chunk, latents // span
     y_size = lat_size // CORES
@@ -452,11 +473,15 @@
             partial.at[slot, pl.ds(share_rows(y, other), share)], recv_one.at[block, y],
             out_one.at[slot, y], in_one.at[block, y], my_y * CORES + other)
 
-    def copy_two(block, step):
+    def copies_two(block, step):
         slot = lax.rem(block, 2)
-        return remote(
-            send_two.at[slot, step - 1], recv_two.at[block, step - 1],
-            out_two.at[slot, step - 1], in_two.at[block, step - 1], y_peer(step) * CORES + core)
+        target = y_peer(step) * CORES + core
+        return [
+            remote(send_two.at[slot, step - 1], recv_two.at[block, step - 1],
+                   out_two.at[slot, step - 1], in_two.at[block, step - 1], target),
+            remote(units_two.at[slot, step - 1], got_two.at[block, step - 1],
+                   outu_two.at[slot, step - 1], inu_two.at[block, step - 1], target),
+        ]
 
     def copy_three(block, step):
         mine = back_out.at[token_rows(block, my_y, core)]
@@ -505,6 +530,11 @@
                 def _():
                     for copy in stores(block - 1, spans - 2 + at, slot):
                         copy.wait()
+
+            @pl.when(block == 0)
+            def _():
+                for load in loads[2 * at + 2 : 2 * at + 4] + (loads[:2] if at == 0 else []):
+                    load.wait()
 
             product[slot] = jnp.dot(
                 inputs_ref[pl.ds(first, chunk), :], enc_ref[:, at * span : (at + 1) * span], preferred_element_type=f32)
@@ -532,8 +562,6 @@
     def exchange(block):
         slot = lax.rem(block, 2)
         for y in range(y_size):
-            copy_one(block, y).start()
-        for y in range(y_size):
             copy_one(block, y).wait_recv()
         for step in list(range(1, y_size)) + [0]:
             y = y_peer(step)
@@ -543,18 +571,23 @@
             else:
                 @pl.when(block >= 2)
                 def _():
-                    copy_two(block - 2, step).wait_send()
-
-                send_two[slot, step - 1] = total
-                copy_two(block, step).start()
+                    for copy in copies_two(block - 2, step):
+                        copy.wait_send()
+
+                code, unit = encode(total)
+                send_two[slot, step - 1] = code
+                put_units(units_two, (slot, step - 1), unit)
+                for copy in copies_two(block, step):
+                    copy.start()
 
     def settle(block):
         slot = lax.rem(block, 2)
         rows = token_rows(block, my_y, core)
         total = own[slot]
         for step in range(1, y_size):
-            copy_two(block, step).wait_recv()
-            total = total + recv_two[block, step - 1]
+            for copy in copies_two(block, step):
+                copy.wait_recv()
+            total = total + decode(recv_two[block, step - 1], get_units(got_two, (block, step - 1), depth))
         error = total + dec_bias_ref[...] - inputs_ref[rows, :].astype(f32)
         mask = jnp.concatenate([mask_ref[rows, :]] * (depth // 128), axis=1)
         low = (scale_ref[0:1, :] * mask * error).astype(bf16)
@@ -574,19 +607,24 @@
         @pl.when(block < chunks)
         def _():
             compute(block)
-            exchange(block)
+            for y in range(y_size):
+                copy_one(block, y).start()
 
         @pl.when((block >= 1) & (block <= chunks))
         def _():
-            settle(block - 1)
-
-        @pl.when(block >= 2)
+            exchange(block - 1)
+
+        @pl.when((block >= 2) & (block <= chunks + 1))
         def _():
-            spread(block - 2)
+            settle(block - 2)
+
+        @pl.when(block >= 3)
+        def _():
+            spread(block - 3)
 
         return carry
 
-    lax.fori_loop(0, chunks + 2, turn, 0)
+    lax.fori_loop(0, chunks + 3, turn, 0)
     for slot in range(2):
         for copy in stores(chunks - 1, spans - 2 + slot, slot):
             copy.wait()
@@ -594,7 +632,8 @@
         for y in range(y_size):
             copy_one(block, y).wait_send()
         for step in range(1, y_size):
-            copy_two(block, step).wait_send()
+            for copy in copies_two(block, step):
+                copy.wait_send()
 
     def drain(block, carry):
         for step in range(1, y_size):
@@ -626,7 +665,7 @@
             jax.ShapeDtypeStruct((tokens, depth), bf16),
             jax.ShapeDtypeStruct((16, depth), f32),
         ],
-        in_specs=[vmem] * 7,
+        in_specs=[hbm] * 4 + [vmem] * 3,
         out_specs=[hbm, hbm, vmem, vmem, vmem],
         scratch_shapes=[
             pltpu.VMEM((2, chunk, span), bf16),
@@ -634,11 +673,16 @@
             pltpu.VMEM((2, chunk, span), f32),
             pltpu.VMEM((2, chunk, depth), f32),
             pltpu.VMEM((2, share, depth), f32),
-            pltpu.VMEM((2, y_size - 1, share, depth), f32),
+            pltpu.VMEM((2, y_size - 1, share, depth), jnp.int16),
+            pltpu.VMEM((2, y_size - 1, 8, 128), f32),
             pltpu.VMEM((chunks, y_size, share, depth), f32),
-            pltpu.VMEM((chunks, y_size - 1, share, depth), f32),
+            pltpu.VMEM((chunks, y_size - 1, share, depth), jnp.int16),
+            pltpu.VMEM((chunks, y_size - 1, 8, 128), f32),
+            *[pltpu.VMEM(a.shape, a.dtype) for a in (inputs, enc_low, dec_cols, mask_lanes)],
+            dma((2 + 2 * (latents // span),)),
             dma((2, span // width)), dma((2, span // width)),
             dma((2, y_size)), dma((chunks, y_size)),
+            dma((2, y_size - 1)), dma((chunks, y_size - 1)),
             dma((2, y_size - 1)), dma((chunks, y_size - 1)),
             dma((chunks, y_size - 1)), dma((chunks, y_size - 1)),
             dma((chunks, y_size)), dma((chunks, y_size)),
@@ -646,7 +690,7 @@
         compiler_params=pltpu.CompilerParams(
             collective_id=1, has_side_effects=True, vmem_limit_bytes=60 * 2**20),
         name="forward",
-    )(inputs, enc_low, dec_cols, enc_bias_row, mask_lanes, dec_bias_row, scale_rows)
+    )(inputs, enc_low, dec_cols, mask_lanes, enc_bias_row, dec_bias_row, scale_rows)
 
 
 def encode(value):
@@ -672,13 +716,13 @@
 
 def backward_kernel(
     rows_size, lat_size,
-    inputs_ref, back_ref, dec_ref, norms_ref, lasso_ref, pull_ref, mass_ref, stats_ref, master_ref,
-    active_hbm, slope_hbm,
+    back_ref, norms_ref, lasso_ref, pull_ref, mass_ref, stats_ref,
+    inputs_hbm, dec_hbm, master_hbm, active_hbm, slope_hbm,
     enc_out, dec_out, bias_out, center_out, totals_out,
     grad_low, active_buf, slope_buf, sums,
     send_one, units_one, recv_one, got_one,
     send_two, units_two, recv_two, got_two,
-    bias_rows, pull_cols, facts, tiles,
+    bias_rows, pull_cols, facts, tiles, inputs_ref, dec_ref, master_ref, load_sem,
     active_sem, slope_sem,
     out_one, in_one, outu_one, inu_one, out_two, in_two, outu_two, inu_two, out_facts, in_facts, out_tiles, in_tiles,
 ):
@@ -802,7 +846,13 @@
             barrier, inc=1, device_id=(target // lat_size, lax.rem(target, lat_size)), device_id_type=MESH)
 
     over_devices(greet)
+    loads = [
+        pltpu.make_async_copy(source, target, load_sem.at[at])
+        for at, (source, target) in enumerate(((dec_hbm, dec_ref), (inputs_hbm, inputs_ref), (master_hbm, master_ref)))
+    ]
     active_copy(0).start()
+    for load in loads:
+        load.start()
     ahead = slope_buf.shape[0] - 1
     for index in range(ahead):
         slope_copy(index).start()
@@ -833,6 +883,11 @@
     def compute_enc(block):
         slot = lax.rem(block, 2)
         cols = columns(block)
+
+        @pl.when(block == 0)
+        def _():
+            for load in loads:
+                load.wait()
 
         def piece(index, total):
             at = block * chunks + index
@@ -993,7 +1048,7 @@
             jax.ShapeDtypeStruct((1, depth), f32),
             jax.ShapeDtypeStruct((8, 128), f32),
         ],
-        in_specs=[vmem] * 9 + [hbm] * 2,
+        in_specs=[vmem] * 6 + [hbm] * 5,
         out_specs=[vmem] * 5,
         scratch_shapes=[
             pltpu.VMEM((tokens, width), bf16),
@@ -1012,6 +1067,8 @@
             pltpu.VMEM((1, latents), f32),
             pltpu.VMEM((2, rows_size, 8, latents // 8), f32),
             pltpu.VMEM((2, devices, 8, 128), f32),
+            *[pltpu.VMEM(a.shape, a.dtype) for a in (inputs, dec_cols, master)],
+            dma((3,)),
             dma((2,)), dma((SLOTS,)),
             dma((2, 2, x_size - 1)), dma((blocks, 2, x_size - 1)),
             dma((2, 2, x_size - 1)), dma((blocks, 2, x_size - 1)),
@@ -1022,7 +1079,50 @@
         compiler_params=pltpu.CompilerParams(
             collective_id=2, has_side_effects=True, vmem_limit_bytes=61 * 2**20),
         name="backward",
-    )(inputs, back, dec_cols, norms_row, lasso_row, pull_row, mass_rows, stats, master, active, slope)
+    )(back, norms_row, lasso_row, pull_row, mass_rows, stats, inputs, dec_cols, master, active, slope)
+
+
+def update_kernel(
+    totals_ref, enc_grad, dec_grad, enc_bias_grad, dec_bias_grad,
+    enc_w, enc_m, enc_s, dec_w, dec_m, dec_s, enc_b, enc_bm, enc_bs, dec_b, dec_bm, dec_bs,
+    enc_w_out, enc_m_out, enc_s_out, dec_w_out, dec_m_out, dec_s_out,
+    enc_b_out, enc_bm_out, enc_bs_out, dec_b_out, dec_bm_out, dec_bs_out, scalars_out,
+):
+    norm = jnp.sqrt(totals_ref[0:1, 0:1])
+    factor = clip_bound / jnp.maximum(norm, clip_bound)
+    groups = (
+        (enc_grad, (enc_w, enc_m, enc_s), (enc_w_out, enc_m_out, enc_s_out), weight_decay),
+        (dec_grad, (dec_w, dec_m, dec_s), (dec_w_out, dec_m_out, dec_s_out), weight_decay),
+        (enc_bias_grad, (enc_b, enc_bm, enc_bs), (enc_b_out, enc_bm_out, enc_bs_out), 0.0),
+        (dec_bias_grad, (dec_b, dec_bm, dec_bs), (dec_b_out, dec_bm_out, dec_bs_out), 0.0),
+    )
+    for grad, olds, news, decay in groups:
+        found = adam_update(*[old[...] for old in olds], grad[...] * factor, decay)
+        for new, value in zip(news, found):
+            new[...] = value
+    scalars_out[0:1, :] = jnp.broadcast_to(norm, (1, 128))
+    scalars_out[1:2, :] = totals_ref[4:5, :]
+    scalars_out[2:8, :] = jnp.zeros((6, 128), f32)
+
+
+def update(totals, grads, states):
+    shard, latents = grads[0].shape
+    depth = grads[3].shape[1]
+    span = latents // 4
+    wide = pl.BlockSpec((shard, span), lambda i: (0, i))
+    row = pl.BlockSpec((1, span), lambda i: (0, i))
+    short = pl.BlockSpec((1, depth), lambda i: (0, 0))
+    tile = pl.BlockSpec((8, 128), lambda i: (0, 0))
+    state_specs = [wide] * 6 + [row] * 3 + [short] * 3
+    return pl.pallas_call(
+        update_kernel,
+        grid=(latents // span,),
+        out_shape=[jax.ShapeDtypeStruct(a.shape, f32) for a in states] + [jax.ShapeDtypeStruct((8, 128), f32)],
+        in_specs=[tile, wide, wide, row, short] + state_specs,
+        out_specs=state_specs + [tile],
+        compiler_params=pltpu.CompilerParams(vmem_limit_bytes=48 * 2**20),
+        name="update",
+    )(totals, *grads, *states)
 
 
 def body(
@@ -1086,35 +1186,19 @@
         lat_size, all_inputs, enc_low, dec_cols, enc_bias[None, :], mask_lanes, dec_bias[None, :], scale_rows)
     grad_enc, grad_dec, bias_total, center, totals = backward(
         rows_size, lat_size, all_inputs, recon_grad, dec_cols, norms_row, lasso_row, pull_row, mass_rows, stats, dec_master, active, slope)
-    grad_enc_bias, grad_dec_bias = bias_total[0], center[0]
-    grad_norm = jnp.sqrt(totals[0, 0])
-    loss_sum = totals[4, 0]
-    count = scale_rows[1, 0]
-    factor = clip_bound / jnp.maximum(grad_norm, clip_bound)
-    enc_new = adam_update(enc_weight, enc_moment, enc_second, grad_enc * factor, weight_decay)
-    dec_new = adam_update(dec_weight, dec_moment, dec_second, grad_dec.T * factor, weight_decay)
-    enc_bias_new = adam_update(
-        enc_bias, enc_bias_moment, enc_bias_second, grad_enc_bias * factor, 0.0
-    )
-    dec_bias_new = adam_update(
-        dec_bias, dec_bias_moment, dec_bias_second, grad_dec_bias * factor, 0.0
-    )
+    states = [
+        enc_weight, enc_moment, enc_second, dec_master, dec_moment.T, dec_second.T,
+        enc_bias[None, :], enc_bias_moment[None, :], enc_bias_second[None, :],
+        dec_bias[None, :], dec_bias_moment[None, :], dec_bias_second[None, :],
+    ]
+    *fresh, scalars = update(totals, (grad_enc, grad_dec, bias_total, center), states)
     return (
-        enc_new[0],
-        enc_new[1],
-        enc_new[2],
-        dec_new[0],
-        dec_new[1],
-        dec_new[2],
-        enc_bias_new[0],
-        enc_bias_new[1],
-        enc_bias_new[2],
-        dec_bias_new[0],
-        dec_bias_new[1],
-        dec_bias_new[2],
-        grad_norm,
-        loss_sum,
-        count,
+        *fresh[:3],
+        *[value.T for value in fresh[3:6]],
+        *[value[0] for value in fresh[6:]],
+        scalars[0, 0],
+        scalars[1, 0],
+        scale_rows[1, 0],
     )
 
 

time: 389 us -> 374 us (0.961)
  Pallas kernels: 323 us -> 314 us
  other arithmetic: 20.6 us -> 11.8 us
  local copies, waits for them, and re-layouts: 30.9 us -> 35.5 us
    pallas_call x1, Pallas kernels: 104 us -> 91.4 us  [forward(): pl.pallas_call(functools.partial(forward_kernel, lat_size), out_shape=[ja...]
    sub x4 -> x0, other arithmetic: 7.18 us -> none  [adam_update(): weight_new = weight - learn_rate * (corrected / scaled + decay * weight)]
    pallas_call x0 -> x1, Pallas kernels: none -> 5.88 us  [update(): pl.pallas_call(update_kernel, grid=(latents // span,), out_shape=[jax.Sha...]
    unnamed x38 -> x42, local copies, waits for them, and re-layouts: 0.38 us -> 6.07 us
where the time goes in v5:
time: 374 us; the launch traced here: 371 us
  Pallas kernels  314 us (84%)
  local copies, waits for them, and re-layouts  35.5 us (9%)
  other arithmetic  11.8 us (3%)
  starting transfers between devices  7.83 us (2%)
    pallas_call x1, Pallas kernels, backward(): pl.pallas_call(functools.partial(backward_kernel, rows_size, lat_size), o...  131 us
    pallas_call x1, Pallas kernels, forward(): pl.pallas_call(functools.partial(forward_kernel, lat_size), out_shape=[ja...  91.4 us
    pallas_call x1, Pallas kernels, front(): pl.pallas_call(functools.partial(front_kernel, rows_size, lat_size), out_...  86.1 us
    gather x1, local copies, waits for them, and re-layouts, body(): picked = jnp.take(embed, jnp.clip(local_ids, 0, vocab_local - 1), axis=0)  24 us
  transfers between devices with their start and end apart: 3, of which 0 were waited for; matrix products, arithmetic and copies ran while one was open for 9% of the time, Pallas kernels for 0%

profile of v5, /device:TPU:0, one launch (start us, length us, event | category | flops | bytes accessed | tf_op | source)
XLA Modules:
  0.0 370.6 jit_solution(16458697532318477034)
XLA Ops:
  0.7 1.3 convert_bitcast_fusion
  2.0 1.3 convert_bitcast_fusion.1
  3.3 0.1 pad_maximum_fusion.1.own_ref
  3.4 0.0 copy-start.15
  3.4 3.0 collective-permute-start.2
  6.4 3.5 collective-permute-start
  9.9 1.3 collective-permute-start.1
  11.3 0.1 mul.62
  11.4 0.6 fusion.3
  12.0 0.6 broadcast_in_dim.84.bias_ref
  12.7 0.7 multiply_add_fusion
  13.4 24.0 %gather_fusion = bf16[4096,512]{1,0:T(8,128)(2,1)} fusion(bf16[12576,512]{1,0:T(8,128)(2,1)} %param.25, s32[4096]{0:T(1024)S(1)} %fusion.2), kind=kCustom, calls=%fused_computation | custom fusion | bytes 8404992 | tf_op jit(solution)/shard_map/jit(_take)/gather | solution.py:1165
  37.3 0.0 copy-done.15
  37.3 2.0 cosine_select_fusion
  39.3 1.3 pad_maximum_fusion.turn_hbm
  40.6 4.5 %select_select_fusion.picked_ref = bf16[4096,512]{1,0:T(8,128)(2,1)} fusion(bf16[4096,512]{1,0:T(8,128)(2,1)S(1)} %copy-done.14, pred[4096]{0:T(1024)(128)(4,1)S(1)} %get-tuple-element.78, pred[4096]{0:T(1024)(128)(4,1)S(1)} %get-tuple-element.77), kind=kLoop, calls=%fused_computation.1 | loop fusion | flops 4194304 | bytes 8396800 | tf_op jit(solution)/shard_map/jit(_where)/select_n | solution.py:1166
  45.1 0.0 collective-permute-done.2
  45.1 0.0 collective-permute-done.left_ref
  45.1 0.0 copy-start.17
  45.1 0.0 collective-permute-done.1.right_ref
  45.1 1.2 broadcast_in_dim.90.level_hbm
  46.3 0.3 copy-done.17
  46.6 86.1 %front.1 = (bf16[4096,512]{1,0:T(8,128)(2,1)}, bf16[512,4096]{1,0:T(8,128)(2,1)}, bf16[512,4096]{1,0:T(8,128)(2,1)}, f32[1,4096]{1,0:T(1,128)}, f32[1,4096]{1,0:...) custom-call(bf16[4096,512]{1,0:T(8,128)(2,1)} %select_select_fusion.picked_ref, f32[4,512]{1,0:T(4,128)} %norm_ref.1, ...), custom_call_target="tpu_custom_call" | custom-call | tf_op jit(solution)/shard_map/front/pallas_call | solution.py:365
  132.7 1.2 slice.11
  133.9 1.9 broadcast_in_dim.91.mask_hbm
  135.8 91.4 %forward.1 = (bf16[8,4096,512]{2,1,0:T(8,128)(2,1)}, f32[8,4096,512]{2,1,0:T(8,128)}, f32[8,4096]{1,0:T(8,128)}, bf16[4096,512]{1,0:T(8,128)(2,1)}, f32[16,512]{1,0:T(8,128)}) custom-call(bf16[4096,512]{1,0:T(8,128)(2,1)} %get-tuple-element.45.inputs_hbm, bf16[512,4096]{1,0:T(8,128)(2,1)} %get-tuple-element.46.enc_hbm, ...), custom_call_target="tpu_custom_call" | custom-call | tf_op jit(solution)/shard_map/forward/pallas_call | solution.py:659
  227.2 0.0 copy-start
  227.2 0.0 copy-start.1
  227.2 0.0 copy-start.5
  227.2 0.0 copy-start.6
  227.3 0.0 copy-start.7
  227.3 0.0 copy-start.9
  227.3 0.0 copy-start.11
  227.3 0.0 copy-start.12
  227.3 130.7 %backward.1 = (f32[64,4096]{1,0:T(8,128)}, f32[64,4096]{1,0:T(8,128)}, f32[1,4096]{1,0:T(1,128)}, f32[1,512]{1,0:T(1,128)}, f32[8,128]{1,0:T(8,128)}) custom-call(bf16[4096,512]{1,0:T(8,128)(2,1)} %get-tuple-element.49.back_ref, f32[1,4096]{1,0:T(1,128)} %get-tuple-element.50.norms_ref, f32[1,4096]{1,0:T(1,128)} %get-tuple-element.51.lasso_ref, ...), custom_call_target="tpu_custom_call" | custom-call | tf_op jit(solution)/shard_map/backward/pallas_call | solution.py:1042
  358.0 0.0 copy-done
  358.0 0.0 copy-done.1
  358.0 0.0 copy-done.5
  358.0 0.0 copy-done.6
  358.0 0.0 copy-start.2
  358.1 1.2 copy-done.2
  359.3 1.2 copy-done.3
  360.5 1.2 copy-done.4
  361.7 0.7 copy-done.8
  362.4 0.7 copy-done.10
  363.1 0.7 copy-done.13
  363.8 5.9 %update.1 = (f32[64,4096]{1,0:T(8,128)}, f32[64,4096]{1,0:T(8,128)}, f32[64,4096]{1,0:T(8,128)}, f32[64,4096]{1,0:T(8,128)}, f32[64,4096]{1,0:T(8,128)}, /*index...) custom-call(f32[8,128]{1,0:T(8,128)S(1)} %copy-done.10, ...), custom_call_target="tpu_custom_call" | custom-call | tf_op jit(solution)/shard_map/update/pallas_call | solution.py:1117
  369.7 0.5 fusion.4
  (25 shorter events, 0.1 us)
Async XLA Ops:
  0.6 10.6 %copy-start.18 = (s32[4096]{0:T(1024)S(1)}, s32[4096]{0:T(1024)}, u32[]{:S(2)}) copy-start(s32[4096]{0:T(1024)} %param.22) | copy-start | bytes 49156
  0.7 10.8 %copy-start.20 = (s32[4096]{0:T(1024)S(1)}, s32[4096]{0:T(1024)}, u32[]{:S(2)}) copy-start(s32[4096]{0:T(1024)} %param.23) | copy-start | bytes 49156
  0.7 11.4 %copy-start.19 = (f32[4608]{0:T(1024)S(1)}, f32[4608]{0:T(1024)}, u32[]{:S(2)}) copy-start(f32[4608]{0:T(1024)} %param.27) | copy-start | bytes 55300
  3.4 34.0 %copy-start.15 = (bf16[2,64,4096]{2,1,0:T(8,128)(2,1)}, bf16[2,64,4096]{2,1,0:T(8,128)(2,1)S(1)}, u32[]{:S(2)}) copy-start(bf16[2,64,4096]{2,1,0:T(8,128)(2,1)S(1)} %pad_maximum_fusion.1.own_ref) | copy-start | bytes 3145732
  3.4 41.7 %collective-permute-start.2 = (bf16[2,64,4096]{2,1,0:T(8,128)(2,1)S(1)}, bf16[2,64,4096]{2,1,0:T(8,128)(2,1)S(1)}, u32[]{:S(2)}, u32[]{:S(2)}) collective-permute-start(bf16[2,64,4096]{2,1,0:T(8,128)(2,1)S(1)} %pad_maximum_fusion.1.own_ref), channel_id=1, source_target_pairs={{4,0},{0,4},{12,8},{8,12},{20,16},{16,20},{28,24},{24,28},{5,1},{1... | collective-permute-start | bytes 3145736 | tf_op jit(solution)/shard_map/ppermute | solution.py:1176
  6.4 38.7 %collective-permute-start = (bf16[2,64,4096]{2,1,0:T(8,128)(2,1)S(1)}, bf16[2,64,4096]{2,1,0:T(8,128)(2,1)S(1)}, u32[]{:S(2)}, u32[]{:S(2)}) collective-permute-start(bf16[2,64,4096]{2,1,0:T(8,128)(2,1)S(1)} %pad_maximum_fusion.1.own_ref), channel_id=1, source_target_pairs={{0,8},{4,12},{8,16},{12,20},{16,24},{20,28},{1,9},{5,13},{9,17},{1... | collective-permute-start | bytes 3145736 | tf_op jit(solution)/shard_map/ppermute | solution.py:1171
  9.9 35.2 %collective-permute-start.1 = (bf16[2,64,4096]{2,1,0:T(8,128)(2,1)S(1)}, bf16[2,64,4096]{2,1,0:T(8,128)(2,1)}, u32[]{:S(2)}, u32[]{:S(2)}) collective-permute-start(bf16[2,64,4096]{2,1,0:T(8,128)(2,1)S(1)} %pad_maximum_fusion.1.own_ref), channel_id=1, source_target_pairs={{8,0},{12,4},{16,8},{20,12},{24,16},{28,20},{9,1},{13,5},{17,9},{2... | collective-permute-start | bytes 3145736 | tf_op jit(solution)/shard_map/ppermute | solution.py:1172
  37.3 3.3 copy-start.14
  45.1 1.2 copy-start.16
  45.1 1.5 copy-start.17
  227.2 130.8 %copy-start = (f32[64,4096]{1,0:T(8,128)S(1)}, f32[64,4096]{1,0:T(8,128)}, u32[]{:S(2)}) copy-start(f32[64,4096]{1,0:T(8,128)} %enc_w.1) | copy-start | bytes 3145732
  227.2 130.8 %copy-start.1 = (f32[64,4096]{1,0:T(8,128)S(1)}, f32[64,4096]{1,0:T(8,128)}, u32[]{:S(2)}) copy-start(f32[64,4096]{1,0:T(8,128)} %enc_m.1) | copy-start | bytes 3145732
  227.2 130.8 %copy-start.5 = (f32[4096]{0:T(1024)S(1)}, f32[4096]{0:T(1024)}, u32[]{:S(2)}) copy-start(f32[4096]{0:T(1024)} %param.38) | copy-start | bytes 49156
  227.2 130.8 %copy-start.6 = (f32[4096]{0:T(1024)S(1)}, f32[4096]{0:T(1024)}, u32[]{:S(2)}) copy-start(f32[4096]{0:T(1024)} %param.39) | copy-start | bytes 49156
  227.3 130.8 %copy-start.7 = (f32[4096]{0:T(1024)S(1)}, f32[4096]{0:T(1024)}, u32[]{:S(2)}) copy-start(f32[4096]{0:T(1024)} %param.40) | copy-start | bytes 49156
  227.3 130.7 %copy-start.9 = (f32[512]{0:T(512)S(1)}, f32[512]{0:T(512)}, u32[]{:S(2)}) copy-start(f32[512]{0:T(512)} %param.41) | copy-start | bytes 6148
  227.3 130.7 %copy-start.11 = (f32[512]{0:T(512)S(1)}, f32[512]{0:T(512)}, u32[]{:S(2)}) copy-start(f32[512]{0:T(512)} %param.42) | copy-start | bytes 6148
  227.3 130.7 %copy-start.12 = (f32[512]{0:T(512)S(1)}, f32[512]{0:T(512)}, u32[]{:S(2)}) copy-start(f32[512]{0:T(512)} %param.43) | copy-start | bytes 6148
  358.0 1.2 copy-start.2
  359.3 1.2 copy-start.3
  360.5 1.2 copy-start.4
  361.7 0.7 copy-start.8
  362.4 0.7 copy-start.10
  363.1 0.7 copy-start.13

commit v6 on v5

--- a/solution.py
+++ b/solution.py
@@ -1,6 +1,7 @@
 import functools
 import jax
 import jax.numpy as jnp
+import numpy as np
 from jax import lax
 from jax.experimental import pallas as pl
 from jax.experimental.pallas import tpu as pltpu
@@ -405,15 +406,15 @@
 
 def turn_tables(length):
     half = ROT // 2
-    freqs = 10000.0 ** (-2.0 * jnp.arange(half, dtype=f32) / ROT)
-    angles = jnp.arange(length, dtype=f32)[:, None] * jnp.tile(freqs, PAIR // half)[None, :]
-    place = jnp.arange(PAIR) % HEAD
-    cosines, sines = jnp.cos(angles), jnp.sin(angles)
-    return jnp.stack([
-        jnp.where(place < ROT, cosines, 1.0),
-        jnp.where(place < half, -sines, 0.0),
-        jnp.where((place >= half) & (place < ROT), sines, 0.0),
-    ])
+    freqs = np.float32(10000.0) ** (np.float32(-2.0) * np.arange(half, dtype=np.float32) / np.float32(ROT))
+    angles = np.arange(length, dtype=np.float32)[:, None] * np.tile(freqs, PAIR // half)[None, :]
+    place = np.arange(PAIR) % HEAD
+    cosines, sines = np.cos(angles.astype(np.float64)), np.sin(angles.astype(np.float64))
+    return np.stack([
+        np.where(place < ROT, cosines, 1.0),
+        np.where(place < half, -sines, 0.0),
+        np.where((place >= half) & (place < ROT), sines, 0.0),
+    ]).astype(np.float32)
 
 
 def softplus_parts(value):
@@ -1083,7 +1084,7 @@
 
 
 def update_kernel(
-    totals_ref, enc_grad, dec_grad, enc_bias_grad, dec_bias_grad,
+    totals_ref, counts_ref, enc_grad, dec_grad, enc_bias_grad, dec_bias_grad,
     enc_w, enc_m, enc_s, dec_w, dec_m, dec_s, enc_b, enc_bm, enc_bs, dec_b, dec_bm, dec_bs,
     enc_w_out, enc_m_out, enc_s_out, dec_w_out, dec_m_out, dec_s_out,
     enc_b_out, enc_bm_out, enc_bs_out, dec_b_out, dec_bm_out, dec_bs_out, scalars_out,
@@ -1102,10 +1103,10 @@
             new[...] = value
     scalars_out[0:1, :] = jnp.broadcast_to(norm, (1, 128))
     scalars_out[1:2, :] = totals_ref[4:5, :]
-    scalars_out[2:8, :] = jnp.zeros((6, 128), f32)
-
-
-def update(totals, grads, states):
+    scalars_out[2:8, :] = counts_ref[2:8, :]
+
+
+def update(totals, counts, grads, states):
     shard, latents = grads[0].shape
     depth = grads[3].shape[1]
     span = latents // 4
@@ -1118,11 +1119,11 @@
         update_kernel,
         grid=(latents // span,),
         out_shape=[jax.ShapeDtypeStruct(a.shape, f32) for a in states] + [jax.ShapeDtypeStruct((8, 128), f32)],
-        in_specs=[tile, wide, wide, row, short] + state_specs,
+        in_specs=[tile, tile, wide, wide, row, short] + state_specs,
         out_specs=state_specs + [tile],
-        compiler_params=pltpu.CompilerParams(vmem_limit_bytes=48 * 2**20),
+        compiler_params=pltpu.CompilerParams(vmem_limit_bytes=61 * 2**20),
         name="update",
-    )(totals, *grads, *states)
+    )(totals, counts, *grads, *states)
 
 
 def body(
@@ -1191,14 +1192,14 @@
         enc_bias[None, :], enc_bias_moment[None, :], enc_bias_second[None, :],
         dec_bias[None, :], dec_bias_moment[None, :], dec_bias_second[None, :],
     ]
-    *fresh, scalars = update(totals, (grad_enc, grad_dec, bias_total, center), states)
+    *fresh, scalars = update(totals, scale_rows, (grad_enc, grad_dec, bias_total, center), states)
     return (
         *fresh[:3],
         *[value.T for value in fresh[3:6]],
         *[value[0] for value in fresh[6:]],
         scalars[0, 0],
         scalars[1, 0],
-        scale_rows[1, 0],
+        scalars[2, 0],
     )
 
 

time: 374 us -> 362 us (0.968)
  local copies, waits for them, and re-layouts: 35.5 us -> 29.2 us
    unnamed x42 -> x12, local copies, waits for them, and re-layouts: 6.07 us -> 0.3 us
    pallas_call x1, Pallas kernels: 86.1 us -> 82 us  [front(): pl.pallas_call(functools.partial(front_kernel, rows_size, lat_size), out_...]
where the time goes in v6:
time: 362 us; the launch traced here: 361 us
  Pallas kernels  312 us (86%)
  local copies, waits for them, and re-layouts  29.2 us (8%)
  starting transfers between devices  9.82 us (3%)
  other arithmetic  9.29 us (3%)
    pallas_call x1, Pallas kernels, backward(): pl.pallas_call(functools.partial(backward_kernel, rows_size, lat_size), o...  132 us
    pallas_call x1, Pallas kernels, forward(): pl.pallas_call(functools.partial(forward_kernel, lat_size), out_shape=[ja...  90.9 us
    pallas_call x1, Pallas kernels, front(): pl.pallas_call(functools.partial(front_kernel, rows_size, lat_size), out_...  82 us
    gather x1, local copies, waits for them, and re-layouts, body(): picked = jnp.take(embed, jnp.clip(local_ids, 0, vocab_local - 1), axis=0)  23.9 us
    pallas_call x1, Pallas kernels, update(): pl.pallas_call(update_kernel, grid=(latents // span,), out_shape=[jax.Sha...  7.32 us
  transfers between devices with their start and end apart: 3, of which 0 were waited for; matrix products, arithmetic and copies ran while one was open for 9% of the time, Pallas kernels for 0%

profile of v6, /device:TPU:0, one launch (start us, length us, event | category | flops | bytes accessed | tf_op | source)
XLA Modules:
  0.0 361.3 jit_solution(4619440734659738254)
XLA Ops:
  0.6 0.0 copy-start.3
  0.7 0.0 copy-start.4
  0.7 0.0 copy-start.5
  0.7 1.3 convert_bitcast_fusion.1
  2.0 1.3 convert_bitcast_fusion
  3.3 0.1 pad_maximum_fusion.own_ref
  3.4 0.0 copy-start
  3.4 3.0 collective-permute-start.2
  6.4 1.3 collective-permute-start.1
  7.7 5.5 %collective-permute-start = (bf16[2,64,4096]{2,1,0:T(8,128)(2,1)S(1)}, bf16[2,64,4096]{2,1,0:T(8,128)(2,1)}, u32[]{:S(2)}, u32[]{:S(2)}) collective-permute-start(bf16[2,64,4096]{2,1,0:T(8,128)(2,1)S(1)} %pad_maximum_fusion.own_ref), channel_id=1, source_target_pairs={{0,8},{4,12},{8,16},{12,20},{16,24},{20,28},{1,9},{5,13},{9,17},{1... | collective-permute-start | bytes 3145736 | tf_op jit(solution)/shard_map/ppermute | solution.py:1172
  13.2 0.0 copy-done.3
  13.3 0.0 copy-done.4
  13.3 0.6 broadcast_in_dim.65.bias_ref
  13.9 0.0 copy-done.5
  13.9 0.6 fusion.1
  14.5 0.7 multiply_add_fusion
  15.2 23.9 %gather_fusion = bf16[4096,512]{1,0:T(8,128)(2,1)} fusion(bf16[12576,512]{1,0:T(8,128)(2,1)} %param.26, s32[4096]{0:T(1024)S(1)} %fusion), kind=kCustom, calls=%fused_computation | custom fusion | bytes 8404992 | tf_op jit(solution)/shard_map/jit(_take)/gather | solution.py:1166
  39.1 0.0 copy-done
  39.1 5.3 %select_select_fusion.picked_ref = bf16[4096,512]{1,0:T(8,128)(2,1)} fusion(bf16[4096,512]{1,0:T(8,128)(2,1)} %gather_fusion, pred[4096]{0:T(1024)(128)(4,1)S(1)} %get-tuple-element.78, pred[4096]{0:T(1024)(128)(4,1)S(1)} %get-tuple-element.77), kind=kLoop, calls=%fused_computation.1 | loop fusion | flops 4194304 | bytes 8396800 | tf_op jit(solution)/shard_map/jit(_where)/select_n | solution.py:1167
  44.4 0.0 collective-permute-done.2
  44.4 0.0 copy-start.1
  44.4 0.0 collective-permute-done.1.right_ref
  44.4 0.0 copy-start.2
  44.4 0.0 collective-permute-done.left_ref
  44.4 1.2 broadcast_in_dim.66.level_hbm
  45.6 0.0 copy-done.1
  45.6 0.3 copy-done.2
  45.9 82.0 %front.1 = (bf16[4096,512]{1,0:T(8,128)(2,1)}, bf16[512,4096]{1,0:T(8,128)(2,1)}, bf16[512,4096]{1,0:T(8,128)(2,1)}, f32[1,4096]{1,0:T(1,128)}, f32[1,4096]{1,0:...) custom-call(bf16[4096,512]{1,0:T(8,128)(2,1)} %select_select_fusion.picked_ref, f32[4,512]{1,0:T(4,128)} %norm_ref.1, ...), custom_call_target="tpu_custom_call" | custom-call | tf_op jit(solution)/shard_map/front/pallas_call | solution.py:366
  127.9 1.9 broadcast_in_dim.67.mask_hbm
  129.8 90.9 %forward.1 = (bf16[8,4096,512]{2,1,0:T(8,128)(2,1)}, f32[8,4096,512]{2,1,0:T(8,128)}, f32[8,4096]{1,0:T(8,128)}, bf16[4096,512]{1,0:T(8,128)(2,1)}, f32[16,512]{1,0:T(8,128)}) custom-call(bf16[4096,512]{1,0:T(8,128)(2,1)} %get-tuple-element.45.inputs_hbm, bf16[512,4096]{1,0:T(8,128)(2,1)} %get-tuple-element.46.enc_hbm, ...), custom_call_target="tpu_custom_call" | custom-call | tf_op jit(solution)/shard_map/forward/pallas_call | solution.py:660
  220.7 131.9 %backward.1 = (f32[64,4096]{1,0:T(8,128)}, f32[64,4096]{1,0:T(8,128)}, f32[1,4096]{1,0:T(1,128)}, f32[1,512]{1,0:T(1,128)}, f32[8,128]{1,0:T(8,128)}) custom-call(bf16[4096,512]{1,0:T(8,128)(2,1)} %get-tuple-element.49.back_ref, f32[1,4096]{1,0:T(1,128)} %get-tuple-element.50.norms_ref, f32[1,4096]{1,0:T(1,128)} %get-tuple-element.51.lasso_ref, ...), custom_call_target="tpu_custom_call" | custom-call | tf_op jit(solution)/shard_map/backward/pallas_call | solution.py:1043
  352.6 7.3 %update.1 = (f32[64,4096]{1,0:T(8,128)}, f32[64,4096]{1,0:T(8,128)}, f32[64,4096]{1,0:T(8,128)}, f32[64,4096]{1,0:T(8,128)}, f32[64,4096]{1,0:T(8,128)}, /*index...) custom-call(f32[8,128]{1,0:T(8,128)} %get-tuple-element.57.totals_re, ...), custom_call_target="tpu_custom_call" | custom-call | tf_op jit(solution)/shard_map/update/pallas_call | solution.py:1118
  359.9 1.3 fusion.2
  (2 shorter events, 0.0 us)
Async XLA Ops:
  0.6 12.6 %copy-start.3 = (s32[4096]{0:T(1024)S(1)}, s32[4096]{0:T(1024)}, u32[]{:S(2)}) copy-start(s32[4096]{0:T(1024)} %param.23) | copy-start | bytes 49156
  0.7 12.6 %copy-start.4 = (f32[4608]{0:T(1024)S(1)}, f32[4608]{0:T(1024)}, u32[]{:S(2)}) copy-start(f32[4608]{0:T(1024)} %param.28) | copy-start | bytes 55300
  0.7 13.2 %copy-start.5 = (s32[4096]{0:T(1024)S(1)}, s32[4096]{0:T(1024)}, u32[]{:S(2)}) copy-start(s32[4096]{0:T(1024)} %param.24) | copy-start | bytes 49156
  3.4 35.7 %copy-start = (bf16[2,64,4096]{2,1,0:T(8,128)(2,1)}, bf16[2,64,4096]{2,1,0:T(8,128)(2,1)S(1)}, u32[]{:S(2)}) copy-start(bf16[2,64,4096]{2,1,0:T(8,128)(2,1)S(1)} %pad_maximum_fusion.own_ref) | copy-start | bytes 3145732
  3.4 41.0 %collective-permute-start.2 = (bf16[2,64,4096]{2,1,0:T(8,128)(2,1)S(1)}, bf16[2,64,4096]{2,1,0:T(8,128)(2,1)S(1)}, u32[]{:S(2)}, u32[]{:S(2)}) collective-permute-start(bf16[2,64,4096]{2,1,0:T(8,128)(2,1)S(1)} %pad_maximum_fusion.own_ref), channel_id=1, source_target_pairs={{4,0},{0,4},{12,8},{8,12},{20,16},{16,20},{28,24},{24,28},{5,1},{1... | collective-permute-start | bytes 3145736 | tf_op jit(solution)/shard_map/ppermute | solution.py:1177
  6.4 38.0 %collective-permute-start.1 = (bf16[2,64,4096]{2,1,0:T(8,128)(2,1)S(1)}, bf16[2,64,4096]{2,1,0:T(8,128)(2,1)S(1)}, u32[]{:S(2)}, u32[]{:S(2)}) collective-permute-start(bf16[2,64,4096]{2,1,0:T(8,128)(2,1)S(1)} %pad_maximum_fusion.own_ref), channel_id=1, source_target_pairs={{8,0},{12,4},{16,8},{20,12},{24,16},{28,20},{9,1},{13,5},{17,9},{2... | collective-permute-start | bytes 3145736 | tf_op jit(solution)/shard_map/ppermute | solution.py:1173
  7.7 36.7 %collective-permute-start = (bf16[2,64,4096]{2,1,0:T(8,128)(2,1)S(1)}, bf16[2,64,4096]{2,1,0:T(8,128)(2,1)}, u32[]{:S(2)}, u32[]{:S(2)}) collective-permute-start(bf16[2,64,4096]{2,1,0:T(8,128)(2,1)S(1)} %pad_maximum_fusion.own_ref), channel_id=1, source_target_pairs={{0,8},{4,12},{8,16},{12,20},{16,24},{20,28},{1,9},{5,13},{9,17},{1... | collective-permute-start | bytes 3145736 | tf_op jit(solution)/shard_map/ppermute | solution.py:1172
  44.4 1.2 copy-start.1
  44.4 1.5 copy-start.2

commit v7 on v6

--- a/solution.py
+++ b/solution.py
@@ -46,10 +46,10 @@
 def front_kernel(
     rows_size, lat_size,
     picked_ref, norm_ref, bias_ref, mask_ref, dec_ref,
-    joined_hbm, attn_hbm, mlp_in_hbm, mlp_out_hbm, turn_hbm, level_hbm, own_ref, left_ref, right_ref, across_ref,
+    joined_hbm, attn_hbm, mlp_in_hbm, mlp_out_hbm, turn_hbm, code_hbm, own_ref, left_ref, right_ref, across_ref,
     inputs_out, enc_out, dec_out, norms_out, lasso_out, pull_out, scale_out,
     from_core, from_y, base, queries, keys, values, context, ready, facts, got_facts,
-    joined_ref, attn_ref, mlp_in_ref, mlp_out_ref, turn_ref, level_ref,
+    joined_ref, attn_ref, mlp_in_ref, mlp_out_ref, turn_ref, code_ref,
     load_sem, place_sem,
     out_right, in_left, out_left, in_right, out_x, in_x, out_fact, in_fact,
     out_core, in_core, out_y, in_y, out_own, in_own, out_near, in_near,
@@ -60,8 +60,8 @@
     loads = [
         pltpu.make_async_copy(source, target, load_sem.at[at])
         for at, (source, target) in enumerate((
-            (joined_hbm, joined_ref), (turn_hbm, turn_ref), (mlp_in_hbm, mlp_in_ref),
-            (mlp_out_hbm, mlp_out_ref), (attn_hbm, attn_ref), (level_hbm, level_ref)))
+            (code_hbm, code_ref), (joined_hbm, joined_ref), (turn_hbm, turn_ref), (mlp_in_hbm, mlp_in_ref),
+            (mlp_out_hbm, mlp_out_ref), (attn_hbm, attn_ref)))
     ]
     for load in loads:
         load.start()
@@ -190,11 +190,19 @@
     for piece in range(pieces):
         for step in list(range(1, y_size)) + [0]:
             core_copy(step, piece).start()
+    def code_rows(y, piece):
+        code = code_ref[pl.ds(pl.multiple_of(y * tokens + piece * PIECE, PIECE), PIECE), :]
+        return jnp.concatenate([code] * (depth // 128), axis=1)
+
+    loads[0].wait()
     for piece in range(pieces):
         here = pl.ds(piece * PIECE, PIECE)
         for step in list(range(1, y_size)) + [0]:
+            holder = lax.shift_right_logical(code_rows(y_peer(step), piece), 4)
             core_copy(step, piece).wait_recv()
-            total = picked_ref[block_rows(y_peer(step), core, piece), :].astype(f32) + from_core[step, here, :].astype(f32)
+            total = jnp.where(
+                holder == lat, picked_ref[block_rows(y_peer(step), core, piece), :].astype(f32),
+                jnp.where(holder == my_y * CORES + other, from_core[step, here, :].astype(f32), 0.0))
             if step == 0:
                 base[here, :] = total
             else:
@@ -225,7 +233,7 @@
                 tile * cosine + pltpu.roll(tile, PAIR - ROT // 2, 1) * low + pltpu.roll(tile, ROT // 2, 1) * high)
         return jnp.concatenate(parts, axis=1)
 
-    for load in loads:
+    for load in loads[1:]:
         load.wait()
     for block in range(tokens // ROWS):
         rows = pl.ds(block * ROWS, ROWS)
@@ -290,7 +298,7 @@
 
         lax.fori_loop(0, depth // PAIR, attend, 0)
         attended = dot(context[here, :], attn_ref[...]) + bias_ref[:, 3 * depth : 4 * depth]
-        level = jnp.concatenate([level_ref[here, :]] * (depth // 128), axis=1)
+        level = 0.5 + 0.25 * (code_rows(my_y, piece) & 15).astype(f32)
         ready[here, :] = ((base[here, :] + attended) * level).astype(bf16)
         keep_copy(piece).start()
         for step in range(1, y_size):
@@ -352,7 +360,7 @@
 
 
 def front(rows_size, lat_size, picked, norm_params, bias_row, w_joined, w_attn_out, w_mlp_in, w_mlp_out,
-          turns, level_lanes, mask_tiles, dec_shard, own, left, right, across):
+          turns, code_lanes, mask_tiles, dec_shard, own, left, right, across):
     group, depth = picked.shape
     tokens = group // lat_size
     shard, latents = dec_shard.shape
@@ -387,7 +395,7 @@
             pltpu.VMEM((tokens, depth), bf16),
             pltpu.VMEM((16, latents // 8), f32),
             pltpu.VMEM((rows_size - 1, 16, latents // 8), f32),
-            *[pltpu.VMEM(a.shape, a.dtype) for a in (w_joined, w_attn_out, w_mlp_in, w_mlp_out, turns, level_lanes)],
+            *[pltpu.VMEM(a.shape, a.dtype) for a in (w_joined, w_attn_out, w_mlp_in, w_mlp_out, turns, code_lanes)],
             dma((6,)), dma((x_size + 3, max(pieces, 2))),
             dma((hops, 2)), dma((hops, 2)), dma((hops, 2)), dma((hops, 2)),
             dma((Z_CHIPS, 2, x_size - 1)), dma((Z_CHIPS, 2, x_size - 1)),
@@ -401,7 +409,7 @@
             collective_id=3, has_side_effects=True, vmem_limit_bytes=60 * 2**20),
         name="front",
     )(picked, norm_params, bias_row, mask_tiles, dec_shard,
-      w_joined, w_attn_out, w_mlp_in, w_mlp_out, turns, level_lanes, own, left, right, across)
+      w_joined, w_attn_out, w_mlp_in, w_mlp_out, turns, code_lanes, own, left, right, across)
 
 
 def turn_tables(length):
@@ -1162,9 +1170,10 @@
     vocab_local = embed.shape[0]
     vocab_first = lat_index * vocab_local
     local_ids = token_ids - vocab_first
-    inside = (local_ids >= 0) & (local_ids < vocab_local)
-    picked = jnp.take(embed, jnp.clip(local_ids, 0, vocab_local - 1), axis=0)
-    picked = jnp.where(inside[:, None], picked, jnp.zeros((), bf16))
+    picked = jnp.take(embed, local_ids, axis=0, mode="clip")
+    codes = (token_ids // vocab_local * 16 + scale_index).reshape(lat_size // CORES, CORES, tok_local)
+    codes = lax.dynamic_index_in_dim(codes, lat_index % CORES, 1, keepdims=False).reshape(-1)
+    code_lanes = jnp.broadcast_to(codes[:, None], (codes.shape[0], 128))
     own = jnp.stack([enc_weight.astype(bf16), dec_master.astype(bf16)])
     x_size = rows_size // Z_CHIPS
     right_pairs = [(i, i + x_size) for i in range(rows_size - x_size)]
@@ -1175,13 +1184,10 @@
     for step in range(1, x_size):
         pairs = [(i // x_size * x_size + (i + step) % x_size, i) for i in range(rows_size)]
         across.append(lax.ppermute(own, "rows", pairs))
-    own_first = lat_index * tok_local
-    scales = 0.5 + 0.25 * lax.dynamic_slice_in_dim(scale_index, own_first, tok_local).astype(f32)
-    level_lanes = jnp.broadcast_to(scales[:, None], (tok_local, 128))
     mask_lanes = jnp.broadcast_to(mask_float[:, None], (group_tokens, 128))
     all_inputs, enc_low, dec_cols, norms_row, lasso_row, pull_row, scale_rows = front(
         rows_size, lat_size, picked, norm_params, bias_row, w_joined, w_attn_out, w_mlp_in, w_mlp_out,
-        turn_tables(tok_local), level_lanes, mask_float.reshape(-1, 128), dec_master,
+        turn_tables(tok_local), code_lanes, mask_float.reshape(-1, 128), dec_master,
         own, from_left, from_right, jnp.stack(across))
     active, slope, mass_rows, recon_grad, stats = forward(
         lat_size, all_inputs, enc_low, dec_cols, enc_bias[None, :], mask_lanes, dec_bias[None, :], scale_rows)

time: 362 us -> 356 us (0.983)
  other arithmetic: 9.29 us -> 3.31 us
    select_n x1 -> x0, other arithmetic: 5.28 us -> none  [body(): picked = jnp.where(inside[:, None], picked, jnp.zeros((), bf16))]
  transfers between devices with their start and end apart: 3 -> 3, of which waited for: 0 -> 0; matrix products, arithmetic and copies ran while one was open for 9% -> 7% of each run, Pallas kernels for 0% -> 0%
where the time goes in v7:
time: 356 us
  Pallas kernels  312 us (88%)
  local copies, waits for them, and re-layouts  29.5 us (8%)
  starting transfers between devices  9.81 us (3%)
    pallas_call x1, Pallas kernels, backward(): pl.pallas_call(functools.partial(backward_kernel, rows_size, lat_size), o...  132 us
    pallas_call x1, Pallas kernels, forward(): pl.pallas_call(functools.partial(forward_kernel, lat_size), out_shape=[ja...  90.8 us
    pallas_call x1, Pallas kernels, front(): pl.pallas_call(functools.partial(front_kernel, rows_size, lat_size), out_...  82.1 us
    gather x1, local copies, waits for them, and re-layouts, body(): picked = jnp.take(embed, local_ids, axis=0, mode='clip')  24 us
    pallas_call x1, Pallas kernels, update(): pl.pallas_call(update_kernel, grid=(latents // span,), out_shape=[jax.Sha...  7.39 us
  transfers between devices with their start and end apart: 3, of which 0 were waited for; matrix products, arithmetic and copies ran while one was open for 7% of the time, Pallas kernels for 0%

profile of v7, /device:TPU:0, one launch (start us, length us, event | category | flops | bytes accessed | tf_op | source)
XLA Modules:
  0.0 355.6 jit_solution(35075983371263454)
XLA Ops:
  0.6 0.0 copy-start.3
  0.7 0.0 copy-start.5
  0.7 0.0 copy-start.6
  0.7 1.3 convert_bitcast_fusion.1
  2.0 1.3 convert_bitcast_fusion
  3.3 0.1 pad_maximum_fusion.own_ref
  3.4 0.0 copy-start
  3.4 3.0 collective-permute-start.2
  6.4 1.3 collective-permute-start.1
  7.7 5.5 %collective-permute-start = (bf16[2,64,4096]{2,1,0:T(8,128)(2,1)S(1)}, bf16[2,64,4096]{2,1,0:T(8,128)(2,1)}, u32[]{:S(2)}, u32[]{:S(2)}) collective-permute-start(bf16[2,64,4096]{2,1,0:T(8,128)(2,1)S(1)} %pad_maximum_fusion.own_ref), channel_id=1, source_target_pairs={{0,8},{4,12},{8,16},{12,20},{16,24},{20,28},{1,9},{5,13},{9,17},{1... | collective-permute-start | bytes 3145736 | tf_op jit(solution)/shard_map/ppermute | solution.py:1181
  13.2 0.0 copy-done.3
  13.2 0.6 broadcast_in_dim.41.bias_ref
  13.8 0.0 copy-done.5
  13.8 0.0 copy-done.6
  13.9 0.0 copy-start.4
  13.9 24.0 %gather_fusion = bf16[4096,512]{1,0:T(8,128)(2,1)} fusion(bf16[12576,512]{1,0:T(8,128)(2,1)} %param.26, s32[4096]{0:T(1024)S(1)} %get-tuple-element.78), kind=kCustom, calls=%fused_computation | custom fusion | bytes 8404992 | tf_op jit(solution)/shard_map/jit(_take)/gather | solution.py:1173
  37.9 0.0 copy-done
  37.9 0.0 copy-done.4
  37.9 0.6 fusion.3
  38.5 0.0 collective-permute-done.2
  38.5 0.0 copy-start.1
  38.5 0.0 collective-permute-done.1.right_ref
  38.5 0.0 copy-start.2
  38.5 0.0 collective-permute-done.left_ref
  38.5 1.6 broadcast_in_dim.43.code_hbm
  40.2 0.0 copy-done.1
  40.2 0.0 copy-done.2
  40.2 82.1 %front.1 = (bf16[4096,512]{1,0:T(8,128)(2,1)}, bf16[512,4096]{1,0:T(8,128)(2,1)}, bf16[512,4096]{1,0:T(8,128)(2,1)}, f32[1,4096]{1,0:T(1,128)}, f32[1,4096]{1,0:...) custom-call(bf16[4096,512]{1,0:T(8,128)(2,1)} %gather_fusion, f32[4,512]{1,0:T(4,128)} %norm_ref.1, ...), custom_call_target="tpu_custom_call" | custom-call | tf_op jit(solution)/shard_map/front/pallas_call | solution.py:374
  122.2 1.9 broadcast_in_dim.44.mask_hbm
  124.2 90.8 %forward.1 = (bf16[8,4096,512]{2,1,0:T(8,128)(2,1)}, f32[8,4096,512]{2,1,0:T(8,128)}, f32[8,4096]{1,0:T(8,128)}, bf16[4096,512]{1,0:T(8,128)(2,1)}, f32[16,512]{1,0:T(8,128)}) custom-call(bf16[4096,512]{1,0:T(8,128)(2,1)} %get-tuple-element.45.inputs_hbm, bf16[512,4096]{1,0:T(8,128)(2,1)} %get-tuple-element.46.enc_hbm, ...), custom_call_target="tpu_custom_call" | custom-call | tf_op jit(solution)/shard_map/forward/pallas_call | solution.py:668
  215.0 131.9 %backward.1 = (f32[64,4096]{1,0:T(8,128)}, f32[64,4096]{1,0:T(8,128)}, f32[1,4096]{1,0:T(1,128)}, f32[1,512]{1,0:T(1,128)}, f32[8,128]{1,0:T(8,128)}) custom-call(bf16[4096,512]{1,0:T(8,128)(2,1)} %get-tuple-element.49.back_ref, f32[1,4096]{1,0:T(1,128)} %get-tuple-element.50.norms_ref, f32[1,4096]{1,0:T(1,128)} %get-tuple-element.51.lasso_ref, ...), custom_call_target="tpu_custom_call" | custom-call | tf_op jit(solution)/shard_map/backward/pallas_call | solution.py:1051
  346.9 7.4 %update.1 = (f32[64,4096]{1,0:T(8,128)}, f32[64,4096]{1,0:T(8,128)}, f32[64,4096]{1,0:T(8,128)}, f32[64,4096]{1,0:T(8,128)}, f32[64,4096]{1,0:T(8,128)}, /*index...) custom-call(f32[8,128]{1,0:T(8,128)} %get-tuple-element.57.totals_re, ...), custom_call_target="tpu_custom_call" | custom-call | tf_op jit(solution)/shard_map/update/pallas_call | solution.py:1126
  354.3 1.3 fusion.4
  (3 shorter events, 0.0 us)
Async XLA Ops:
  0.6 12.6 %copy-start.3 = (f32[4608]{0:T(1024)S(1)}, f32[4608]{0:T(1024)}, u32[]{:S(2)}) copy-start(f32[4608]{0:T(1024)} %param.28) | copy-start | bytes 55300
  0.7 13.2 %copy-start.5 = (s32[4096]{0:T(1024)S(1)}, s32[4096]{0:T(1024)}, u32[]{:S(2)}) copy-start(s32[4096]{0:T(1024)} %param.25) | copy-start | bytes 49156
  0.7 13.2 %copy-start.6 = (s32[4096]{0:T(1024)S(1)}, s32[4096]{0:T(1024)}, u32[]{:S(2)}) copy-start(s32[4096]{0:T(1024)} %param.23) | copy-start | bytes 49156
  3.4 34.5 %copy-start = (bf16[2,64,4096]{2,1,0:T(8,128)(2,1)}, bf16[2,64,4096]{2,1,0:T(8,128)(2,1)S(1)}, u32[]{:S(2)}) copy-start(bf16[2,64,4096]{2,1,0:T(8,128)(2,1)S(1)} %pad_maximum_fusion.own_ref) | copy-start | bytes 3145732
  3.4 35.1 %collective-permute-start.2 = (bf16[2,64,4096]{2,1,0:T(8,128)(2,1)S(1)}, bf16[2,64,4096]{2,1,0:T(8,128)(2,1)S(1)}, u32[]{:S(2)}, u32[]{:S(2)}) collective-permute-start(bf16[2,64,4096]{2,1,0:T(8,128)(2,1)S(1)} %pad_maximum_fusion.own_ref), channel_id=1, source_target_pairs={{4,0},{0,4},{12,8},{8,12},{20,16},{16,20},{28,24},{24,28},{5,1},{1... | collective-permute-start | bytes 3145736 | tf_op jit(solution)/shard_map/ppermute | solution.py:1186
  6.4 32.1 %collective-permute-start.1 = (bf16[2,64,4096]{2,1,0:T(8,128)(2,1)S(1)}, bf16[2,64,4096]{2,1,0:T(8,128)(2,1)S(1)}, u32[]{:S(2)}, u32[]{:S(2)}) collective-permute-start(bf16[2,64,4096]{2,1,0:T(8,128)(2,1)S(1)} %pad_maximum_fusion.own_ref), channel_id=1, source_target_pairs={{8,0},{12,4},{16,8},{20,12},{24,16},{28,20},{9,1},{13,5},{17,9},{2... | collective-permute-start | bytes 3145736 | tf_op jit(solution)/shard_map/ppermute | solution.py:1182
  7.7 30.9 %collective-permute-start = (bf16[2,64,4096]{2,1,0:T(8,128)(2,1)S(1)}, bf16[2,64,4096]{2,1,0:T(8,128)(2,1)}, u32[]{:S(2)}, u32[]{:S(2)}) collective-permute-start(bf16[2,64,4096]{2,1,0:T(8,128)(2,1)S(1)} %pad_maximum_fusion.own_ref), channel_id=1, source_target_pairs={{0,8},{4,12},{8,16},{12,20},{16,24},{20,28},{1,9},{5,13},{9,17},{1... | collective-permute-start | bytes 3145736 | tf_op jit(solution)/shard_map/ppermute | solution.py:1181
  13.9 24.0 %copy-start.4 = (s32[4096]{0:T(1024)S(1)}, s32[4096]{0:T(1024)}, u32[]{:S(2)}) copy-start(s32[4096]{0:T(1024)} %param.24) | copy-start | bytes 49156
  38.5 1.7 copy-start.1
  38.5 1.7 copy-start.2

commit v8 on v7

--- a/solution.py
+++ b/solution.py
@@ -456,7 +456,7 @@
     chunks, spans = tokens // chunk, latents // span
     y_size = lat_size // CORES
     share = chunk // lat_size
-    strip = 16
+    strip = 32
     row = lax.axis_index("rows")
     lat = lax.axis_index("lat")
     my_y, core = lat // CORES, lax.rem(lat, CORES)
@@ -1117,7 +1117,7 @@
 def update(totals, counts, grads, states):
     shard, latents = grads[0].shape
     depth = grads[3].shape[1]
-    span = latents // 4
+    span = latents // 8
     wide = pl.BlockSpec((shard, span), lambda i: (0, i))
     row = pl.BlockSpec((1, span), lambda i: (0, i))
     short = pl.BlockSpec((1, depth), lambda i: (0, 0))

time: 356 us -> 357 us (level)
  no operation moved by 1% of the time
where the time goes in v8:
time: 357 us
  Pallas kernels  313 us (88%)
  local copies, waits for them, and re-layouts  29.5 us (8%)
  starting transfers between devices  9.81 us (3%)
    pallas_call x1, Pallas kernels, backward(): pl.pallas_call(functools.partial(backward_kernel, rows_size, lat_size), o...  132 us
    pallas_call x1, Pallas kernels, forward(): pl.pallas_call(functools.partial(forward_kernel, lat_size), out_shape=[ja...  90.3 us
    pallas_call x1, Pallas kernels, front(): pl.pallas_call(functools.partial(front_kernel, rows_size, lat_size), out_...  82.1 us
    gather x1, local copies, waits for them, and re-layouts, body(): picked = jnp.take(embed, local_ids, axis=0, mode='clip')  24 us
    pallas_call x1, Pallas kernels, update(): pl.pallas_call(update_kernel, grid=(latents // span,), out_shape=[jax.Sha...  9.12 us
  transfers between devices with their start and end apart: 3, of which 0 were waited for; matrix products, arithmetic and copies ran while one was open for 7% of the time, Pallas kernels for 0%

profile of v8, /device:TPU:0, one launch (start us, length us, event | category | flops | bytes accessed | tf_op | source)
XLA Modules:
  0.0 356.8 jit_solution(18238495286502662340)
XLA Ops:
  0.6 0.0 copy-start.3
  0.7 0.0 copy-start.5
  0.7 0.0 copy-start.6
  0.7 1.3 convert_bitcast_fusion.1
  2.0 1.3 convert_bitcast_fusion
  3.3 0.1 pad_maximum_fusion.own_ref
  3.4 0.0 copy-start
  3.4 3.0 collective-permute-start.2
  6.4 1.3 collective-permute-start.1
  7.7 5.5 %collective-permute-start = (bf16[2,64,4096]{2,1,0:T(8,128)(2,1)S(1)}, bf16[2,64,4096]{2,1,0:T(8,128)(2,1)}, u32[]{:S(2)}, u32[]{:S(2)}) collective-permute-start(bf16[2,64,4096]{2,1,0:T(8,128)(2,1)S(1)} %pad_maximum_fusion.own_ref), channel_id=1, source_target_pairs={{0,8},{4,12},{8,16},{12,20},{16,24},{20,28},{1,9},{5,13},{9,17},{1... | collective-permute-start | bytes 3145736 | tf_op jit(solution)/shard_map/ppermute | solution.py:1181
  13.2 0.0 copy-done.3
  13.2 0.6 broadcast_in_dim.41.bias_ref
  13.8 0.0 copy-done.5
  13.8 0.0 copy-done.6
  13.9 0.0 copy-start.4
  13.9 24.0 %gather_fusion = bf16[4096,512]{1,0:T(8,128)(2,1)} fusion(bf16[12576,512]{1,0:T(8,128)(2,1)} %param.26, s32[4096]{0:T(1024)S(1)} %get-tuple-element.78), kind=kCustom, calls=%fused_computation | custom fusion | bytes 8404992 | tf_op jit(solution)/shard_map/jit(_take)/gather | solution.py:1173
  37.9 0.0 copy-done
  37.9 0.0 copy-done.4
  37.9 0.6 fusion.3
  38.5 0.0 collective-permute-done.2
  38.5 0.0 copy-start.1
  38.5 0.0 collective-permute-done.1.right_ref
  38.5 0.0 copy-start.2
  38.5 0.0 collective-permute-done.left_ref
  38.5 1.6 broadcast_in_dim.43.code_hbm
  40.2 0.0 copy-done.1
  40.2 0.0 copy-done.2
  40.2 82.1 %front.1 = (bf16[4096,512]{1,0:T(8,128)(2,1)}, bf16[512,4096]{1,0:T(8,128)(2,1)}, bf16[512,4096]{1,0:T(8,128)(2,1)}, f32[1,4096]{1,0:T(1,128)}, f32[1,4096]{1,0:...) custom-call(bf16[4096,512]{1,0:T(8,128)(2,1)} %gather_fusion, f32[4,512]{1,0:T(4,128)} %norm_ref.1, ...), custom_call_target="tpu_custom_call" | custom-call | tf_op jit(solution)/shard_map/front/pallas_call | solution.py:374
  122.2 1.9 broadcast_in_dim.44.mask_hbm
  124.2 90.3 %forward.1 = (bf16[8,4096,512]{2,1,0:T(8,128)(2,1)}, f32[8,4096,512]{2,1,0:T(8,128)}, f32[8,4096]{1,0:T(8,128)}, bf16[4096,512]{1,0:T(8,128)(2,1)}, f32[16,512]{1,0:T(8,128)}) custom-call(bf16[4096,512]{1,0:T(8,128)(2,1)} %get-tuple-element.45.inputs_hbm, bf16[512,4096]{1,0:T(8,128)(2,1)} %get-tuple-element.46.enc_hbm, ...), custom_call_target="tpu_custom_call" | custom-call | tf_op jit(solution)/shard_map/forward/pallas_call | solution.py:668
  214.5 131.9 %backward.1 = (f32[64,4096]{1,0:T(8,128)}, f32[64,4096]{1,0:T(8,128)}, f32[1,4096]{1,0:T(1,128)}, f32[1,512]{1,0:T(1,128)}, f32[8,128]{1,0:T(8,128)}) custom-call(bf16[4096,512]{1,0:T(8,128)(2,1)} %get-tuple-element.49.back_ref, f32[1,4096]{1,0:T(1,128)} %get-tuple-element.50.norms_ref, f32[1,4096]{1,0:T(1,128)} %get-tuple-element.51.lasso_ref, ...), custom_call_target="tpu_custom_call" | custom-call | tf_op jit(solution)/shard_map/backward/pallas_call | solution.py:1051
  346.4 9.1 %update.1 = (f32[64,4096]{1,0:T(8,128)}, f32[64,4096]{1,0:T(8,128)}, f32[64,4096]{1,0:T(8,128)}, f32[64,4096]{1,0:T(8,128)}, f32[64,4096]{1,0:T(8,128)}, /*index...) custom-call(f32[8,128]{1,0:T(8,128)} %get-tuple-element.57.totals_re, ...), custom_call_target="tpu_custom_call" | custom-call | tf_op jit(solution)/shard_map/update/pallas_call | solution.py:1126
  355.5 1.3 fusion.4
  (3 shorter events, 0.0 us)
Async XLA Ops:
  0.6 12.6 %copy-start.3 = (f32[4608]{0:T(1024)S(1)}, f32[4608]{0:T(1024)}, u32[]{:S(2)}) copy-start(f32[4608]{0:T(1024)} %param.28) | copy-start | bytes 55300
  0.7 13.2 %copy-start.5 = (s32[4096]{0:T(1024)S(1)}, s32[4096]{0:T(1024)}, u32[]{:S(2)}) copy-start(s32[4096]{0:T(1024)} %param.25) | copy-start | bytes 49156
  0.7 13.2 %copy-start.6 = (s32[4096]{0:T(1024)S(1)}, s32[4096]{0:T(1024)}, u32[]{:S(2)}) copy-start(s32[4096]{0:T(1024)} %param.23) | copy-start | bytes 49156
  3.4 34.5 %copy-start = (bf16[2,64,4096]{2,1,0:T(8,128)(2,1)}, bf16[2,64,4096]{2,1,0:T(8,128)(2,1)S(1)}, u32[]{:S(2)}) copy-start(bf16[2,64,4096]{2,1,0:T(8,128)(2,1)S(1)} %pad_maximum_fusion.own_ref) | copy-start | bytes 3145732
  3.4 35.1 %collective-permute-start.2 = (bf16[2,64,4096]{2,1,0:T(8,128)(2,1)S(1)}, bf16[2,64,4096]{2,1,0:T(8,128)(2,1)S(1)}, u32[]{:S(2)}, u32[]{:S(2)}) collective-permute-start(bf16[2,64,4096]{2,1,0:T(8,128)(2,1)S(1)} %pad_maximum_fusion.own_ref), channel_id=1, source_target_pairs={{4,0},{0,4},{12,8},{8,12},{20,16},{16,20},{28,24},{24,28},{5,1},{1... | collective-permute-start | bytes 3145736 | tf_op jit(solution)/shard_map/ppermute | solution.py:1186
  6.4 32.1 %collective-permute-start.1 = (bf16[2,64,4096]{2,1,0:T(8,128)(2,1)S(1)}, bf16[2,64,4096]{2,1,0:T(8,128)(2,1)S(1)}, u32[]{:S(2)}, u32[]{:S(2)}) collective-permute-start(bf16[2,64,4096]{2,1,0:T(8,128)(2,1)S(1)} %pad_maximum_fusion.own_ref), channel_id=1, source_target_pairs={{8,0},{12,4},{16,8},{20,12},{24,16},{28,20},{9,1},{13,5},{17,9},{2... | collective-permute-start | bytes 3145736 | tf_op jit(solution)/shard_map/ppermute | solution.py:1182
  7.7 30.9 %collective-permute-start = (bf16[2,64,4096]{2,1,0:T(8,128)(2,1)S(1)}, bf16[2,64,4096]{2,1,0:T(8,128)(2,1)}, u32[]{:S(2)}, u32[]{:S(2)}) collective-permute-start(bf16[2,64,4096]{2,1,0:T(8,128)(2,1)S(1)} %pad_maximum_fusion.own_ref), channel_id=1, source_target_pairs={{0,8},{4,12},{8,16},{12,20},{16,24},{20,28},{1,9},{5,13},{9,17},{1... | collective-permute-start | bytes 3145736 | tf_op jit(solution)/shard_map/ppermute | solution.py:1181
  13.9 24.0 %copy-start.4 = (s32[4096]{0:T(1024)S(1)}, s32[4096]{0:T(1024)}, u32[]{:S(2)}) copy-start(s32[4096]{0:T(1024)} %param.24) | copy-start | bytes 49156
  38.5 1.7 copy-start.1
  38.5 1.7 copy-start.2
